TPU v7x, 128 devices: a whole 4x4x4 slice. The times are simulated.
128 devices in a mesh: rep: 16 (over y, z_hi, core), grp: 8 (over z_lo, x).
Axes of the slice: x: 4, y: 4, z: 4 (z_hi: 2, z_lo: 2; z = z_hi * 2 + z_lo), core: 2. Of those that a mesh axis runs over, the one named last changes fastest.
Arguments:
- activations: bfloat16 [16384, 5120], P(('rep', 'grp')), may hold values from -20 to 20
- token_ids: int32 [16384], P('rep'), may hold values from 0 to 151935, as said below
- cotangent: bfloat16 [16384, 4096], P('rep', 'grp'), may hold values from -20 to 20
- inner_weight: bfloat16 [16, 32, 128, 5120], P('rep', 'grp'), may hold values from -6 to 6
- query_gain: float32 [128], replicated, may hold values from 0.1 to 1.9
- outer_weight: float32 [32, 128, 5120], P('grp', 'rep'), may hold values from -6 to 6
- momentum: float32 [32, 128, 5120], P('grp', 'rep'), may hold values from -6 to 6
- average_weight: float32 [32, 128, 5120], P('grp', 'rep'), may hold values from -6 to 6
Outputs:
- new_outer: float32 [32, 128, 5120], P('grp', 'rep')
- new_momentum: float32 [32, 128, 5120], P('grp', 'rep')
- new_average: float32 [32, 128, 5120], P('grp', 'rep')
Inputs may be any that keep to these rules, and one draw needn't show every extreme that they name: `token_ids`: id 0 marks padding; padded positions form the tail of each aligned block of 128 tokens, at most half of it.
All inputs are finite; a program needn't handle non-finite values.
Results may differ from a plain program's by a relative error of at most 0.0015.
Values may be sent and summed in bfloat16 or wider, within the bound.
No kernel may reach another device: no remote copies, remote signals or barrier semaphores. Data moves between devices by JAX's collectives and lax.ppermute only.
A program may use at most 128 MiB of HBM per device.

v0:
```python
import math

import jax
import jax.numpy as jnp
from jax import lax
from jax.sharding import PartitionSpec as P

ITERS = 5


COEF_A = 3.4445
COEF_B = -4.775
COEF_C = 2.0315


def norm_backward(queries, upstream, query_gain, live_rows):
    mean_square = jnp.mean(queries * queries, axis=-1, keepdims=True) + 1e-06
    inverse = lax.rsqrt(mean_square)
    normed = queries * inverse
    scaled = query_gain * upstream.astype(jnp.float32)
    projection = jnp.mean(normed * scaled, axis=-1, keepdims=True)
    return (live_rows[:, None, None] * (scaled - normed * projection) * inverse).astype(
        jnp.bfloat16
    )


def orthogonalize(gradient):
    frobenius = jnp.sqrt(jnp.sum(gradient * gradient, axis=(1, 2), keepdims=True))
    iterate = gradient / (frobenius + 1e-07)
    for number in range(ITERS):
        gram_matrix = jnp.einsum("hik,hjk->hij", iterate, iterate, precision=lax.Precision.HIGHEST)
        squared = jnp.einsum(
            "hij,hjk->hik", gram_matrix, gram_matrix, precision=lax.Precision.HIGHEST
        )
        polynomial = COEF_B * gram_matrix + COEF_C * squared
        applied = jnp.einsum("hij,hjk->hik", polynomial, iterate, precision=lax.Precision.HIGHEST)
        iterate = COEF_A * iterate + applied
    return iterate


def renew_weights(gradient, weights):
    orthogonal = orthogonalize(gradient)
    model_width = weights.shape[-1]
    renewed = (weights.astype(jnp.float32) - 0.2 * math.sqrt(model_width) * orthogonal).astype(
        jnp.bfloat16
    )
    renewed = lax.optimization_barrier(renewed)
    return renewed.astype(jnp.float32)


def shards(
    activations,
    token_ids,
    cotangent,
    inner_weight,
    query_gain,
    outer_weight,
    momentum,
    average_weight,
):
    weights = inner_weight[0]
    head_count, head_size, model_width = weights.shape
    flat_weight = weights.reshape(head_count * head_size, model_width)
    live_all = (token_ids != 0).astype(jnp.float32)
    shard_rows = lax.all_gather(activations, "grp", axis=0, tiled=True)
    row_count = shard_rows.shape[0]
    queries = lax.dot_general(
        shard_rows, flat_weight, (((1,), (1,)), ((), ())), preferred_element_type=jnp.float32
    )
    query_grad = norm_backward(
        queries.reshape(row_count, head_count, head_size),
        cotangent.reshape(row_count, head_count, head_size),
        query_gain,
        live_all,
    )
    query_grad = query_grad.reshape(row_count, head_count * head_size)
    gradient = lax.dot_general(
        query_grad, shard_rows, (((0,), (0,)), ((), ())), preferred_element_type=jnp.float32
    )
    gradient = gradient.reshape(head_count, head_size, model_width)
    renewed = renew_weights(gradient, weights)
    summed = lax.psum(renewed, "rep")
    share_rows = outer_weight.shape[1]
    summed = lax.dynamic_slice_in_dim(summed, lax.axis_index("rep") * share_rows, share_rows, 1)
    mean_weight = summed / lax.axis_size("rep")
    pseudo = outer_weight - mean_weight
    new_momentum = 0.9 * momentum + pseudo
    new_outer = outer_weight - 0.7 * (pseudo + 0.9 * new_momentum)
    new_average = 0.9 * average_weight + 0.1 * new_outer
    return (new_outer, new_momentum, new_average)


def solution(mesh):
    placed = (
        P(("rep", "grp"), None),
        P("rep"),
        P("rep", "grp"),
        P("rep", "grp", None, None),
        P(),
        P("grp", "rep", None),
        P("grp", "rep", None),
        P("grp", "rep", None),
    )
    return jax.shard_map(
        shards,
        mesh=mesh,
        in_specs=placed,
        out_specs=(P("grp", "rep", None), P("grp", "rep", None), P("grp", "rep", None)),
        check_vma=False,
    )
```

profile of v0, /device:TPU:1, one launch (start us, length us, event | category | flops | bytes accessed | tf_op | source)
XLA Modules:
  0.0 540.1 jit_solution(8232370546217740371)
XLA Ops:
  7.2 0.0 all-gather.2.cloned.1.call-start
  7.2 0.7 all-gather.2.cloned.1.call-update
  7.9 1.5 copy.11
  9.4 0.7 compare_convert_fusion
  10.1 114.4 %all-gather.2.cloned.1.call-done = bf16[1024,5120]{1,0:T(8,128)(2,1)} async-done(((bf16[128,5120]{1,0:T(8,128)(2,1)}), bf16[1024,5120]{1,0:T(8,128)(2,1)}) %all-gather.2.cloned.1.call-update) | async-done | bytes 10485776 | tf_op jit(solution)/shard_map/all_gather | solution.py:65
  124.5 10.0 %multiply_reduce_fusion.2 = (f32[1024,4]{0,1:T(4,128)S(1)}, f32[1024,4,128]{0,2,1:T(8,128)S(1)}) fusion(bf16[1,4,128,5120]{3,2,1,0:T(8,128)(2,1)} %param.11, bf16[1024,5120]{1,0:T(8,128)(2,1)} %all-gather.2.cloned.1.call-done), kind=kOutput, calls=%fused_computation.14 | convolution fusion | flops 5369753600 | bytes 17842176 | tf_op jit(solution)/shard_map/dot_general | solution.py:67
  134.6 0.0 copy-done.4
  134.6 0.6 multiply_reduce_fusion.1
  135.2 0.0 copy-done.5
  135.2 8.5 %multiply_reduce_fusion = (f32[4]{0:T(128)S(1)}, f32[4,128,5120]{2,1,0:T(8,128)}) fusion(bf16[1024,5120]{1,0:T(8,128)(2,1)S(1)} %copy-done.5, f32[1024,4,128]{0,2,1:T(8,128)S(1)} %get-tuple-element.7, f32[1024,512]{0,1:T(8,128)S(1)} %copy.11, f32[1024,4]{0,1:T(4,128)S(1)} %broadcast_multiply_fusion, f32[1024,4]{0,1:T(4,128)S(1)} %add_rsqrt_fusion, ...), kind=kOutput, calls=%fused_computation.9 | convolution fusion | flops 5377622016 | bytes 25203216 | tf_op jit(solution)/shard_map/dot_general | solution.py:77
  143.7 17.5 %fusion.5 = f32[4,128,128]{2,1,0:T(8,128)S(1)} fusion(f32[4,128,5120]{2,1,0:T(8,128)} %get-tuple-element.9, f32[4]{0:T(128)S(1)} %sqrt_add_fusion), kind=kOutput, calls=%fused_computation.15 | convolution fusion | flops 4029153280 | bytes 10747920 | tf_op jit(solution)/shard_map/hik,hjk->hij/dot_general | solution.py:31
  161.3 0.4 fusion.10
  161.6 17.9 %multiply_add_fusion.3 = f32[4,128,5120]{2,1,0:T(8,128)S(1)} fusion(f32[4,128,128]{2,1,0:T(8,128)S(1)} %fusion.10, f32[4,128,5120]{2,1,0:T(8,128)} %get-tuple-element.9, f32[4]{0:T(128)S(1)} %sqrt_add_fusion), kind=kOutput, calls=%fused_computation.8 | convolution fusion | flops 4037017600 | bytes 21233680 | tf_op jit(solution)/shard_map/hij,hjk->hik/dot_general | solution.py:36
  179.6 0.0 copy-start
  179.6 9.6 %fusion.17 = f32[4,128,128]{2,1,0:T(8,128)S(1)} fusion(f32[4,128,5120]{2,1,0:T(8,128)S(1)} %multiply_add_fusion.3), kind=kOutput, calls=%fused_computation.39 | convolution fusion | flops 4026531840 | bytes 10747904 | tf_op jit(solution)/shard_map/hik,hjk->hij/dot_general | solution.py:31
  189.1 0.0 copy-done
  189.2 0.4 fusion.9
  189.5 29.4 %multiply_add_fusion.2 = f32[4,128,5120]{2,1,0:T(8,128)S(1)} fusion(f32[4,128,5120]{2,1,0:T(8,128)} %copy-done, f32[4,128,128]{2,1,0:T(8,128)S(1)} %fusion.9), kind=kOutput, calls=%fused_computation.7 | convolution fusion | flops 4031774720 | bytes 21233664 | tf_op jit(solution)/shard_map/hij,hjk->hik/dot_general | solution.py:36
  219.0 9.6 %fusion.18 = f32[4,128,128]{2,1,0:T(8,128)S(1)} fusion(f32[4,128,5120]{2,1,0:T(8,128)S(1)} %multiply_add_fusion.2), kind=kOutput, calls=%fused_computation.40 | convolution fusion | flops 4026531840 | bytes 10747904 | tf_op jit(solution)/shard_map/hik,hjk->hij/dot_general | solution.py:31
  228.6 0.4 fusion.8
  229.0 13.3 %multiply_add_fusion.1 = f32[4,128,5120]{2,1,0:T(8,128)} fusion(f32[4,128,5120]{2,1,0:T(8,128)S(1)} %multiply_add_fusion.2, f32[4,128,128]{2,1,0:T(8,128)S(1)} %fusion.8), kind=kOutput, calls=%fused_computation.6 | convolution fusion | flops 4031774720 | bytes 21233664 | tf_op jit(solution)/shard_map/hij,hjk->hik/dot_general | solution.py:36
  242.3 16.5 %fusion.19 = f32[4,128,128]{2,1,0:T(8,128)S(1)} fusion(f32[4,128,5120]{2,1,0:T(8,128)} %multiply_add_fusion.1), kind=kOutput, calls=%fused_computation.41 | convolution fusion | flops 4026531840 | bytes 10747904 | tf_op jit(solution)/shard_map/hik,hjk->hij/dot_general | solution.py:31
  258.8 0.4 fusion.7
  259.2 17.7 %multiply_add_fusion = f32[4,128,5120]{2,1,0:T(8,128)S(1)} fusion(f32[4,128,5120]{2,1,0:T(8,128)} %multiply_add_fusion.1, f32[4,128,128]{2,1,0:T(8,128)S(1)} %fusion.7), kind=kOutput, calls=%fused_computation.5 | convolution fusion | flops 4031774720 | bytes 21233664 | tf_op jit(solution)/shard_map/hij,hjk->hik/dot_general | solution.py:36
  276.9 9.6 %fusion.20 = f32[4,128,128]{2,1,0:T(8,128)S(1)} fusion(f32[4,128,5120]{2,1,0:T(8,128)S(1)} %multiply_add_fusion), kind=kOutput, calls=%fused_computation.42 | convolution fusion | flops 4026531840 | bytes 10747904 | tf_op jit(solution)/shard_map/hik,hjk->hij/dot_general | solution.py:31
  286.5 0.4 fusion.6
  286.9 13.6 %subtract_convert_fusion = bf16[4,128,5120]{2,1,0:T(8,128)(2,1)} fusion(f32[4,128,5120]{2,1,0:T(8,128)S(1)} %multiply_add_fusion, f32[4,128,128]{2,1,0:T(8,128)S(1)} %fusion.6, bf16[1,4,128,5120]{3,2,1,0:T(8,128)(2,1)} %param.11), kind=kOutput, calls=%fused_computation.4 | convolution fusion | flops 4042260480 | bytes 21233664 | tf_op jit(solution)/shard_map/hij,hjk->hik/dot_general | solution.py:36
  300.4 230.0 %all-reduce.1 = f32[4,128,5120]{2,1,0:T(8,128)} all-reduce(bf16[4,128,5120]{2,1,0:T(8,128)(2,1)} %subtract_convert_fusion), channel_id=1, replica_groups=mesh['rep'=16,'grp'=8] {'rep'}, use_global_device_ids=true, to_apply=%region_3.0 | all-reduce | flops 2621440 | bytes 15728640 | tf_op jit(solution)/shard_map/psum | solution.py:82
  530.4 0.0 copy-done.1
  530.4 0.0 copy-done.2
  530.4 0.0 copy-done.3
  530.4 2.5 multiply_add_fusion.4
  (8 shorter events, 0.0 us)
Async XLA Ops:
  7.2 117.3 %all-gather.2.cloned.1.call-start = ((), (), s32[]{:S(2)}) async-start(), calls=%async_computation | async-start | bytes 11796480 | tf_op jit(solution)/shard_map/all_gather | solution.py:65
  10.1 124.5 %copy-start.4 = (f32[128]{0:T(128)S(1)}, f32[128]{0:T(128)}, u32[]{:S(2)}) copy-start(f32[128]{0:T(128)} %param.12) | copy-start | bytes 1540
  124.5 10.7 %copy-start.5 = (bf16[1024,5120]{1,0:T(8,128)(2,1)S(1)}, bf16[1024,5120]{1,0:T(8,128)(2,1)}, u32[]{:S(2)}) copy-start(bf16[1024,5120]{1,0:T(8,128)(2,1)} %all-gather.2.cloned.1.call-done) | copy-start | bytes 31457284
  179.6 9.6 %copy-start = (f32[4,128,5120]{2,1,0:T(8,128)}, f32[4,128,5120]{2,1,0:T(8,128)S(1)}, u32[]{:S(2)}) copy-start(f32[4,128,5120]{2,1,0:T(8,128)S(1)} %multiply_add_fusion.3) | copy-start | bytes 31457284
  300.4 230.0 %copy-start.1 = (f32[4,8,5120]{2,1,0:T(8,128)S(1)}, f32[4,8,5120]{2,1,0:T(8,128)}, u32[]{:S(2)}) copy-start(f32[4,8,5120]{2,1,0:T(8,128)} %param.15) | copy-start | bytes 1966084
  300.4 230.0 %copy-start.2 = (f32[4,8,5120]{2,1,0:T(8,128)S(1)}, f32[4,8,5120]{2,1,0:T(8,128)}, u32[]{:S(2)}) copy-start(f32[4,8,5120]{2,1,0:T(8,128)} %param.13) | copy-start | bytes 1966084
  300.4 230.0 %copy-start.3 = (f32[4,8,5120]{2,1,0:T(8,128)S(1)}, f32[4,8,5120]{2,1,0:T(8,128)}, u32[]{:S(2)}) copy-start(f32[4,8,5120]{2,1,0:T(8,128)} %param.14) | copy-start | bytes 1966084
Sparse Core Ops, SparseCore 0:
  9.6 114.8 all-gather.1
where the time goes:
time: 549 us; the launch traced here: 540 us
  blocking collectives  230 us (42%)
  matrix products  175 us (32%)
  waiting for transfers between devices  115 us (21%)
  between operations  14.4 us (3%)
    psum x1, blocking collectives, shards(): summed = lax.psum(renewed, 'rep')  230 us
    all_gather x1, waiting for transfers between devices, shards(): shard_rows = lax.all_gather(activations, 'grp', axis=0, tiled=True)  114 us
    dot_general x5, matrix products, orthogonalize(): jnp.einsum('hij,hjk->hik', polynomial, iterate, precision=lax.Precision.H...  92 us
    dot_general x5, matrix products, orthogonalize(): jnp.einsum('hik,hjk->hij', iterate, iterate, precision=lax.Precision.HIGH...  62.8 us
  transfers between devices with their start and end apart: 1, of which 1 were waited for; matrix products, arithmetic and copies ran while one was open for 0% of the time, Pallas kernels for 0%

commit v1 on v0

v1 whole, which is shorter than its diff:
```python
import functools
import math

import jax
import jax.numpy as jnp
from jax import lax
from jax.experimental import pallas as pl
from jax.experimental.pallas import tpu as pltpu
from jax.sharding import PartitionSpec as P

ITERS = 5
COEF_A = 3.4445
COEF_B = -4.775
COEF_C = 2.0315

RING = 4
BLOCK = 128
ROWS_A = 80
FAR, FAR_A = 64, 48
TILE = 640
EARLY_VMEM, LATE_VMEM, RENEW_VMEM = 18, 12, 26


def along_x(array, step):
    pairs = [(z * RING + x, z * RING + (x + step) % RING) for z in range(2) for x in range(RING)]
    return lax.ppermute(array, "grp", pairs)


def across_z(array):
    return lax.ppermute(array, "grp", [(g, (g + RING) % (2 * RING)) for g in range(2 * RING)])


def to_other_core(array):
    return lax.ppermute(array, "rep", [(r, r ^ 1) for r in range(16)])


def to_chip(array, step_y, step_z):
    pairs = []
    for y in range(4):
        for z in range(2):
            for core in range(2):
                source = (y * 2 + z) * 2 + core
                target = (((y + step_y) % 4) * 2 + (z + step_z) % 2) * 2 + core
                pairs.append((source, target))
    return lax.ppermute(array, "rep", pairs)


def contract(left, right, left_dim, right_dim):
    return lax.dot_general(
        left, right, (((left_dim,), (right_dim,)), ((), ())), preferred_element_type=jnp.float32
    )


def halves(value):
    high = value.astype(jnp.bfloat16)
    return high, (value - high.astype(jnp.float32)).astype(jnp.bfloat16)


def product(left, right):
    high, low = left
    right_high, right_low = right
    wide = contract(
        jnp.concatenate([high, low], 1), jnp.concatenate([right_high, right_high], 0), 1, 0
    )
    return wide + contract(high, right_low, 1, 0)


def orthogonal_factors(grams, width):
    size = grams[0].shape[0]
    eye = (
        lax.broadcasted_iota(jnp.int32, (size, size), 0)
        == lax.broadcasted_iota(jnp.int32, (size, size), 1)
    ).astype(jnp.float32)
    scales, current = [], []
    for gram in grams:
        square_sum = jnp.sum(gram * eye, keepdims=True)
        scale = 1.0 / (jnp.sqrt(square_sum) + 1e-07)
        scales.append(scale)
        current.append(gram * scale * scale)
    totals = None
    for number in range(ITERS):
        split = [halves(gram) for gram in current]
        squares = [product(gram, gram) for gram in split]
        steps = [
            COEF_A * eye + COEF_B * gram + COEF_C * square for gram, square in zip(current, squares)
        ]
        step_split = [halves(step) for step in steps]
        if totals is None:
            totals_next = steps
        else:
            total_split = [halves(total) for total in totals]
            totals_next = [product(s, t) for s, t in zip(step_split, total_split)]
        if number < ITERS - 1:
            half = [halves(product(s, g)) for s, g in zip(step_split, split)]
            current = [product(h, s) for h, s in zip(half, step_split)]
        totals = totals_next
    factor = 0.2 * math.sqrt(width)
    return [total * (scale * factor) for total, scale in zip(totals, scales)]


class Copies:
    def __init__(self, sems):
        self.sems, self.count = sems, 0

    def start(self, source, target):
        copy = pltpu.make_async_copy(source, target, self.sems.at[self.count])
        copy.start()
        self.count += 1
        return copy


def start_tokens(copies, pieces, spans, tokens, offset=0):
    started = []
    for piece, (begin, count) in zip(pieces, spans):
        target = tokens.at[pl.ds(offset, count)]
        started.append(copies.start(piece.at[pl.ds(begin, count)], target))
        offset += count
    return started


def start_upstream(copies, place_ref, first_block, upstream_ref, upstream):
    started = []
    for block in range(upstream.shape[0] // BLOCK):
        begin = pl.multiple_of(place_ref[first_block + block] * BLOCK, BLOCK)
        target = upstream.at[pl.ds(block * BLOCK, BLOCK)]
        started.append(copies.start(upstream_ref.at[pl.ds(begin, BLOCK)], target))
    return started


def wait_all(copies):
    for copy in copies:
        copy.wait()


def head_gradient(queries, upstream, gain):
    inverse = lax.rsqrt(jnp.mean(queries * queries, axis=0, keepdims=True) + 1e-06)
    normed = queries * inverse
    scaled = gain * upstream
    projection = jnp.mean(normed * scaled, axis=0, keepdims=True)
    return (scaled - normed * projection) * inverse


def rotated_gradient(
    place_ref, first_block, gain_ref, ids_ref, tokens, weight, upstream, turned, rotated, base, ready
):
    rows = upstream.shape[0]
    size = gain_ref.shape[0]
    heads = weight.shape[0] // size
    for block in range(rows // BLOCK):
        span = slice(block * BLOCK, (block + 1) * BLOCK)
        for head in range(heads):
            columns = slice(head * size, (head + 1) * size)
            turned[columns, span] = upstream[span, columns].astype(jnp.float32).T
    live = []
    for block in range(rows // BLOCK):
        ids = ids_ref[pl.ds(place_ref[first_block + block], 1), :]
        live.append((ids != 0).astype(jnp.float32))
    gain = gain_ref[...]
    wait_all(ready)
    for block in range(rows // BLOCK):
        span = pl.ds(base + block * BLOCK, BLOCK)
        queries = contract(weight[...], tokens[span, :], 1, 1)
        for head in range(heads):
            columns = slice(head * size, (head + 1) * size)
            there = slice(block * BLOCK, (block + 1) * BLOCK)
            grad = head_gradient(queries[columns], turned[columns, there], gain)
            rotated[columns, span] = (grad * live[block]).astype(jnp.bfloat16)


def early_kernel(first_block, spans, *refs):
    count = len(spans)
    place_ref, gain_ref, ids_ref, upstream_ref, weight = refs[:5]
    pieces, refs = refs[5 : 5 + count], refs[5 + count :]
    out_ref, zero_ref, tokens, upstream, turned, rotated, sems = refs
    copies = Copies(sems)
    needed = start_upstream(copies, place_ref, first_block, upstream_ref, upstream)
    ready = start_tokens(copies, pieces, spans, tokens)
    zero_ref[0] = 0
    wait_all(needed)
    rotated_gradient(
        place_ref, first_block, gain_ref, ids_ref, tokens, weight, upstream, turned, rotated, 0, ready
    )

    @pl.loop(0, out_ref.shape[1] // TILE)
    def _(tile):
        columns = pl.ds(pl.multiple_of(tile * TILE, TILE), TILE)
        out_ref[:, columns] = contract(rotated[...], tokens[:, columns], 1, 0)


def late_kernel(first_block, spans, *refs):
    count = len(spans)
    place_ref, gain_ref, ids_ref, upstream_ref, weight = refs[:5]
    pieces, refs = refs[5 : 5 + count], refs[5 + count :]
    out_ref, tokens, upstream, turned, sems = refs
    copies = Copies(sems)
    needed = start_upstream(copies, place_ref, first_block, upstream_ref, upstream)
    ready = start_tokens(copies, pieces, spans, tokens)
    wait_all(needed)
    rotated_gradient(
        place_ref, first_block, gain_ref, ids_ref, tokens, weight, upstream, turned, out_ref, 0, ready
    )


def renew_kernel(first_block, late_spans, spans, *refs):
    late_count, count = len(late_spans), len(spans)
    place_ref, gain_ref, ids_ref, upstream_ref, weight, before_ref, late_ref = refs[:7]
    late, refs = refs[7 : 7 + late_count], refs[7 + late_count :]
    pieces, (mine_ref, theirs_ref) = refs[:count], refs[count : count + 2]
    tokens, upstream, turned, rotated, split, factors, sems = refs[count + 2 :]
    all_rows, width = weight.shape
    size = gain_ref.shape[0]
    heads = all_rows // size
    tiles = width // TILE
    rows = upstream.shape[0]
    late_rows = tokens.shape[0] - rows
    copies = Copies(sems)
    needed = start_upstream(copies, place_ref, first_block, upstream_ref, upstream)
    ready = start_tokens(copies, pieces, spans, tokens, late_rows)
    others = start_tokens(copies, late, late_spans, tokens)
    rotated[:, :late_rows] = late_ref[...]
    wait_all(needed)
    rotated_gradient(
        place_ref, first_block, gain_ref, ids_ref, tokens, weight, upstream, turned, rotated,
        late_rows, ready,
    )
    wait_all(others)

    @pl.loop(0, tiles)
    def _(tile):
        columns = pl.ds(pl.multiple_of(tile * TILE, TILE), TILE)
        part = contract(rotated[...], tokens[:, columns], 1, 0) + before_ref[:, columns]
        high, low = halves(part)
        for head in range(heads):
            span = slice(head * size, (head + 1) * size)
            split[head, :size, columns] = high[span]
            split[head, size:, columns] = low[span]

    grams = []
    for head in range(heads):
        both = split[head]
        whole = contract(both, both, 1, 1)
        grams.append(
            whole[:size, :size] + whole[:size, size:] + whole[size:, :size] + whole[size:, size:]
        )
    for head, factor in enumerate(orthogonal_factors(grams, width)):
        high, low = halves(factor)
        factors[head, :size, :size] = high
        factors[head, :size, size:] = high
        factors[head, size:, :size] = low
        factors[head, size:, size:] = jnp.zeros_like(low)

    core_is_zero = place_ref[10] == 0
    indices = []
    for chip in range(8):
        step_y = lax.rem(chip // 2 - place_ref[8] + 4, 4)
        step_z = lax.rem(chip % 2 - place_ref[9] + 2, 2)
        indices.append(step_y * 2 + step_z)

    @pl.loop(0, tiles)
    def _(tile):
        columns = pl.ds(pl.multiple_of(tile * TILE, TILE), TILE)
        for pair in range(heads // 2):
            renewed = []
            for head in (2 * pair, 2 * pair + 1):
                both = contract(factors[head], split[head, :, columns], 1, 0)
                change = both[:size] + both[size:]
                old = weight[head * size : (head + 1) * size, columns].astype(jnp.float32)
                renewed.append(old - change)
            span = pl.ds(pair * 16, 16)
            for chip, index in enumerate(indices):
                parts = []
                for core in range(2):
                    begin = (chip * 2 + core) * 8
                    parts.append(
                        jnp.concatenate([value[begin : begin + 8] for value in renewed], 0)
                    )
                mine = jnp.where(core_is_zero, parts[0], parts[1])
                theirs = jnp.where(core_is_zero, parts[1], parts[0])
                mine_ref[index, span, columns] = mine.astype(jnp.bfloat16)
                theirs_ref[index, span, columns] = theirs.astype(jnp.bfloat16)


ANYWHERE = pl.BlockSpec(memory_space=pl.ANY)
INSIDE = pl.BlockSpec(memory_space=pltpu.VMEM)
SCALARS = pl.BlockSpec(memory_space=pltpu.SMEM)


def call(kernel, out_shape, in_specs, out_specs, scratch, flops, moved, vmem, operands):
    return pl.pallas_call(
        kernel,
        out_shape=out_shape,
        in_specs=in_specs,
        out_specs=out_specs,
        scratch_shapes=scratch,
        compiler_params=pltpu.CompilerParams(vmem_limit_bytes=vmem * 1024 * 1024),
        cost_estimate=pl.CostEstimate(flops=flops, bytes_accessed=moved, transcendentals=0),
    )(*operands)


def scratch_of(common, rows):
    all_rows, width = common[-1].shape
    return [
        pltpu.VMEM((rows, all_rows), jnp.bfloat16),
        pltpu.VMEM((all_rows, rows), jnp.float32),
    ]


def arrays_of(pieces):
    return [piece[0] if isinstance(piece, tuple) else piece for piece in pieces]


def spans_of(pieces):
    return [piece[1:] if isinstance(piece, tuple) else (0, piece.shape[0]) for piece in pieces]


def rows_of(pieces):
    return sum(count for _, count in spans_of(pieces))


COMMON_SPECS = [SCALARS, INSIDE, INSIDE, ANYWHERE, INSIDE]


def early_call(common, first_block, pieces):
    all_rows, width = common[-1].shape
    rows = rows_of(pieces)
    return call(
        functools.partial(early_kernel, first_block, spans_of(pieces)),
        (
            jax.ShapeDtypeStruct((all_rows, width), jnp.float32),
            jax.ShapeDtypeStruct((1,), jnp.int32),
        ),
        COMMON_SPECS + [ANYWHERE] * len(pieces),
        (INSIDE, SCALARS),
        [pltpu.VMEM((rows, width), jnp.bfloat16)]
        + scratch_of(common, rows)
        + [
            pltpu.VMEM((all_rows, rows), jnp.bfloat16),
            pltpu.SemaphoreType.DMA((len(pieces) + rows // BLOCK,)),
        ],
        4 * rows * all_rows * width,
        (6 * all_rows + 2 * rows) * width,
        EARLY_VMEM,
        [*common, *arrays_of(pieces)],
    )


def late_call(common, first_block, pieces):
    all_rows, width = common[-1].shape
    rows = rows_of(pieces)
    return call(
        functools.partial(late_kernel, first_block, spans_of(pieces)),
        jax.ShapeDtypeStruct((all_rows, rows), jnp.bfloat16),
        COMMON_SPECS + [ANYWHERE] * len(pieces),
        INSIDE,
        [pltpu.VMEM((rows, width), jnp.bfloat16)]
        + scratch_of(common, rows)
        + [pltpu.SemaphoreType.DMA((len(pieces) + rows // BLOCK,))],
        2 * rows * all_rows * width,
        2 * (rows + all_rows) * width,
        LATE_VMEM,
        [*common, *arrays_of(pieces)],
    )


def renew_call(common, first_block, before, late_rotated, late, pieces):
    all_rows, width = common[-1].shape
    size = common[1].shape[0]
    heads = all_rows // size
    rows = rows_of(pieces)
    total = rows + rows_of(late)
    shape = jax.ShapeDtypeStruct((8, all_rows // 16, width), jnp.bfloat16)
    return call(
        functools.partial(renew_kernel, first_block, spans_of(late), spans_of(pieces)),
        (shape, shape),
        COMMON_SPECS + [INSIDE, INSIDE] + [ANYWHERE] * (len(late) + len(pieces)),
        (INSIDE, INSIDE),
        [pltpu.VMEM((total, width), jnp.bfloat16)]
        + scratch_of(common, rows)
        + [
            pltpu.VMEM((all_rows, total), jnp.bfloat16),
            pltpu.VMEM((heads, 2 * size, width), jnp.bfloat16),
            pltpu.VMEM((heads, 2 * size, 2 * size), jnp.bfloat16),
            pltpu.SemaphoreType.DMA((len(late) + len(pieces) + rows // BLOCK,)),
        ],
        (4 * rows + 16 * size) * all_rows * width,
        8 * all_rows * width,
        RENEW_VMEM,
        [*common, before, late_rotated, *arrays_of(late), *arrays_of(pieces)],
    )


def shards(
    activations,
    token_ids,
    cotangent,
    inner_weight,
    query_gain,
    outer_weight,
    momentum,
    average_weight,
):
    weights = inner_weight[0]
    head_count, head_size, model_width = weights.shape
    flat_weight = weights.reshape(head_count * head_size, model_width)

    place = lax.axis_index("grp")
    spot = lax.axis_index("rep")
    numbers = []
    for step_z, step_x in ((0, 0), (0, -1), (0, 1), (1, 0), (0, 2), (1, -1), (1, 1), (1, 2)):
        numbers.append(((place // RING + step_z) % 2) * RING + (place + step_x) % RING)
    numbers += [spot // 4, (spot // 2) % 2, spot % 2]
    common = (
        jnp.stack(numbers).astype(jnp.int32),
        query_gain[:, None],
        token_ids.reshape(2 * RING, BLOCK),
        cotangent,
        flat_weight,
    )

    left, right = along_x(activations, 1), along_x(activations, -1)
    over_a = across_z(activations[:ROWS_A])
    over_left_a, over_right_a = along_x(over_a, 1), along_x(over_a, -1)
    over_b = across_z(activations[ROWS_A:])
    far0, far1 = along_x(left[:FAR], 1), along_x(right[FAR:], -1)
    over_b2 = across_z(jnp.concatenate([left[ROWS_A:], right[ROWS_A:]]))
    before, zero = early_call(common, 0, [activations, left, right, over_a, over_b])
    over_far0 = along_x(lax.dynamic_slice_in_dim(over_left_a, zero[0], FAR_A), 1)
    over_far1 = along_x(
        lax.dynamic_slice_in_dim(over_right_a, zero[0] + FAR_A, ROWS_A - FAR_A), -1
    )
    over_far_b = across_z(
        lax.dynamic_slice_in_dim(far1, zero[0] + ROWS_A - FAR, BLOCK - ROWS_A)
    )
    rows_b = BLOCK - ROWS_A
    late = [far0, far1, over_left_a, (over_b2, 0, rows_b), over_right_a, (over_b2, rows_b, rows_b)]
    late_rotated = late_call(common, 4, late)
    mine, theirs = renew_call(
        common, 7, before, late_rotated, late, [over_far0, over_far1, over_far_b]
    )

    theirs = to_other_core(theirs)
    summed = None
    for step_y, step_z in ((2, 1), (1, 1), (3, 1), (1, 0), (3, 0), (2, 0), (0, 1), (0, 0)):
        index = step_y * 2 + step_z
        pair = mine[index].astype(jnp.float32) + theirs[index].astype(jnp.float32)
        if index:
            pair = to_chip(pair.astype(jnp.bfloat16), step_y, step_z).astype(jnp.float32)
        summed = pair if summed is None else summed + pair
    summed = summed.reshape(outer_weight.shape)

    mean_weight = summed / lax.axis_size("rep")
    pseudo = outer_weight - mean_weight
    new_momentum = 0.9 * momentum + pseudo
    new_outer = outer_weight - 0.7 * (pseudo + 0.9 * new_momentum)
    new_average = 0.9 * average_weight + 0.1 * new_outer
    return (new_outer, new_momentum, new_average)


def solution(mesh):
    placed = (
        P(("rep", "grp"), None),
        P("rep"),
        P("rep", "grp"),
        P("rep", "grp", None, None),
        P(),
        P("grp", "rep", None),
        P("grp", "rep", None),
        P("grp", "rep", None),
    )
    return jax.shard_map(
        shards,
        mesh=mesh,
        in_specs=placed,
        out_specs=(P("grp", "rep", None), P("grp", "rep", None), P("grp", "rep", None)),
        check_vma=False,
    )
```

time: 549 us -> 157 us (0.29); the launches traced: 540 us -> 156 us
  blocking collectives: 230 us -> 0 us
  matrix products: 175 us -> 0 us
  waiting for transfers between devices: 115 us -> 49.3 us
  Pallas kernels: 0 us -> 40.7 us
  starting transfers between devices: 0.04 us -> 36 us
  local copies, waits for them, and re-layouts: 1.51 us -> 21.9 us
  between operations: 14.4 us -> 4.75 us
    psum x1 -> x0, blocking collectives: 230 us -> none  [shards(): summed = lax.psum(renewed, 'rep')]
    dot_general x17 -> x0, matrix products: 175 us -> none  [the longest x5 92 us: orthogonalize(): jnp.einsum('hij,hjk->hik', polynomial, iterate, precision=lax.Precision.H...]
    all_gather x1 -> x0, waiting for transfers between devices: 114 us -> none  [shards(): shard_rows = lax.all_gather(activations, 'grp', axis=0, tiled=True)]
    ppermute x0 -> x20, waiting for transfers between devices: none -> 49.3 us  [the longest x7 24.4 us: to_chip(): return lax.ppermute(array, 'rep', pairs)]
    pallas_call x0 -> x3, Pallas kernels: none -> 40.7 us  [call(): pl.pallas_call(kernel, out_shape=out_shape, in_specs=in_specs, out_specs=...]
    ppermute x0 -> x20, starting transfers between devices: none -> 36 us  [the longest x7 16.5 us: to_chip(): return lax.ppermute(array, 'rep', pairs)]
    unnamed x12 -> x30, local copies, waits for them, and re-layouts: 0.02 us -> 12.1 us
    slice x0 -> x6, local copies, waits for them, and re-layouts: none -> 9.26 us  [the longest x2 4.03 us: shards(): far0, far1 = (along_x(left[:FAR], 1), along_x(right[FAR:], -1))]
  transfers between devices with their start and end apart: 1 -> 20, of which waited for: 1 -> 8; matrix products, arithmetic and copies ran while one was open for 0% -> 7% of each run, Pallas kernels for 0% -> 13%
where the time goes in v1:
time: 157 us; the launch traced here: 156 us
  waiting for transfers between devices  49.3 us (31%)
  Pallas kernels  40.7 us (26%)
  starting transfers between devices  36 us (23%)
  local copies, waits for them, and re-layouts  21.9 us (14%)
  between operations  4.75 us (3%)
  other arithmetic  3.69 us (2%)
    pallas_call x3, Pallas kernels, call(): pl.pallas_call(kernel, out_shape=out_shape, in_specs=in_specs, out_specs=...  40.7 us
    ppermute x7, waiting for transfers between devices, to_chip(): return lax.ppermute(array, 'rep', pairs)  24.4 us
    ppermute x7, starting transfers between devices, to_chip(): return lax.ppermute(array, 'rep', pairs)  16.5 us
    ppermute x4, waiting for transfers between devices, across_z(): lax.ppermute(array, 'grp', [(g, (g + RING) % (2 * RING)) for g in range(2...  15.6 us
    ppermute x8, starting transfers between devices, along_x(): return lax.ppermute(array, 'grp', pairs)  12.1 us
    unnamed x30, local copies, waits for them, and re-layouts  12.1 us
    ppermute x8, waiting for transfers between devices, along_x(): return lax.ppermute(array, 'grp', pairs)  4.82 us
    ppermute x1, waiting for transfers between devices, to_other_core(): return lax.ppermute(array, 'rep', [(r, r ^ 1) for r in range(16)])  4.54 us
  transfers between devices with their start and end apart: 20, of which 8 were waited for; matrix products, arithmetic and copies ran while one was open for 7% of the time, Pallas kernels for 13%

profile of v1, /device:TPU:1, one launch (start us, length us, event | category | flops | bytes accessed | tf_op | source)
XLA Modules:
  0.0 156.4 jit_solution(10415053857791806870)
XLA Ops:
  0.6 3.4 %collective-permute-start.1 = (bf16[128,5120]{1,0:T(8,128)(2,1)}, bf16[128,5120]{1,0:T(8,128)(2,1)}, u32[]{:S(2)}, u32[]{:S(2)}) collective-permute-start(bf16[128,5120]{1,0:T(8,128)(2,1)} %refs_5_.1), channel_id=1, source_target_pairs={{0,3},{1,0},{2,1},{3,2},{4,7},{5,4},{6,5},{7,6},{8,11},{9,8},{10,9... | collective-permute-start | bytes 3932168 | tf_op jit(solution)/shard_map/ppermute | solution.py:26
  4.0 1.3 slice.66
  5.3 1.7 %collective-permute-start.2 = (bf16[80,5120]{1,0:T(8,128)(2,1)S(1)}, bf16[80,5120]{1,0:T(8,128)(2,1)}, u32[]{:S(2)}, u32[]{:S(2)}) collective-permute-start(bf16[80,5120]{1,0:T(8,128)(2,1)S(1)} %slice.66), channel_id=1, source_target_pairs={{0,4},{1,5},{2,6},{3,7},{4,0},{5,1},{6,2},{7,3},{8,12},{9,13},{10,... | collective-permute-start | bytes 2457608 | tf_op jit(solution)/shard_map/ppermute | solution.py:30
  7.0 1.8 %slice.67 = bf16[48,5120]{1,0:T(8,128)(2,1)} slice(bf16[128,5120]{1,0:T(8,128)(2,1)} %refs_5_.1), slice={[80:128], [0:5120]} | slice | bytes 983040 | tf_op jit(solution)/shard_map/slice | solution.py:423
  9.1 15.6 %collective-permute-done.2.refs_8_ = bf16[80,5120]{1,0:T(8,128)(2,1)} collective-permute-done((bf16[80,5120]{1,0:T(8,128)(2,1)S(1)}, bf16[80,5120]{1,0:T(8,128)(2,1)}, u32[]{:S(2)}, u32[]{:S(2)}) %collective-permute-start.2) | collective-permute-done | bytes 819232 | tf_op jit(solution)/shard_map/ppermute | solution.py:30
  24.6 2.3 %collective-permute-start.8 = (bf16[80,5120]{1,0:T(8,128)(2,1)}, bf16[80,5120]{1,0:T(8,128)(2,1)S(1)}, u32[]{:S(2)}, u32[]{:S(2)}) collective-permute-start(bf16[80,5120]{1,0:T(8,128)(2,1)} %collective-permute-done.2.refs_8_), channel_id=1, source_target_pairs={{0,3},{1,0},{2,1},{3,2},{4,7},{5,4},{6,5},{7,6},{8,11},{9,8},{10,9... | collective-permute-start | bytes 2457608 | tf_op jit(solution)/shard_map/ppermute | solution.py:26
  27.0 4.8 %collective-permute-done.1.refs_7_ = bf16[128,5120]{1,0:T(8,128)(2,1)} collective-permute-done((bf16[128,5120]{1,0:T(8,128)(2,1)}, bf16[128,5120]{1,0:T(8,128)(2,1)}, u32[]{:S(2)}, u32[]{:S(2)}) %collective-permute-start.1) | collective-permute-done | bytes 1310752 | tf_op jit(solution)/shard_map/ppermute | solution.py:26
  31.8 2.1 %slice.89 = bf16[64,5120]{1,0:T(8,128)(2,1)} slice(bf16[128,5120]{1,0:T(8,128)(2,1)} %collective-permute-done.1.refs_7_), slice={[64:128], [0:5120]} | slice | bytes 1310720 | tf_op jit(solution)/shard_map/slice | solution.py:424
  33.9 3.4 %collective-permute-start.5 = (bf16[64,5120]{1,0:T(8,128)(2,1)}, bf16[64,5120]{1,0:T(8,128)(2,1)S(1)}, u32[]{:S(2)}, u32[]{:S(2)}) collective-permute-start(bf16[64,5120]{1,0:T(8,128)(2,1)} %slice.89), channel_id=1, source_target_pairs={{0,3},{1,0},{2,1},{3,2},{4,7},{5,4},{6,5},{7,6},{8,11},{9,8},{10,9... | collective-permute-start | bytes 1966088 | tf_op jit(solution)/shard_map/ppermute | solution.py:26
  37.3 2.0 %slice.88 = bf16[64,5120]{1,0:T(8,128)(2,1)} slice(bf16[128,5120]{1,0:T(8,128)(2,1)} %collective-permute-done.refs_6_), slice={[0:64], [0:5120]} | slice | bytes 1310720 | tf_op jit(solution)/shard_map/slice | solution.py:424
  39.2 1.1 slice.91
  40.3 1.1 slice.90
  43.2 1.6 %collective-permute-start.7 = (bf16[96,5120]{1,0:T(8,128)(2,1)}, bf16[96,5120]{1,0:T(8,128)(2,1)S(1)}, u32[]{:S(2)}, u32[]{:S(2)}) collective-permute-start(bf16[96,5120]{1,0:T(8,128)(2,1)} %pad_maximum_fusion), channel_id=1, source_target_pairs={{0,4},{1,5},{2,6},{3,7},{4,0},{5,1},{6,2},{7,3},{8,12},{9,13},{10,... | collective-permute-start | bytes 2949128 | tf_op jit(solution)/shard_map/ppermute | solution.py:30
  44.8 1.2 copy-done.4
  47.1 13.9 %shard_map.103 = (f32[512,5120]{1,0:T(8,128)S(1)}, s32[1]{0:T(128)}) custom-call(s32[11]{0:T(128)S(1)} %stack.47.refs_0_, f32[128,1]{1,0:T(8,128)S(1)} %copy.13.refs_1_, s32[8,128]{1,0:T(8,128)S(1)} %bitcast.40, bf16[1024,512]{1,0:T(8,128)(2,1)S(1)} %copy-done.4, bf16[512,5120]{1,0:T(8,128)(2,1)S(1)} %bitcast.37, bf16[128,5120]{1,0:T(8,128)(2,1)S(1)} %copy-done.3, ...), custom_call_target="tpu_custom_call" | custom-call | flops 5368709120 | bytes 20971520 | tf_op jit(solution)/shard_map/pallas_call | solution.py:289
  61.0 4.0 %copy-done.9 = f32[512,5120]{1,0:T(8,128)} copy-done((f32[512,5120]{1,0:T(8,128)}, f32[512,5120]{1,0:T(8,128)S(1)}, u32[]{:S(2)}) %copy-start.9) | copy-done | bytes 10485784
  69.5 2.9 %collective-permute-start.10 = (bf16[32,5120]{1,0:T(8,128)(2,1)S(1)}, bf16[32,5120]{1,0:T(8,128)(2,1)S(1)}, u32[]{:S(2)}, u32[]{:S(2)}) collective-permute-start(bf16[32,5120]{1,0:T(8,128)(2,1)S(1)} %constant_dynamic-slice_fusion.1), channel_id=1, source_target_pairs={{0,3},{1,0},{2,1},{3,2},{4,7},{5,4},{6,5},{7,6},{8,11},{9,8},{10,9... | collective-permute-start | bytes 983048 | tf_op jit(solution)/shard_map/ppermute | solution.py:26
  72.4 2.5 %copy-done.1 = bf16[1,4,128,5120]{3,2,1,0:T(8,128)(2,1)S(1)} copy-done((bf16[1,4,128,5120]{3,2,1,0:T(8,128)(2,1)S(1)}, bf16[1,4,128,5120]{3,2,1,0:T(8,128)(2,1)}, u32[]{:S(2)}) %copy-start.1) | copy-done | bytes 5242904
  74.9 7.0 %shard_map.104.refs_6_ = bf16[512,384]{1,0:T(8,128)(2,1)S(1)} custom-call(s32[11]{0:T(128)S(1)} %stack.47.refs_0_, f32[128,1]{1,0:T(8,128)S(1)} %copy.13.refs_1_, s32[8,128]{1,0:T(8,128)S(1)} %bitcast.41, bf16[1024,512]{1,0:T(8,128)(2,1)S(1)} %copy-done.5, bf16[512,5120]{1,0:T(8,128)(2,1)S(1)} %bitcast.38, ...), custom_call_target="tpu_custom_call" | custom-call | flops 2013265920 | bytes 9175040 | tf_op jit(solution)/shard_map/pallas_call | solution.py:289
  82.0 2.5 %copy-done.2 = bf16[1,4,128,5120]{3,2,1,0:T(8,128)(2,1)S(1)} copy-done((bf16[1,4,128,5120]{3,2,1,0:T(8,128)(2,1)S(1)}, bf16[1,4,128,5120]{3,2,1,0:T(8,128)(2,1)}, u32[]{:S(2)}) %copy-start.2) | copy-done | bytes 5242904
  84.5 19.8 %shard_map.105 = (bf16[8,32,5120]{2,1,0:T(8,128)(2,1)S(1)}, bf16[8,32,5120]{2,1,0:T(8,128)(2,1)S(1)}) custom-call(s32[11]{0:T(128)S(1)} %stack.47.refs_0_, f32[128,1]{1,0:T(8,128)S(1)} %copy.13.refs_1_, s32[8,128]{1,0:T(8,128)S(1)} %bitcast.42, bf16[1024,512]{1,0:T(8,128)(2,1)S(1)} %copy-done.5, bf16[512,5120]{1,0:T(8,128)(2,1)S(1)} %bitcast.39, ...), custom_call_target="tpu_custom_call" | custom-call | flops 6710886400 | bytes 20971520 | tf_op jit(solution)/shard_map/pallas_call | solution.py:289
  104.3 4.0 %collective-permute-start.12 = (bf16[8,32,5120]{2,1,0:T(8,128)(2,1)S(1)}, bf16[8,32,5120]{2,1,0:T(8,128)(2,1)S(1)}, u32[]{:S(2)}, u32[]{:S(2)}) collective-permute-start(bf16[8,32,5120]{2,1,0:T(8,128)(2,1)S(1)} %get-tuple-element.10), channel_id=1, source_target_pairs={{0,8},{8,0},{16,24},{24,16},{32,40},{40,32},{48,56},{56,48},{64,72... | collective-permute-start | bytes 7864328 | tf_op jit(solution)/shard_map/ppermute | solution.py:34
  108.3 4.5 %collective-permute-done.12 = bf16[8,32,5120]{2,1,0:T(8,128)(2,1)S(1)} collective-permute-done((bf16[8,32,5120]{2,1,0:T(8,128)(2,1)S(1)}, bf16[8,32,5120]{2,1,0:T(8,128)(2,1)S(1)}, u32[]{:S(2)}, u32[]{:S(2)}) %collective-permute-start.12) | collective-permute-done | bytes 2621472 | tf_op jit(solution)/shard_map/ppermute | solution.py:34
  113.6 6.3 %collective-permute-start.13 = (bf16[32,5120]{1,0:T(8,128)(2,1)S(1)}, bf16[32,5120]{1,0:T(8,128)(2,1)S(1)}, u32[]{:S(2)}, u32[]{:S(2)}) collective-permute-start(bf16[32,5120]{1,0:T(8,128)(2,1)S(1)} %get-tuple-element.14), channel_id=1, source_target_pairs={{0,80},{8,88},{16,64},{24,72},{32,112},{40,120},{48,96},{56,104},{... | collective-permute-start | bytes 983048 | tf_op jit(solution)/shard_map/ppermute | solution.py:45
  120.3 2.4 %collective-permute-start.17 = (bf16[32,5120]{1,0:T(8,128)(2,1)S(1)}, bf16[32,5120]{1,0:T(8,128)(2,1)S(1)}, u32[]{:S(2)}, u32[]{:S(2)}) collective-permute-start(bf16[32,5120]{1,0:T(8,128)(2,1)S(1)} %get-tuple-element.17), channel_id=1, source_target_pairs={{0,96},{8,104},{16,112},{24,120},{32,0},{40,8},{48,16},{56,24},{64... | collective-permute-start | bytes 983048 | tf_op jit(solution)/shard_map/ppermute | solution.py:45
  122.8 5.0 %collective-permute-done.13 = bf16[32,5120]{1,0:T(8,128)(2,1)S(1)} collective-permute-done((bf16[32,5120]{1,0:T(8,128)(2,1)S(1)}, bf16[32,5120]{1,0:T(8,128)(2,1)S(1)}, u32[]{:S(2)}, u32[]{:S(2)}) %collective-permute-start.13) | collective-permute-done | bytes 327712 | tf_op jit(solution)/shard_map/ppermute | solution.py:45
  127.7 5.0 %collective-permute-start.15 = (bf16[32,5120]{1,0:T(8,128)(2,1)S(1)}, bf16[32,5120]{1,0:T(8,128)(2,1)S(1)}, u32[]{:S(2)}, u32[]{:S(2)}) collective-permute-start(bf16[32,5120]{1,0:T(8,128)(2,1)S(1)} %get-tuple-element.19), channel_id=1, source_target_pairs={{0,112},{8,120},{16,96},{24,104},{32,16},{40,24},{48,0},{56,8},{64... | collective-permute-start | bytes 983048 | tf_op jit(solution)/shard_map/ppermute | solution.py:45
  132.7 2.5 %collective-permute-done.19 = bf16[32,5120]{1,0:T(8,128)(2,1)S(1)} collective-permute-done((bf16[32,5120]{1,0:T(8,128)(2,1)S(1)}, bf16[32,5120]{1,0:T(8,128)(2,1)S(1)}, u32[]{:S(2)}, u32[]{:S(2)}) %collective-permute-start.19) | collective-permute-done | bytes 327712 | tf_op jit(solution)/shard_map/ppermute | solution.py:45
  135.2 2.4 %collective-permute-start.14 = (bf16[32,5120]{1,0:T(8,128)(2,1)S(1)}, bf16[32,5120]{1,0:T(8,128)(2,1)S(1)}, u32[]{:S(2)}, u32[]{:S(2)}) collective-permute-start(bf16[32,5120]{1,0:T(8,128)(2,1)S(1)} %get-tuple-element.20), channel_id=1, source_target_pairs={{0,48},{8,56},{16,32},{24,40},{32,80},{40,88},{48,64},{56,72},{64,... | collective-permute-start | bytes 983048 | tf_op jit(solution)/shard_map/ppermute | solution.py:45
  137.6 4.4 %collective-permute-done.17 = bf16[32,5120]{1,0:T(8,128)(2,1)S(1)} collective-permute-done((bf16[32,5120]{1,0:T(8,128)(2,1)S(1)}, bf16[32,5120]{1,0:T(8,128)(2,1)S(1)}, u32[]{:S(2)}, u32[]{:S(2)}) %collective-permute-start.17) | collective-permute-done | bytes 327712 | tf_op jit(solution)/shard_map/ppermute | solution.py:45
  142.3 12.3 %collective-permute-done.15 = bf16[32,5120]{1,0:T(8,128)(2,1)S(1)} collective-permute-done((bf16[32,5120]{1,0:T(8,128)(2,1)S(1)}, bf16[32,5120]{1,0:T(8,128)(2,1)S(1)}, u32[]{:S(2)}, u32[]{:S(2)}) %collective-permute-start.15) | collective-permute-done | bytes 327712 | tf_op jit(solution)/shard_map/ppermute | solution.py:45
  154.6 1.8 %multiply_add_fusion = (f32[4,8,5120]{2,1,0:T(8,128)}, f32[4,8,5120]{2,1,0:T(8,128)}, f32[4,8,5120]{2,1,0:T(8,128)}) fusion(f32[4,8,5120]{2,1,0:T(8,128)S(1)} %copy-done.11, f32[4,8,5120]{2,1,0:T(8,128)S(1)} %copy-done.12, f32[4,8,5120]{2,1,0:T(8,128)S(1)} %copy-done.13, bf16[8,32,5120]{2,1,0:T(8,128)(2,1)S(1)} %collective-permute-done.12, ...), kind=kLoop, calls=%fused_computation.4 | loop fusion | flops 4587520 | bytes 6881280 | tf_op jit(solution)/shard_map/add | solution.py:455
  (55 shorter events, 5.2 us)
Async XLA Ops:
  0.6 8.2 %copy-start.14 = (f32[128]{0:T(128)S(1)}, f32[128]{0:T(128)}, u32[]{:S(2)}) copy-start(f32[128]{0:T(128)} %param.12) | copy-start | bytes 1540
  0.6 31.1 %collective-permute-start.1 = (bf16[128,5120]{1,0:T(8,128)(2,1)}, bf16[128,5120]{1,0:T(8,128)(2,1)}, u32[]{:S(2)}, u32[]{:S(2)}) collective-permute-start(bf16[128,5120]{1,0:T(8,128)(2,1)} %refs_5_.1), channel_id=1, source_target_pairs={{0,3},{1,0},{2,1},{3,2},{4,7},{5,4},{6,5},{7,6},{8,11},{9,8},{10,9... | collective-permute-start | bytes 3932168 | tf_op jit(solution)/shard_map/ppermute | solution.py:26
  4.0 33.2 %collective-permute-start = (bf16[128,5120]{1,0:T(8,128)(2,1)}, bf16[128,5120]{1,0:T(8,128)(2,1)}, u32[]{:S(2)}, u32[]{:S(2)}) collective-permute-start(bf16[128,5120]{1,0:T(8,128)(2,1)} %refs_5_.1), channel_id=1, source_target_pairs={{0,1},{1,2},{2,3},{3,0},{4,5},{5,6},{6,7},{7,4},{8,9},{9,10},{10,1... | collective-permute-start | bytes 3932168 | tf_op jit(solution)/shard_map/ppermute | solution.py:26
  5.3 19.4 %collective-permute-start.2 = (bf16[80,5120]{1,0:T(8,128)(2,1)S(1)}, bf16[80,5120]{1,0:T(8,128)(2,1)}, u32[]{:S(2)}, u32[]{:S(2)}) collective-permute-start(bf16[80,5120]{1,0:T(8,128)(2,1)S(1)} %slice.66), channel_id=1, source_target_pairs={{0,4},{1,5},{2,6},{3,7},{4,0},{5,1},{6,2},{7,3},{8,12},{9,13},{10,... | collective-permute-start | bytes 2457608 | tf_op jit(solution)/shard_map/ppermute | solution.py:30
  8.8 33.6 %collective-permute-start.3 = (bf16[48,5120]{1,0:T(8,128)(2,1)}, bf16[48,5120]{1,0:T(8,128)(2,1)S(1)}, u32[]{:S(2)}, u32[]{:S(2)}) collective-permute-start(bf16[48,5120]{1,0:T(8,128)(2,1)} %slice.67), channel_id=1, source_target_pairs={{0,4},{1,5},{2,6},{3,7},{4,0},{5,1},{6,2},{7,3},{8,12},{9,13},{10,... | collective-permute-start | bytes 1474568 | tf_op jit(solution)/shard_map/ppermute | solution.py:30
  8.9 36.0 %copy-start.6 = (s32[1024]{0:T(1024)S(1)}, s32[1024]{0:T(1024)}, u32[]{:S(2)}) copy-start(s32[1024]{0:T(1024)} %param.9) | copy-start | bytes 12292
  24.6 44.7 %collective-permute-start.8 = (bf16[80,5120]{1,0:T(8,128)(2,1)}, bf16[80,5120]{1,0:T(8,128)(2,1)S(1)}, u32[]{:S(2)}, u32[]{:S(2)}) collective-permute-start(bf16[80,5120]{1,0:T(8,128)(2,1)} %collective-permute-done.2.refs_8_), channel_id=1, source_target_pairs={{0,3},{1,0},{2,1},{3,2},{4,7},{5,4},{6,5},{7,6},{8,11},{9,8},{10,9... | collective-permute-start | bytes 2457608 | tf_op jit(solution)/shard_map/ppermute | solution.py:26
  27.0 41.9 %collective-permute-start.6 = (bf16[80,5120]{1,0:T(8,128)(2,1)}, bf16[80,5120]{1,0:T(8,128)(2,1)S(1)}, u32[]{:S(2)}, u32[]{:S(2)}) collective-permute-start(bf16[80,5120]{1,0:T(8,128)(2,1)} %collective-permute-done.2.refs_8_), channel_id=1, source_target_pairs={{0,1},{1,2},{2,3},{3,0},{4,5},{5,6},{6,7},{7,4},{8,9},{9,10},{10,1... | collective-permute-start | bytes 2457608 | tf_op jit(solution)/shard_map/ppermute | solution.py:26
  31.8 13.0 %copy-start.3 = (bf16[128,5120]{1,0:T(8,128)(2,1)S(1)}, bf16[128,5120]{1,0:T(8,128)(2,1)}, u32[]{:S(2)}) copy-start(bf16[128,5120]{1,0:T(8,128)(2,1)} %refs_5_.1) | copy-start | bytes 3932164
  33.8 11.0 %copy-start = (bf16[1,4,128,5120]{3,2,1,0:T(8,128)(2,1)S(1)}, bf16[1,4,128,5120]{3,2,1,0:T(8,128)(2,1)}, u32[]{:S(2)}) copy-start(bf16[1,4,128,5120]{3,2,1,0:T(8,128)(2,1)} %param.11) | copy-start | bytes 15728644
  33.9 35.3 %collective-permute-start.5 = (bf16[64,5120]{1,0:T(8,128)(2,1)}, bf16[64,5120]{1,0:T(8,128)(2,1)S(1)}, u32[]{:S(2)}, u32[]{:S(2)}) collective-permute-start(bf16[64,5120]{1,0:T(8,128)(2,1)} %slice.89), channel_id=1, source_target_pairs={{0,3},{1,0},{2,1},{3,2},{4,7},{5,4},{6,5},{7,6},{8,11},{9,8},{10,9... | collective-permute-start | bytes 1966088 | tf_op jit(solution)/shard_map/ppermute | solution.py:26
  39.2 33.2 %collective-permute-start.4 = (bf16[64,5120]{1,0:T(8,128)(2,1)}, bf16[64,5120]{1,0:T(8,128)(2,1)}, u32[]{:S(2)}, u32[]{:S(2)}) collective-permute-start(bf16[64,5120]{1,0:T(8,128)(2,1)} %slice.88), channel_id=1, source_target_pairs={{0,1},{1,2},{2,3},{3,0},{4,5},{5,6},{6,7},{7,4},{8,9},{9,10},{10,1... | collective-permute-start | bytes 1966088 | tf_op jit(solution)/shard_map/ppermute | solution.py:26
  43.2 29.2 %collective-permute-start.7 = (bf16[96,5120]{1,0:T(8,128)(2,1)}, bf16[96,5120]{1,0:T(8,128)(2,1)S(1)}, u32[]{:S(2)}, u32[]{:S(2)}) collective-permute-start(bf16[96,5120]{1,0:T(8,128)(2,1)} %pad_maximum_fusion), channel_id=1, source_target_pairs={{0,4},{1,5},{2,6},{3,7},{4,0},{5,1},{6,2},{7,3},{8,12},{9,13},{10,... | collective-permute-start | bytes 2949128 | tf_op jit(solution)/shard_map/ppermute | solution.py:30
  61.0 4.0 %copy-start.9 = (f32[512,5120]{1,0:T(8,128)}, f32[512,5120]{1,0:T(8,128)S(1)}, u32[]{:S(2)}) copy-start(f32[512,5120]{1,0:T(8,128)S(1)} %get-tuple-element.7.refs_5_) | copy-start | bytes 31457284
  68.9 3.5 %copy-start.5 = (bf16[1024,512]{1,0:T(8,128)(2,1)S(1)}, bf16[1024,512]{1,0:T(8,128)(2,1)}, u32[]{:S(2)}) copy-start(bf16[1024,512]{1,0:T(8,128)(2,1)} %refs_3_.5) | copy-start | bytes 3145732
  69.1 12.9 %collective-permute-start.9 = (bf16[48,5120]{1,0:T(8,128)(2,1)S(1)}, bf16[48,5120]{1,0:T(8,128)(2,1)S(1)}, u32[]{:S(2)}, u32[]{:S(2)}) collective-permute-start(bf16[48,5120]{1,0:T(8,128)(2,1)S(1)} %constant_dynamic-slice_fusion.2), channel_id=1, source_target_pairs={{0,1},{1,2},{2,3},{3,0},{4,5},{5,6},{6,7},{7,4},{8,9},{9,10},{10,1... | collective-permute-start | bytes 1474568 | tf_op jit(solution)/shard_map/ppermute | solution.py:26
  69.3 12.7 %collective-permute-start.11 = (bf16[48,5120]{1,0:T(8,128)(2,1)S(1)}, bf16[48,5120]{1,0:T(8,128)(2,1)S(1)}, u32[]{:S(2)}, u32[]{:S(2)}) collective-permute-start(bf16[48,5120]{1,0:T(8,128)(2,1)S(1)} %constant_dynamic-slice_fusion), channel_id=1, source_target_pairs={{0,4},{1,5},{2,6},{3,7},{4,0},{5,1},{6,2},{7,3},{8,12},{9,13},{10,... | collective-permute-start | bytes 1474568 | tf_op jit(solution)/shard_map/ppermute | solution.py:30
  69.5 12.5 %collective-permute-start.10 = (bf16[32,5120]{1,0:T(8,128)(2,1)S(1)}, bf16[32,5120]{1,0:T(8,128)(2,1)S(1)}, u32[]{:S(2)}, u32[]{:S(2)}) collective-permute-start(bf16[32,5120]{1,0:T(8,128)(2,1)S(1)} %constant_dynamic-slice_fusion.1), channel_id=1, source_target_pairs={{0,3},{1,0},{2,1},{3,2},{4,7},{5,4},{6,5},{7,6},{8,11},{9,8},{10,9... | collective-permute-start | bytes 983048 | tf_op jit(solution)/shard_map/ppermute | solution.py:26
  72.4 2.5 %copy-start.1 = (bf16[1,4,128,5120]{3,2,1,0:T(8,128)(2,1)S(1)}, bf16[1,4,128,5120]{3,2,1,0:T(8,128)(2,1)}, u32[]{:S(2)}) copy-start(bf16[1,4,128,5120]{3,2,1,0:T(8,128)(2,1)} %param.11) | copy-start | bytes 15728644
  74.9 7.1 %copy-start.10 = (f32[512,5120]{1,0:T(8,128)S(1)}, f32[512,5120]{1,0:T(8,128)}, u32[]{:S(2)}) copy-start(f32[512,5120]{1,0:T(8,128)} %copy-done.9) | copy-start | bytes 31457284
  82.0 2.5 %copy-start.2 = (bf16[1,4,128,5120]{3,2,1,0:T(8,128)(2,1)S(1)}, bf16[1,4,128,5120]{3,2,1,0:T(8,128)(2,1)}, u32[]{:S(2)}) copy-start(bf16[1,4,128,5120]{3,2,1,0:T(8,128)(2,1)} %param.11) | copy-start | bytes 15728644
  104.3 8.5 %collective-permute-start.12 = (bf16[8,32,5120]{2,1,0:T(8,128)(2,1)S(1)}, bf16[8,32,5120]{2,1,0:T(8,128)(2,1)S(1)}, u32[]{:S(2)}, u32[]{:S(2)}) collective-permute-start(bf16[8,32,5120]{2,1,0:T(8,128)(2,1)S(1)} %get-tuple-element.10), channel_id=1, source_target_pairs={{0,8},{8,0},{16,24},{24,16},{32,40},{40,32},{48,56},{56,48},{64,72... | collective-permute-start | bytes 7864328 | tf_op jit(solution)/shard_map/ppermute | solution.py:34
  112.8 41.8 %copy-start.11 = (f32[4,8,5120]{2,1,0:T(8,128)S(1)}, f32[4,8,5120]{2,1,0:T(8,128)}, u32[]{:S(2)}) copy-start(f32[4,8,5120]{2,1,0:T(8,128)} %param.15) | copy-start | bytes 1966084
  112.8 41.8 %copy-start.12 = (f32[4,8,5120]{2,1,0:T(8,128)S(1)}, f32[4,8,5120]{2,1,0:T(8,128)}, u32[]{:S(2)}) copy-start(f32[4,8,5120]{2,1,0:T(8,128)} %param.13) | copy-start | bytes 1966084
  112.8 41.8 %copy-start.13 = (f32[4,8,5120]{2,1,0:T(8,128)S(1)}, f32[4,8,5120]{2,1,0:T(8,128)}, u32[]{:S(2)}) copy-start(f32[4,8,5120]{2,1,0:T(8,128)} %param.14) | copy-start | bytes 1966084
  113.6 14.1 %collective-permute-start.13 = (bf16[32,5120]{1,0:T(8,128)(2,1)S(1)}, bf16[32,5120]{1,0:T(8,128)(2,1)S(1)}, u32[]{:S(2)}, u32[]{:S(2)}) collective-permute-start(bf16[32,5120]{1,0:T(8,128)(2,1)S(1)} %get-tuple-element.14), channel_id=1, source_target_pairs={{0,80},{8,88},{16,64},{24,72},{32,112},{40,120},{48,96},{56,104},{... | collective-permute-start | bytes 983048 | tf_op jit(solution)/shard_map/ppermute | solution.py:45
  120.0 15.2 %collective-permute-start.19 = (bf16[32,5120]{1,0:T(8,128)(2,1)S(1)}, bf16[32,5120]{1,0:T(8,128)(2,1)S(1)}, u32[]{:S(2)}, u32[]{:S(2)}) collective-permute-start(bf16[32,5120]{1,0:T(8,128)(2,1)S(1)} %get-tuple-element.15), channel_id=1, source_target_pairs={{0,16},{8,24},{16,0},{24,8},{32,48},{40,56},{48,32},{56,40},{64,80... | collective-permute-start | bytes 983048 | tf_op jit(solution)/shard_map/ppermute | solution.py:45
  120.0 17.6 %collective-permute-start.18 = (bf16[32,5120]{1,0:T(8,128)(2,1)S(1)}, bf16[32,5120]{1,0:T(8,128)(2,1)S(1)}, u32[]{:S(2)}, u32[]{:S(2)}) collective-permute-start(bf16[32,5120]{1,0:T(8,128)(2,1)S(1)} %get-tuple-element.16), channel_id=1, source_target_pairs={{0,64},{8,72},{16,80},{24,88},{32,96},{40,104},{48,112},{56,120},{... | collective-permute-start | bytes 983048 | tf_op jit(solution)/shard_map/ppermute | solution.py:45
  120.3 21.6 %collective-permute-start.17 = (bf16[32,5120]{1,0:T(8,128)(2,1)S(1)}, bf16[32,5120]{1,0:T(8,128)(2,1)S(1)}, u32[]{:S(2)}, u32[]{:S(2)}) collective-permute-start(bf16[32,5120]{1,0:T(8,128)(2,1)S(1)} %get-tuple-element.17), channel_id=1, source_target_pairs={{0,96},{8,104},{16,112},{24,120},{32,0},{40,8},{48,16},{56,24},{64... | collective-permute-start | bytes 983048 | tf_op jit(solution)/shard_map/ppermute | solution.py:45
  122.8 19.5 %collective-permute-start.16 = (bf16[32,5120]{1,0:T(8,128)(2,1)S(1)}, bf16[32,5120]{1,0:T(8,128)(2,1)S(1)}, u32[]{:S(2)}, u32[]{:S(2)}) collective-permute-start(bf16[32,5120]{1,0:T(8,128)(2,1)S(1)} %get-tuple-element.18), channel_id=1, source_target_pairs={{0,32},{8,40},{16,48},{24,56},{32,64},{40,72},{48,80},{56,88},{64,... | collective-permute-start | bytes 983048 | tf_op jit(solution)/shard_map/ppermute | solution.py:45
  127.7 26.8 %collective-permute-start.15 = (bf16[32,5120]{1,0:T(8,128)(2,1)S(1)}, bf16[32,5120]{1,0:T(8,128)(2,1)S(1)}, u32[]{:S(2)}, u32[]{:S(2)}) collective-permute-start(bf16[32,5120]{1,0:T(8,128)(2,1)S(1)} %get-tuple-element.19), channel_id=1, source_target_pairs={{0,112},{8,120},{16,96},{24,104},{32,16},{40,24},{48,0},{56,8},{64... | collective-permute-start | bytes 983048 | tf_op jit(solution)/shard_map/ppermute | solution.py:45
  135.2 19.4 %collective-permute-start.14 = (bf16[32,5120]{1,0:T(8,128)(2,1)S(1)}, bf16[32,5120]{1,0:T(8,128)(2,1)S(1)}, u32[]{:S(2)}, u32[]{:S(2)}) collective-permute-start(bf16[32,5120]{1,0:T(8,128)(2,1)S(1)} %get-tuple-element.20), channel_id=1, source_target_pairs={{0,48},{8,56},{16,32},{24,40},{32,80},{40,88},{48,64},{56,72},{64,... | collective-permute-start | bytes 983048 | tf_op jit(solution)/shard_map/ppermute | solution.py:45
  (3 other events, 3.0 us)

commit v2 on v1

--- a/solution.py
+++ b/solution.py
@@ -17,8 +17,8 @@
 BLOCK = 128
 ROWS_A = 80
 FAR, FAR_A = 64, 48
-TILE = 640
-EARLY_VMEM, LATE_VMEM, RENEW_VMEM = 18, 12, 26
+TILE = 1280
+EARLY_VMEM, LATE_VMEM, RENEW_VMEM, PICK_VMEM = 18, 12, 26, 8
 
 
 def along_x(array, step):
@@ -132,10 +132,9 @@
         copy.wait()
 
 
-def head_gradient(queries, upstream, gain):
+def head_gradient(queries, scaled):
     inverse = lax.rsqrt(jnp.mean(queries * queries, axis=0, keepdims=True) + 1e-06)
     normed = queries * inverse
-    scaled = gain * upstream
     projection = jnp.mean(normed * scaled, axis=0, keepdims=True)
     return (scaled - normed * projection) * inverse
 
@@ -144,38 +143,39 @@
     place_ref, first_block, gain_ref, ids_ref, tokens, weight, upstream, turned, rotated, base, ready
 ):
     rows = upstream.shape[0]
-    size = gain_ref.shape[0]
+    size = gain_ref.shape[1]
     heads = weight.shape[0] // size
+    gain = jnp.broadcast_to(gain_ref[...], (BLOCK, size)).T
     for block in range(rows // BLOCK):
         span = slice(block * BLOCK, (block + 1) * BLOCK)
         for head in range(heads):
             columns = slice(head * size, (head + 1) * size)
-            turned[columns, span] = upstream[span, columns].astype(jnp.float32).T
+            turned[columns, span] = gain * upstream[span, columns].astype(jnp.float32).T
     live = []
     for block in range(rows // BLOCK):
         ids = ids_ref[pl.ds(place_ref[first_block + block], 1), :]
         live.append((ids != 0).astype(jnp.float32))
-    gain = gain_ref[...]
+    live = jnp.concatenate(live, 1)
     wait_all(ready)
-    for block in range(rows // BLOCK):
-        span = pl.ds(base + block * BLOCK, BLOCK)
+    for begin in range(0, rows, 2 * BLOCK):
+        count = min(2 * BLOCK, rows - begin)
+        span = pl.ds(base + begin, count)
+        there = slice(begin, begin + count)
         queries = contract(weight[...], tokens[span, :], 1, 1)
         for head in range(heads):
             columns = slice(head * size, (head + 1) * size)
-            there = slice(block * BLOCK, (block + 1) * BLOCK)
-            grad = head_gradient(queries[columns], turned[columns, there], gain)
-            rotated[columns, span] = (grad * live[block]).astype(jnp.bfloat16)
+            grad = head_gradient(queries[columns], turned[columns, there])
+            rotated[columns, span] = (grad * live[:, there]).astype(jnp.bfloat16)
 
 
 def early_kernel(first_block, spans, *refs):
     count = len(spans)
     place_ref, gain_ref, ids_ref, upstream_ref, weight = refs[:5]
     pieces, refs = refs[5 : 5 + count], refs[5 + count :]
-    out_ref, zero_ref, tokens, upstream, turned, rotated, sems = refs
+    _, out_ref, _, tokens, upstream, turned, rotated, sems = refs
     copies = Copies(sems)
     needed = start_upstream(copies, place_ref, first_block, upstream_ref, upstream)
     ready = start_tokens(copies, pieces, spans, tokens)
-    zero_ref[0] = 0
     wait_all(needed)
     rotated_gradient(
         place_ref, first_block, gain_ref, ids_ref, tokens, weight, upstream, turned, rotated, 0, ready
@@ -208,7 +208,7 @@
     pieces, (mine_ref, theirs_ref) = refs[:count], refs[count : count + 2]
     tokens, upstream, turned, rotated, split, factors, sems = refs[count + 2 :]
     all_rows, width = weight.shape
-    size = gain_ref.shape[0]
+    size = gain_ref.shape[1]
     heads = all_rows // size
     tiles = width // TILE
     rows = upstream.shape[0]
@@ -280,18 +280,23 @@
                 theirs_ref[index, span, columns] = theirs.astype(jnp.bfloat16)
 
 
-ANYWHERE = pl.BlockSpec(memory_space=pl.ANY)
+OUTSIDE = pl.BlockSpec(memory_space=pltpu.HBM)
 INSIDE = pl.BlockSpec(memory_space=pltpu.VMEM)
 SCALARS = pl.BlockSpec(memory_space=pltpu.SMEM)
 
 
-def call(kernel, out_shape, in_specs, out_specs, scratch, flops, moved, vmem, operands):
+def outside(array):
+    return pltpu.with_memory_space_constraint(array, pltpu.HBM)
+
+
+def call(kernel, out_shape, in_specs, out_specs, scratch, flops, moved, vmem, operands, aliases=None):
     return pl.pallas_call(
         kernel,
         out_shape=out_shape,
         in_specs=in_specs,
         out_specs=out_specs,
         scratch_shapes=scratch,
+        input_output_aliases=aliases or {},
         compiler_params=pltpu.CompilerParams(vmem_limit_bytes=vmem * 1024 * 1024),
         cost_estimate=pl.CostEstimate(flops=flops, bytes_accessed=moved, transcendentals=0),
     )(*operands)
@@ -306,7 +311,7 @@
 
 
 def arrays_of(pieces):
-    return [piece[0] if isinstance(piece, tuple) else piece for piece in pieces]
+    return [outside(piece[0] if isinstance(piece, tuple) else piece) for piece in pieces]
 
 
 def spans_of(pieces):
@@ -317,20 +322,53 @@
     return sum(count for _, count in spans_of(pieces))
 
 
-COMMON_SPECS = [SCALARS, INSIDE, INSIDE, ANYWHERE, INSIDE]
-
-
-def early_call(common, first_block, pieces):
+COMMON_SPECS = [SCALARS, INSIDE, INSIDE, OUTSIDE, INSIDE]
+
+
+def pick_kernel(picks, count, *refs):
+    sources, targets, sems = refs[:count], refs[-1 - len(picks) : -1], refs[-1]
+    copies = Copies(sems)
+    started = []
+    for target, parts in zip(targets, picks):
+        offset = 0
+        for number, begin, rows in parts:
+            source = sources[number].at[pl.ds(begin, rows)]
+            started.append(copies.start(source, target.at[pl.ds(offset, rows)]))
+            offset += rows
+    wait_all(started)
+
+
+def pick_call(arrays, picks):
+    shapes = []
+    for parts in picks:
+        rows = sum(part[2] for part in parts)
+        shapes.append(jax.ShapeDtypeStruct((rows, arrays[0].shape[1]), arrays[0].dtype))
+    moved = 4 * sum(shape.size for shape in shapes)
+    scratch = [pltpu.SemaphoreType.DMA((sum(len(parts) for parts in picks),))]
+    return call(
+        functools.partial(pick_kernel, picks, len(arrays)),
+        tuple(shapes),
+        [OUTSIDE] * len(arrays),
+        (INSIDE,) * len(shapes),
+        scratch,
+        0,
+        moved,
+        PICK_VMEM,
+        list(map(outside, arrays)),
+    )
+
+
+def early_call(common, first_block, pieces, passed):
     all_rows, width = common[-1].shape
     rows = rows_of(pieces)
     return call(
         functools.partial(early_kernel, first_block, spans_of(pieces)),
         (
             jax.ShapeDtypeStruct((all_rows, width), jnp.float32),
-            jax.ShapeDtypeStruct((1,), jnp.int32),
+            jax.ShapeDtypeStruct(passed.shape, passed.dtype),
         ),
-        COMMON_SPECS + [ANYWHERE] * len(pieces),
-        (INSIDE, SCALARS),
+        COMMON_SPECS + [OUTSIDE] * (len(pieces) + 1),
+        (INSIDE, OUTSIDE),
         [pltpu.VMEM((rows, width), jnp.bfloat16)]
         + scratch_of(common, rows)
         + [
@@ -340,7 +378,8 @@
         4 * rows * all_rows * width,
         (6 * all_rows + 2 * rows) * width,
         EARLY_VMEM,
-        [*common, *arrays_of(pieces)],
+        [*common, *arrays_of(pieces), passed],
+        {len(common) + len(pieces): 1},
     )
 
 
@@ -350,7 +389,7 @@
     return call(
         functools.partial(late_kernel, first_block, spans_of(pieces)),
         jax.ShapeDtypeStruct((all_rows, rows), jnp.bfloat16),
-        COMMON_SPECS + [ANYWHERE] * len(pieces),
+        COMMON_SPECS + [OUTSIDE] * len(pieces),
         INSIDE,
         [pltpu.VMEM((rows, width), jnp.bfloat16)]
         + scratch_of(common, rows)
@@ -364,7 +403,7 @@
 
 def renew_call(common, first_block, before, late_rotated, late, pieces):
     all_rows, width = common[-1].shape
-    size = common[1].shape[0]
+    size = common[1].shape[1]
     heads = all_rows // size
     rows = rows_of(pieces)
     total = rows + rows_of(late)
@@ -372,7 +411,7 @@
     return call(
         functools.partial(renew_kernel, first_block, spans_of(late), spans_of(pieces)),
         (shape, shape),
-        COMMON_SPECS + [INSIDE, INSIDE] + [ANYWHERE] * (len(late) + len(pieces)),
+        COMMON_SPECS + [INSIDE, INSIDE] + [OUTSIDE] * (len(late) + len(pieces)),
         (INSIDE, INSIDE),
         [pltpu.VMEM((total, width), jnp.bfloat16)]
         + scratch_of(common, rows)
@@ -411,28 +450,41 @@
     numbers += [spot // 4, (spot // 2) % 2, spot % 2]
     common = (
         jnp.stack(numbers).astype(jnp.int32),
-        query_gain[:, None],
+        query_gain[None, :],
         token_ids.reshape(2 * RING, BLOCK),
-        cotangent,
+        outside(cotangent),
         flat_weight,
     )
 
+    rows_b = BLOCK - ROWS_A
     left, right = along_x(activations, 1), along_x(activations, -1)
-    over_a = across_z(activations[:ROWS_A])
+    own_a, own_b = pick_call([activations], [[(0, 0, ROWS_A)], [(0, ROWS_A, rows_b)]])
+    over_a = across_z(own_a)
     over_left_a, over_right_a = along_x(over_a, 1), along_x(over_a, -1)
-    over_b = across_z(activations[ROWS_A:])
-    far0, far1 = along_x(left[:FAR], 1), along_x(right[FAR:], -1)
-    over_b2 = across_z(jnp.concatenate([left[ROWS_A:], right[ROWS_A:]]))
-    before, zero = early_call(common, 0, [activations, left, right, over_a, over_b])
-    over_far0 = along_x(lax.dynamic_slice_in_dim(over_left_a, zero[0], FAR_A), 1)
-    over_far1 = along_x(
-        lax.dynamic_slice_in_dim(over_right_a, zero[0] + FAR_A, ROWS_A - FAR_A), -1
-    )
-    over_far_b = across_z(
-        lax.dynamic_slice_in_dim(far1, zero[0] + ROWS_A - FAR, BLOCK - ROWS_A)
-    )
-    rows_b = BLOCK - ROWS_A
-    late = [far0, far1, over_left_a, (over_b2, 0, rows_b), over_right_a, (over_b2, rows_b, rows_b)]
+    over_b = across_z(own_b)
+    left_far, right_far, right_b, sides_b = pick_call(
+        [left, right],
+        [
+            [(0, 0, FAR)],
+            [(1, FAR, ROWS_A - FAR)],
+            [(1, ROWS_A, rows_b)],
+            [(0, ROWS_A, rows_b), (1, ROWS_A, rows_b)],
+        ],
+    )
+    far_b = along_x(right_b, -1)
+    far0 = along_x(left_far, 1)
+    over_b2 = across_z(sides_b)
+    before, right_far = early_call(common, 0, [activations, left, right, over_a, over_b], right_far)
+    over_left_far, over_right_far, right_far = pick_call(
+        [over_left_a, over_right_a, right_far],
+        [[(0, 0, FAR_A)], [(1, FAR_A, ROWS_A - FAR_A)], [(2, 0, ROWS_A - FAR)]],
+    )
+    over_far0, over_far1 = along_x(over_left_far, 1), along_x(over_right_far, -1)
+    far1 = along_x(right_far, -1)
+    over_far_b = across_z(far_b)
+    late = [
+        far0, far1, far_b, over_left_a, (over_b2, 0, rows_b), over_right_a, (over_b2, rows_b, rows_b)
+    ]
     late_rotated = late_call(common, 4, late)
     mine, theirs = renew_call(
         common, 7, before, late_rotated, late, [over_far0, over_far1, over_far_b]
@@ -440,7 +492,7 @@
 
     theirs = to_other_core(theirs)
     summed = None
-    for step_y, step_z in ((2, 1), (1, 1), (3, 1), (1, 0), (3, 0), (2, 0), (0, 1), (0, 0)):
+    for step_y, step_z in ((0, 1), (2, 1), (2, 0), (3, 1), (1, 1), (3, 0), (1, 0), (0, 0)):
         index = step_y * 2 + step_z
         pair = mine[index].astype(jnp.float32) + theirs[index].astype(jnp.float32)
         if index:

time: 157 us -> 146 us (0.930)
  local copies, waits for them, and re-layouts: 21.9 us -> 6.82 us
  waiting for transfers between devices: 49.3 us -> 61.9 us
  between operations: 4.75 us -> 0.78 us
  Pallas kernels: 40.7 us -> 36.9 us
    ppermute x8 -> x9, waiting for transfers between devices: 4.82 us -> 14.8 us  [along_x(): return lax.ppermute(array, 'grp', pairs)]
    slice x6 -> x0, local copies, waits for them, and re-layouts: 9.26 us -> none  [the longest x2 4.03 us: shards(): far0, far1 = (along_x(left[:FAR], 1), along_x(right[FAR:], -1))]
    unnamed x30 -> x36, local copies, waits for them, and re-layouts: 12.1 us -> 6.74 us
    pallas_call x3 -> x6, Pallas kernels: 40.7 us -> 36.9 us  [call(): pl.pallas_call(kernel, out_shape=out_shape, in_specs=in_specs, out_specs=...]
    ppermute x1, starting transfers between devices: 3.95 us -> 1.92 us  [to_other_core(): return lax.ppermute(array, 'rep', [(r, r ^ 1) for r in range(16)])]
    ppermute x4, waiting for transfers between devices: 15.6 us -> 17.6 us  [across_z(): lax.ppermute(array, 'grp', [(g, (g + RING) % (2 * RING)) for g in range(2...]
    ppermute x4, starting transfers between devices: 3.46 us -> 5.16 us  [across_z(): lax.ppermute(array, 'grp', [(g, (g + RING) % (2 * RING)) for g in range(2...]
    ppermute x8 -> x9, starting transfers between devices: 12.1 us -> 12.7 us  [along_x(): return lax.ppermute(array, 'grp', pairs)]
  transfers between devices with their start and end apart: 20 -> 21, of which waited for: 8 -> 12; matrix products, arithmetic and copies ran while one was open for 7% -> 0% of each run, Pallas kernels for 13% -> 14%
where the time goes in v2:
time: 146 us
  waiting for transfers between devices  61.9 us (42%)
  Pallas kernels  36.9 us (25%)
  starting transfers between devices  36.5 us (25%)
  local copies, waits for them, and re-layouts  6.82 us (5%)
  other arithmetic  2.65 us (2%)
    pallas_call x6, Pallas kernels, call(): pl.pallas_call(kernel, out_shape=out_shape, in_specs=in_specs, out_specs=...  36.9 us
    ppermute x7, waiting for transfers between devices, to_chip(): return lax.ppermute(array, 'rep', pairs)  25 us
    ppermute x4, waiting for transfers between devices, across_z(): lax.ppermute(array, 'grp', [(g, (g + RING) % (2 * RING)) for g in range(2...  17.6 us
    ppermute x7, starting transfers between devices, to_chip(): return lax.ppermute(array, 'rep', pairs)  16.8 us
    ppermute x9, waiting for transfers between devices, along_x(): return lax.ppermute(array, 'grp', pairs)  14.8 us
    ppermute x9, starting transfers between devices, along_x(): return lax.ppermute(array, 'grp', pairs)  12.7 us
    unnamed x36, local copies, waits for them, and re-layouts  6.74 us
    ppermute x4, starting transfers between devices, across_z(): lax.ppermute(array, 'grp', [(g, (g + RING) % (2 * RING)) for g in range(2...  5.16 us
  transfers between devices with their start and end apart: 21, of which 12 were waited for; matrix products, arithmetic and copies ran while one was open for 0% of the time, Pallas kernels for 14%

profile of v2, /device:TPU:1, one launch (start us, length us, event | category | flops | bytes accessed | tf_op | source)
XLA Modules:
  0.0 145.6 jit_solution(13334480494081189944)
XLA Ops:
  0.7 3.4 %collective-permute-start.1 = (bf16[128,5120]{1,0:T(8,128)(2,1)}, bf16[128,5120]{1,0:T(8,128)(2,1)S(1)}, u32[]{:S(2)}, u32[]{:S(2)}) collective-permute-start(bf16[128,5120]{1,0:T(8,128)(2,1)} %refs_5_.1), channel_id=1, source_target_pairs={{0,3},{1,0},{2,1},{3,2},{4,7},{5,4},{6,5},{7,6},{8,11},{9,8},{10,9... | collective-permute-start | bytes 3932168 | tf_op jit(solution)/shard_map/ppermute | solution.py:26
  5.3 1.7 %collective-permute-start.2 = (bf16[80,5120]{1,0:T(8,128)(2,1)S(1)}, bf16[80,5120]{1,0:T(8,128)(2,1)}, u32[]{:S(2)}, u32[]{:S(2)}) collective-permute-start(bf16[80,5120]{1,0:T(8,128)(2,1)S(1)} %get-tuple-element.16), channel_id=1, source_target_pairs={{0,4},{1,5},{2,6},{3,7},{4,0},{5,1},{6,2},{7,3},{8,12},{9,13},{10,... | collective-permute-start | bytes 2457608 | tf_op jit(solution)/shard_map/ppermute | solution.py:30
  7.1 17.5 %collective-permute-done.2.refs_8_ = bf16[80,5120]{1,0:T(8,128)(2,1)} collective-permute-done((bf16[80,5120]{1,0:T(8,128)(2,1)S(1)}, bf16[80,5120]{1,0:T(8,128)(2,1)}, u32[]{:S(2)}, u32[]{:S(2)}) %collective-permute-start.2) | collective-permute-done | bytes 819232 | tf_op jit(solution)/shard_map/ppermute | solution.py:30
  24.7 2.4 %collective-permute-start.6 = (bf16[80,5120]{1,0:T(8,128)(2,1)}, bf16[80,5120]{1,0:T(8,128)(2,1)}, u32[]{:S(2)}, u32[]{:S(2)}) collective-permute-start(bf16[80,5120]{1,0:T(8,128)(2,1)} %collective-permute-done.2.refs_8_), channel_id=1, source_target_pairs={{0,3},{1,0},{2,1},{3,2},{4,7},{5,4},{6,5},{7,6},{8,11},{9,8},{10,9... | collective-permute-start | bytes 2457608 | tf_op jit(solution)/shard_map/ppermute | solution.py:26
  27.1 4.7 %collective-permute-done.1.refs_1_.refs_7_ = bf16[128,5120]{1,0:T(8,128)(2,1)S(1)} collective-permute-done((bf16[128,5120]{1,0:T(8,128)(2,1)}, bf16[128,5120]{1,0:T(8,128)(2,1)S(1)}, u32[]{:S(2)}, u32[]{:S(2)}) %collective-permute-start.1) | collective-permute-done | bytes 1310752 | tf_op jit(solution)/shard_map/ppermute | solution.py:26
  31.8 3.0 %collective-permute-done.refs_0_.refs_6_ = bf16[128,5120]{1,0:T(8,128)(2,1)S(1)} collective-permute-done((bf16[128,5120]{1,0:T(8,128)(2,1)}, bf16[128,5120]{1,0:T(8,128)(2,1)S(1)}, u32[]{:S(2)}, u32[]{:S(2)}) %collective-permute-start) | collective-permute-done | bytes 1310752 | tf_op jit(solution)/shard_map/ppermute | solution.py:26
  35.9 1.6 %shard_map.104 = (bf16[64,5120]{1,0:T(8,128)(2,1)S(1)}, bf16[16,5120]{1,0:T(8,128)(2,1)S(1)}, bf16[48,5120]{1,0:T(8,128)(2,1)S(1)}, bf16[96,5120]{1,0:T(8,128)(2,1)S(1)}) custom-call(bf16[128,5120]{1,0:T(8,128)(2,1)} %copy-done.5, bf16[128,5120]{1,0:T(8,128)(2,1)} %copy-done.4), custom_call_target="tpu_custom_call" | custom-call | bytes 4587520 | tf_op jit(solution)/shard_map/pallas_call | solution.py:293
  37.5 1.7 %collective-permute-start.9 = (bf16[96,5120]{1,0:T(8,128)(2,1)S(1)}, bf16[96,5120]{1,0:T(8,128)(2,1)}, u32[]{:S(2)}, u32[]{:S(2)}) collective-permute-start(bf16[96,5120]{1,0:T(8,128)(2,1)S(1)} %get-tuple-element.24), channel_id=1, source_target_pairs={{0,4},{1,5},{2,6},{3,7},{4,0},{5,1},{6,2},{7,3},{8,12},{9,13},{10,... | collective-permute-start | bytes 2949128 | tf_op jit(solution)/shard_map/ppermute | solution.py:30
  39.3 1.4 collective-permute-start.8
  41.5 2.5 %copy-done = bf16[1,4,128,5120]{3,2,1,0:T(8,128)(2,1)S(1)} copy-done((bf16[1,4,128,5120]{3,2,1,0:T(8,128)(2,1)S(1)}, bf16[1,4,128,5120]{3,2,1,0:T(8,128)(2,1)}, u32[]{:S(2)}) %copy-start) | copy-done | bytes 5242904
  44.0 10.0 %shard_map.105 = (f32[512,5120]{1,0:T(8,128)S(1)}, bf16[16,5120]{1,0:T(8,128)(2,1)S(1)}) custom-call(s32[11]{0:T(128)S(1)} %stack.47.refs_0_, f32[1,128]{1,0:T(1,128)S(1)} %bitcast.44, s32[8,128]{1,0:T(8,128)S(1)} %bitcast.41, bf16[1024,512]{1,0:T(8,128)(2,1)} %refs_3_.5, bf16[512,5120]{1,0:T(8,128)(2,1)S(1)} %bitcast.36, ...), custom_call_target="tpu_custom_call", output_to_operand_aliasing={{1}: (10, {})} | custom-call | flops 5368709120 | bytes 20971520 | tf_op jit(solution)/shard_map/pallas_call | solution.py:293
  55.9 2.0 %collective-permute-start.7 = (bf16[16,5120]{1,0:T(8,128)(2,1)S(1)}, bf16[16,5120]{1,0:T(8,128)(2,1)S(1)}, u32[]{:S(2)}, u32[]{:S(2)}) collective-permute-start(bf16[16,5120]{1,0:T(8,128)(2,1)S(1)} %get-tuple-element.22), channel_id=1, source_target_pairs={{0,3},{1,0},{2,1},{3,2},{4,7},{5,4},{6,5},{7,6},{8,11},{9,8},{10,9... | collective-permute-start | bytes 491528 | tf_op jit(solution)/shard_map/ppermute | solution.py:26
  57.9 1.9 %collective-permute-done.8.refs_7_.refs_9_ = bf16[48,5120]{1,0:T(8,128)(2,1)S(1)} collective-permute-done((bf16[48,5120]{1,0:T(8,128)(2,1)S(1)}, bf16[48,5120]{1,0:T(8,128)(2,1)S(1)}, u32[]{:S(2)}, u32[]{:S(2)}) %collective-permute-start.8) | collective-permute-done | bytes 491552 | tf_op jit(solution)/shard_map/ppermute | solution.py:26
  59.8 1.6 %collective-permute-start.12 = (bf16[48,5120]{1,0:T(8,128)(2,1)S(1)}, bf16[48,5120]{1,0:T(8,128)(2,1)S(1)}, u32[]{:S(2)}, u32[]{:S(2)}) collective-permute-start(bf16[48,5120]{1,0:T(8,128)(2,1)S(1)} %collective-permute-done.8.refs_7_.refs_9_), channel_id=1, source_target_pairs={{0,4},{1,5},{2,6},{3,7},{4,0},{5,1},{6,2},{7,3},{8,12},{9,13},{10,... | collective-permute-start | bytes 1474568 | tf_op jit(solution)/shard_map/ppermute | solution.py:30
  61.4 1.5 %collective-permute-done.7.refs_6_.refs_8_ = bf16[16,5120]{1,0:T(8,128)(2,1)S(1)} collective-permute-done((bf16[16,5120]{1,0:T(8,128)(2,1)S(1)}, bf16[16,5120]{1,0:T(8,128)(2,1)S(1)}, u32[]{:S(2)}, u32[]{:S(2)}) %collective-permute-start.7) | collective-permute-done | bytes 163872 | tf_op jit(solution)/shard_map/ppermute | solution.py:26
  62.9 3.4 %collective-permute-start.11 = (bf16[32,5120]{1,0:T(8,128)(2,1)S(1)}, bf16[32,5120]{1,0:T(8,128)(2,1)S(1)}, u32[]{:S(2)}, u32[]{:S(2)}) collective-permute-start(bf16[32,5120]{1,0:T(8,128)(2,1)S(1)} %get-tuple-element.26), channel_id=1, source_target_pairs={{0,3},{1,0},{2,1},{3,2},{4,7},{5,4},{6,5},{7,6},{8,11},{9,8},{10,9... | collective-permute-start | bytes 983048 | tf_op jit(solution)/shard_map/ppermute | solution.py:26
  67.2 6.0 %shard_map.107.refs_6_ = bf16[512,384]{1,0:T(8,128)(2,1)S(1)} custom-call(s32[11]{0:T(128)S(1)} %stack.47.refs_0_, f32[1,128]{1,0:T(1,128)S(1)} %bitcast.45, s32[8,128]{1,0:T(8,128)S(1)} %bitcast.42, bf16[1024,512]{1,0:T(8,128)(2,1)} %refs_3_.5, bf16[512,5120]{1,0:T(8,128)(2,1)S(1)} %bitcast.37, bf16[64,5120]{1,0:T(8,128)(2,1)} %copy-done.6, ...), custom_call_target="tpu_custom_call" | custom-call | flops 2013265920 | bytes 9175040 | tf_op jit(solution)/shard_map/pallas_call | solution.py:293
  73.2 3.7 %collective-permute-done.10.refs_14_ = bf16[48,5120]{1,0:T(8,128)(2,1)S(1)} collective-permute-done((bf16[48,5120]{1,0:T(8,128)(2,1)S(1)}, bf16[48,5120]{1,0:T(8,128)(2,1)S(1)}, u32[]{:S(2)}, u32[]{:S(2)}) %collective-permute-start.10) | collective-permute-done | bytes 491552 | tf_op jit(solution)/shard_map/ppermute | solution.py:26
  77.9 16.8 %shard_map.108 = (bf16[8,32,5120]{2,1,0:T(8,128)(2,1)S(1)}, bf16[8,32,5120]{2,1,0:T(8,128)(2,1)S(1)}) custom-call(s32[11]{0:T(128)S(1)} %stack.47.refs_0_, f32[1,128]{1,0:T(1,128)S(1)} %bitcast.46, s32[8,128]{1,0:T(8,128)S(1)} %bitcast.43, bf16[1024,512]{1,0:T(8,128)(2,1)} %refs_3_.5, bf16[512,5120]{1,0:T(8,128)(2,1)S(1)} %bitcast.40, ...), custom_call_target="tpu_custom_call" | custom-call | flops 6710886400 | bytes 20971520 | tf_op jit(solution)/shard_map/pallas_call | solution.py:293
  94.7 1.9 %collective-permute-start.13 = (bf16[8,32,5120]{2,1,0:T(8,128)(2,1)S(1)}, bf16[8,32,5120]{2,1,0:T(8,128)(2,1)S(1)}, u32[]{:S(2)}, u32[]{:S(2)}) collective-permute-start(bf16[8,32,5120]{2,1,0:T(8,128)(2,1)S(1)} %get-tuple-element.28), channel_id=1, source_target_pairs={{0,8},{8,0},{16,24},{24,16},{32,40},{40,32},{48,56},{56,48},{64,72... | collective-permute-start | bytes 7864328 | tf_op jit(solution)/shard_map/ppermute | solution.py:34
  96.6 4.5 %collective-permute-done.13 = bf16[8,32,5120]{2,1,0:T(8,128)(2,1)S(1)} collective-permute-done((bf16[8,32,5120]{2,1,0:T(8,128)(2,1)S(1)}, bf16[8,32,5120]{2,1,0:T(8,128)(2,1)S(1)}, u32[]{:S(2)}, u32[]{:S(2)}) %collective-permute-start.13) | collective-permute-done | bytes 2621472 | tf_op jit(solution)/shard_map/ppermute | solution.py:34
  102.0 3.7 %collective-permute-start.14 = (bf16[32,5120]{1,0:T(8,128)(2,1)S(1)}, bf16[32,5120]{1,0:T(8,128)(2,1)S(1)}, u32[]{:S(2)}, u32[]{:S(2)}) collective-permute-start(bf16[32,5120]{1,0:T(8,128)(2,1)S(1)} %get-tuple-element.32), channel_id=1, source_target_pairs={{0,16},{8,24},{16,0},{24,8},{32,48},{40,56},{48,32},{56,40},{64,80... | collective-permute-start | bytes 983048 | tf_op jit(solution)/shard_map/ppermute | solution.py:45
  105.7 1.3 collective-permute-start.20
  107.0 1.5 %collective-permute-start.19 = (bf16[32,5120]{1,0:T(8,128)(2,1)S(1)}, bf16[32,5120]{1,0:T(8,128)(2,1)S(1)}, u32[]{:S(2)}, u32[]{:S(2)}) collective-permute-start(bf16[32,5120]{1,0:T(8,128)(2,1)S(1)} %get-tuple-element.34), channel_id=1, source_target_pairs={{0,96},{8,104},{16,112},{24,120},{32,0},{40,8},{48,16},{56,24},{64... | collective-permute-start | bytes 983048 | tf_op jit(solution)/shard_map/ppermute | solution.py:45
  108.4 5.1 %collective-permute-start.17 = (bf16[32,5120]{1,0:T(8,128)(2,1)S(1)}, bf16[32,5120]{1,0:T(8,128)(2,1)S(1)}, u32[]{:S(2)}, u32[]{:S(2)}) collective-permute-start(bf16[32,5120]{1,0:T(8,128)(2,1)S(1)} %get-tuple-element.36), channel_id=1, source_target_pairs={{0,112},{8,120},{16,96},{24,104},{32,16},{40,24},{48,0},{56,8},{64... | collective-permute-start | bytes 983048 | tf_op jit(solution)/shard_map/ppermute | solution.py:45
  113.5 2.9 %collective-permute-start.16 = (bf16[32,5120]{1,0:T(8,128)(2,1)S(1)}, bf16[32,5120]{1,0:T(8,128)(2,1)S(1)}, u32[]{:S(2)}, u32[]{:S(2)}) collective-permute-start(bf16[32,5120]{1,0:T(8,128)(2,1)S(1)} %get-tuple-element.37), channel_id=1, source_target_pairs={{0,64},{8,72},{16,80},{24,88},{32,96},{40,104},{48,112},{56,120},{... | collective-permute-start | bytes 983048 | tf_op jit(solution)/shard_map/ppermute | solution.py:45
  116.4 2.4 %collective-permute-start.15 = (bf16[32,5120]{1,0:T(8,128)(2,1)S(1)}, bf16[32,5120]{1,0:T(8,128)(2,1)S(1)}, u32[]{:S(2)}, u32[]{:S(2)}) collective-permute-start(bf16[32,5120]{1,0:T(8,128)(2,1)S(1)} %get-tuple-element.38), channel_id=1, source_target_pairs={{0,80},{8,88},{16,64},{24,72},{32,112},{40,120},{48,96},{56,104},{... | collective-permute-start | bytes 983048 | tf_op jit(solution)/shard_map/ppermute | solution.py:45
  118.8 7.5 %collective-permute-done.18 = bf16[32,5120]{1,0:T(8,128)(2,1)S(1)} collective-permute-done((bf16[32,5120]{1,0:T(8,128)(2,1)S(1)}, bf16[32,5120]{1,0:T(8,128)(2,1)S(1)}, u32[]{:S(2)}, u32[]{:S(2)}) %collective-permute-start.18) | collective-permute-done | bytes 327712 | tf_op jit(solution)/shard_map/ppermute | solution.py:45
  126.3 1.9 %collective-permute-done.17 = bf16[32,5120]{1,0:T(8,128)(2,1)S(1)} collective-permute-done((bf16[32,5120]{1,0:T(8,128)(2,1)S(1)}, bf16[32,5120]{1,0:T(8,128)(2,1)S(1)}, u32[]{:S(2)}, u32[]{:S(2)}) %collective-permute-start.17) | collective-permute-done | bytes 327712 | tf_op jit(solution)/shard_map/ppermute | solution.py:45
  128.2 7.6 %collective-permute-done.16 = bf16[32,5120]{1,0:T(8,128)(2,1)S(1)} collective-permute-done((bf16[32,5120]{1,0:T(8,128)(2,1)S(1)}, bf16[32,5120]{1,0:T(8,128)(2,1)S(1)}, u32[]{:S(2)}, u32[]{:S(2)}) %collective-permute-start.16) | collective-permute-done | bytes 327712 | tf_op jit(solution)/shard_map/ppermute | solution.py:45
  135.8 8.0 %collective-permute-done.15 = bf16[32,5120]{1,0:T(8,128)(2,1)S(1)} collective-permute-done((bf16[32,5120]{1,0:T(8,128)(2,1)S(1)}, bf16[32,5120]{1,0:T(8,128)(2,1)S(1)}, u32[]{:S(2)}, u32[]{:S(2)}) %collective-permute-start.15) | collective-permute-done | bytes 327712 | tf_op jit(solution)/shard_map/ppermute | solution.py:45
  143.8 1.8 %multiply_add_fusion = (f32[4,8,5120]{2,1,0:T(8,128)}, f32[4,8,5120]{2,1,0:T(8,128)}, f32[4,8,5120]{2,1,0:T(8,128)}) fusion(f32[4,8,5120]{2,1,0:T(8,128)S(1)} %copy-done.7, f32[4,8,5120]{2,1,0:T(8,128)S(1)} %copy-done.8, f32[4,8,5120]{2,1,0:T(8,128)S(1)} %copy-done.9, bf16[8,32,5120]{2,1,0:T(8,128)(2,1)S(1)} %collective-permute-done.13, ...), kind=kLoop, calls=%fused_computation.3 | loop fusion | flops 4587520 | bytes 6881280 | tf_op jit(solution)/shard_map/add | solution.py:507
  (56 shorter events, 7.9 us)
Async XLA Ops:
  0.6 40.9 %copy-start.3 = (f32[128]{0:T(128)S(1)}, f32[128]{0:T(128)}, u32[]{:S(2)}) copy-start(f32[128]{0:T(128)} %param.12) | copy-start | bytes 1540
  0.6 40.9 %copy-start.2 = (s32[1024]{0:T(1024)S(1)}, s32[1024]{0:T(1024)}, u32[]{:S(2)}) copy-start(s32[1024]{0:T(1024)} %param.9) | copy-start | bytes 12292
  0.7 31.1 %collective-permute-start.1 = (bf16[128,5120]{1,0:T(8,128)(2,1)}, bf16[128,5120]{1,0:T(8,128)(2,1)S(1)}, u32[]{:S(2)}, u32[]{:S(2)}) collective-permute-start(bf16[128,5120]{1,0:T(8,128)(2,1)} %refs_5_.1), channel_id=1, source_target_pairs={{0,3},{1,0},{2,1},{3,2},{4,7},{5,4},{6,5},{7,6},{8,11},{9,8},{10,9... | collective-permute-start | bytes 3932168 | tf_op jit(solution)/shard_map/ppermute | solution.py:26
  4.0 30.7 %collective-permute-start = (bf16[128,5120]{1,0:T(8,128)(2,1)}, bf16[128,5120]{1,0:T(8,128)(2,1)S(1)}, u32[]{:S(2)}, u32[]{:S(2)}) collective-permute-start(bf16[128,5120]{1,0:T(8,128)(2,1)} %refs_5_.1), channel_id=1, source_target_pairs={{0,1},{1,2},{2,3},{3,0},{4,5},{5,6},{6,7},{7,4},{8,9},{9,10},{10,1... | collective-permute-start | bytes 3932168 | tf_op jit(solution)/shard_map/ppermute | solution.py:26
  5.3 19.4 %collective-permute-start.2 = (bf16[80,5120]{1,0:T(8,128)(2,1)S(1)}, bf16[80,5120]{1,0:T(8,128)(2,1)}, u32[]{:S(2)}, u32[]{:S(2)}) collective-permute-start(bf16[80,5120]{1,0:T(8,128)(2,1)S(1)} %get-tuple-element.16), channel_id=1, source_target_pairs={{0,4},{1,5},{2,6},{3,7},{4,0},{5,1},{6,2},{7,3},{8,12},{9,13},{10,... | collective-permute-start | bytes 2457608 | tf_op jit(solution)/shard_map/ppermute | solution.py:30
  7.0 33.7 %collective-permute-start.3 = (bf16[48,5120]{1,0:T(8,128)(2,1)S(1)}, bf16[48,5120]{1,0:T(8,128)(2,1)S(1)}, u32[]{:S(2)}, u32[]{:S(2)}) collective-permute-start(bf16[48,5120]{1,0:T(8,128)(2,1)S(1)} %get-tuple-element.17), channel_id=1, source_target_pairs={{0,4},{1,5},{2,6},{3,7},{4,0},{5,1},{6,2},{7,3},{8,12},{9,13},{10,... | collective-permute-start | bytes 1474568 | tf_op jit(solution)/shard_map/ppermute | solution.py:30
  24.7 30.0 %collective-permute-start.6 = (bf16[80,5120]{1,0:T(8,128)(2,1)}, bf16[80,5120]{1,0:T(8,128)(2,1)}, u32[]{:S(2)}, u32[]{:S(2)}) collective-permute-start(bf16[80,5120]{1,0:T(8,128)(2,1)} %collective-permute-done.2.refs_8_), channel_id=1, source_target_pairs={{0,3},{1,0},{2,1},{3,2},{4,7},{5,4},{6,5},{7,6},{8,11},{9,8},{10,9... | collective-permute-start | bytes 2457608 | tf_op jit(solution)/shard_map/ppermute | solution.py:26
  27.0 27.7 %collective-permute-start.5 = (bf16[80,5120]{1,0:T(8,128)(2,1)}, bf16[80,5120]{1,0:T(8,128)(2,1)}, u32[]{:S(2)}, u32[]{:S(2)}) collective-permute-start(bf16[80,5120]{1,0:T(8,128)(2,1)} %collective-permute-done.2.refs_8_), channel_id=1, source_target_pairs={{0,1},{1,2},{2,3},{3,0},{4,5},{5,6},{6,7},{7,4},{8,9},{9,10},{10,1... | collective-permute-start | bytes 2457608 | tf_op jit(solution)/shard_map/ppermute | solution.py:26
  31.8 3.0 %copy-start.4 = (bf16[128,5120]{1,0:T(8,128)(2,1)}, bf16[128,5120]{1,0:T(8,128)(2,1)S(1)}, u32[]{:S(2)}) copy-start(bf16[128,5120]{1,0:T(8,128)(2,1)S(1)} %collective-permute-done.1.refs_1_.refs_7_) | copy-start | bytes 3932164
  37.5 28.9 %collective-permute-start.9 = (bf16[96,5120]{1,0:T(8,128)(2,1)S(1)}, bf16[96,5120]{1,0:T(8,128)(2,1)}, u32[]{:S(2)}, u32[]{:S(2)}) collective-permute-start(bf16[96,5120]{1,0:T(8,128)(2,1)S(1)} %get-tuple-element.24), channel_id=1, source_target_pairs={{0,4},{1,5},{2,6},{3,7},{4,0},{5,1},{6,2},{7,3},{8,12},{9,13},{10,... | collective-permute-start | bytes 2949128 | tf_op jit(solution)/shard_map/ppermute | solution.py:30
  39.3 20.4 %collective-permute-start.8 = (bf16[48,5120]{1,0:T(8,128)(2,1)S(1)}, bf16[48,5120]{1,0:T(8,128)(2,1)S(1)}, u32[]{:S(2)}, u32[]{:S(2)}) collective-permute-start(bf16[48,5120]{1,0:T(8,128)(2,1)S(1)} %get-tuple-element.23), channel_id=1, source_target_pairs={{0,3},{1,0},{2,1},{3,2},{4,7},{5,4},{6,5},{7,6},{8,11},{9,8},{10,9... | collective-permute-start | bytes 1474568 | tf_op jit(solution)/shard_map/ppermute | solution.py:26
  40.7 25.6 %collective-permute-start.4 = (bf16[64,5120]{1,0:T(8,128)(2,1)S(1)}, bf16[64,5120]{1,0:T(8,128)(2,1)S(1)}, u32[]{:S(2)}, u32[]{:S(2)}) collective-permute-start(bf16[64,5120]{1,0:T(8,128)(2,1)S(1)} %get-tuple-element.20), channel_id=1, source_target_pairs={{0,1},{1,2},{2,3},{3,0},{4,5},{5,6},{6,7},{7,4},{8,9},{9,10},{10,1... | collective-permute-start | bytes 1966088 | tf_op jit(solution)/shard_map/ppermute | solution.py:26
  55.9 7.0 %collective-permute-start.7 = (bf16[16,5120]{1,0:T(8,128)(2,1)S(1)}, bf16[16,5120]{1,0:T(8,128)(2,1)S(1)}, u32[]{:S(2)}, u32[]{:S(2)}) collective-permute-start(bf16[16,5120]{1,0:T(8,128)(2,1)S(1)} %get-tuple-element.22), channel_id=1, source_target_pairs={{0,3},{1,0},{2,1},{3,2},{4,7},{5,4},{6,5},{7,6},{8,11},{9,8},{10,9... | collective-permute-start | bytes 491528 | tf_op jit(solution)/shard_map/ppermute | solution.py:26
  57.9 19.0 %collective-permute-start.10 = (bf16[48,5120]{1,0:T(8,128)(2,1)S(1)}, bf16[48,5120]{1,0:T(8,128)(2,1)S(1)}, u32[]{:S(2)}, u32[]{:S(2)}) collective-permute-start(bf16[48,5120]{1,0:T(8,128)(2,1)S(1)} %get-tuple-element.25), channel_id=1, source_target_pairs={{0,1},{1,2},{2,3},{3,0},{4,5},{5,6},{6,7},{7,4},{8,9},{9,10},{10,1... | collective-permute-start | bytes 1474568 | tf_op jit(solution)/shard_map/ppermute | solution.py:26
  59.8 6.6 %copy-start.10 = (bf16[48,5120]{1,0:T(8,128)(2,1)}, bf16[48,5120]{1,0:T(8,128)(2,1)S(1)}, u32[]{:S(2)}) copy-start(bf16[48,5120]{1,0:T(8,128)(2,1)S(1)} %collective-permute-done.8.refs_7_.refs_9_) | copy-start | bytes 1474564
  59.8 17.1 %collective-permute-start.12 = (bf16[48,5120]{1,0:T(8,128)(2,1)S(1)}, bf16[48,5120]{1,0:T(8,128)(2,1)S(1)}, u32[]{:S(2)}, u32[]{:S(2)}) collective-permute-start(bf16[48,5120]{1,0:T(8,128)(2,1)S(1)} %collective-permute-done.8.refs_7_.refs_9_), channel_id=1, source_target_pairs={{0,4},{1,5},{2,6},{3,7},{4,0},{5,1},{6,2},{7,3},{8,12},{9,13},{10,... | collective-permute-start | bytes 1474568 | tf_op jit(solution)/shard_map/ppermute | solution.py:30
  62.9 3.5 %copy-start.11 = (bf16[16,5120]{1,0:T(8,128)(2,1)}, bf16[16,5120]{1,0:T(8,128)(2,1)S(1)}, u32[]{:S(2)}) copy-start(bf16[16,5120]{1,0:T(8,128)(2,1)S(1)} %collective-permute-done.7.refs_6_.refs_8_) | copy-start | bytes 491524
  62.9 15.0 %slice-start = ((s8[5242880]{0:T(1024)(128)(4,1)}), s8[4194304]{0:T(1024)(128)(4,1)S(1)}, s32[]{:S(2)}) async-start(s8[5242880]{0:T(1024)(128)(4,1)} %bitcast.38), calls=%async_computation | async-start | bytes 8388608
  62.9 15.0 %slice-start.1 = ((s8[5242880]{0:T(1024)(128)(4,1)}), s8[1048576]{0:T(1024)(128)(4,1)S(1)}, s32[]{:S(2)}) async-start(s8[5242880]{0:T(1024)(128)(4,1)} %bitcast.38), calls=%async_computation.1 | async-start | bytes 2097152
  62.9 10.3 %collective-permute-start.11 = (bf16[32,5120]{1,0:T(8,128)(2,1)S(1)}, bf16[32,5120]{1,0:T(8,128)(2,1)S(1)}, u32[]{:S(2)}, u32[]{:S(2)}) collective-permute-start(bf16[32,5120]{1,0:T(8,128)(2,1)S(1)} %get-tuple-element.26), channel_id=1, source_target_pairs={{0,3},{1,0},{2,1},{3,2},{4,7},{5,4},{6,5},{7,6},{8,11},{9,8},{10,9... | collective-permute-start | bytes 983048 | tf_op jit(solution)/shard_map/ppermute | solution.py:26
  73.2 3.7 %copy-start.15 = (bf16[32,5120]{1,0:T(8,128)(2,1)}, bf16[32,5120]{1,0:T(8,128)(2,1)S(1)}, u32[]{:S(2)}) copy-start(bf16[32,5120]{1,0:T(8,128)(2,1)S(1)} %collective-permute-done.11.refs_15_) | copy-start | bytes 983044
  94.7 6.5 %collective-permute-start.13 = (bf16[8,32,5120]{2,1,0:T(8,128)(2,1)S(1)}, bf16[8,32,5120]{2,1,0:T(8,128)(2,1)S(1)}, u32[]{:S(2)}, u32[]{:S(2)}) collective-permute-start(bf16[8,32,5120]{2,1,0:T(8,128)(2,1)S(1)} %get-tuple-element.28), channel_id=1, source_target_pairs={{0,8},{8,0},{16,24},{24,16},{32,40},{40,32},{48,56},{56,48},{64,72... | collective-permute-start | bytes 7864328 | tf_op jit(solution)/shard_map/ppermute | solution.py:34
  101.1 42.7 %copy-start.7 = (f32[4,8,5120]{2,1,0:T(8,128)S(1)}, f32[4,8,5120]{2,1,0:T(8,128)}, u32[]{:S(2)}) copy-start(f32[4,8,5120]{2,1,0:T(8,128)} %param.15) | copy-start | bytes 1966084
  101.1 42.7 %copy-start.8 = (f32[4,8,5120]{2,1,0:T(8,128)S(1)}, f32[4,8,5120]{2,1,0:T(8,128)}, u32[]{:S(2)}) copy-start(f32[4,8,5120]{2,1,0:T(8,128)} %param.13) | copy-start | bytes 1966084
  101.1 42.7 %copy-start.9 = (f32[4,8,5120]{2,1,0:T(8,128)S(1)}, f32[4,8,5120]{2,1,0:T(8,128)}, u32[]{:S(2)}) copy-start(f32[4,8,5120]{2,1,0:T(8,128)} %param.14) | copy-start | bytes 1966084
  102.0 11.5 %collective-permute-start.14 = (bf16[32,5120]{1,0:T(8,128)(2,1)S(1)}, bf16[32,5120]{1,0:T(8,128)(2,1)S(1)}, u32[]{:S(2)}, u32[]{:S(2)}) collective-permute-start(bf16[32,5120]{1,0:T(8,128)(2,1)S(1)} %get-tuple-element.32), channel_id=1, source_target_pairs={{0,16},{8,24},{16,0},{24,8},{32,48},{40,56},{48,32},{56,40},{64,80... | collective-permute-start | bytes 983048 | tf_op jit(solution)/shard_map/ppermute | solution.py:45
  105.7 10.7 %collective-permute-start.20 = (bf16[32,5120]{1,0:T(8,128)(2,1)S(1)}, bf16[32,5120]{1,0:T(8,128)(2,1)S(1)}, u32[]{:S(2)}, u32[]{:S(2)}) collective-permute-start(bf16[32,5120]{1,0:T(8,128)(2,1)S(1)} %get-tuple-element.33), channel_id=1, source_target_pairs={{0,32},{8,40},{16,48},{24,56},{32,64},{40,72},{48,80},{56,88},{64,... | collective-permute-start | bytes 983048 | tf_op jit(solution)/shard_map/ppermute | solution.py:45
  107.0 11.8 %collective-permute-start.19 = (bf16[32,5120]{1,0:T(8,128)(2,1)S(1)}, bf16[32,5120]{1,0:T(8,128)(2,1)S(1)}, u32[]{:S(2)}, u32[]{:S(2)}) collective-permute-start(bf16[32,5120]{1,0:T(8,128)(2,1)S(1)} %get-tuple-element.34), channel_id=1, source_target_pairs={{0,96},{8,104},{16,112},{24,120},{32,0},{40,8},{48,16},{56,24},{64... | collective-permute-start | bytes 983048 | tf_op jit(solution)/shard_map/ppermute | solution.py:45
  108.4 17.9 %collective-permute-start.18 = (bf16[32,5120]{1,0:T(8,128)(2,1)S(1)}, bf16[32,5120]{1,0:T(8,128)(2,1)S(1)}, u32[]{:S(2)}, u32[]{:S(2)}) collective-permute-start(bf16[32,5120]{1,0:T(8,128)(2,1)S(1)} %get-tuple-element.35), channel_id=1, source_target_pairs={{0,48},{8,56},{16,32},{24,40},{32,80},{40,88},{48,64},{56,72},{64,... | collective-permute-start | bytes 983048 | tf_op jit(solution)/shard_map/ppermute | solution.py:45
  108.4 19.8 %collective-permute-start.17 = (bf16[32,5120]{1,0:T(8,128)(2,1)S(1)}, bf16[32,5120]{1,0:T(8,128)(2,1)S(1)}, u32[]{:S(2)}, u32[]{:S(2)}) collective-permute-start(bf16[32,5120]{1,0:T(8,128)(2,1)S(1)} %get-tuple-element.36), channel_id=1, source_target_pairs={{0,112},{8,120},{16,96},{24,104},{32,16},{40,24},{48,0},{56,8},{64... | collective-permute-start | bytes 983048 | tf_op jit(solution)/shard_map/ppermute | solution.py:45
  113.5 22.3 %collective-permute-start.16 = (bf16[32,5120]{1,0:T(8,128)(2,1)S(1)}, bf16[32,5120]{1,0:T(8,128)(2,1)S(1)}, u32[]{:S(2)}, u32[]{:S(2)}) collective-permute-start(bf16[32,5120]{1,0:T(8,128)(2,1)S(1)} %get-tuple-element.37), channel_id=1, source_target_pairs={{0,64},{8,72},{16,80},{24,88},{32,96},{40,104},{48,112},{56,120},{... | collective-permute-start | bytes 983048 | tf_op jit(solution)/shard_map/ppermute | solution.py:45
  116.4 27.4 %collective-permute-start.15 = (bf16[32,5120]{1,0:T(8,128)(2,1)S(1)}, bf16[32,5120]{1,0:T(8,128)(2,1)S(1)}, u32[]{:S(2)}, u32[]{:S(2)}) collective-permute-start(bf16[32,5120]{1,0:T(8,128)(2,1)S(1)} %get-tuple-element.38), channel_id=1, source_target_pairs={{0,80},{8,88},{16,64},{24,72},{32,112},{40,120},{48,96},{56,104},{... | collective-permute-start | bytes 983048 | tf_op jit(solution)/shard_map/ppermute | solution.py:45
  (7 other events, 7.6 us)

commit v3 on v2

--- a/solution.py
+++ b/solution.py
@@ -17,7 +17,7 @@
 BLOCK = 128
 ROWS_A = 80
 FAR, FAR_A = 64, 48
-TILE = 1280
+TILE = 2560
 EARLY_VMEM, LATE_VMEM, RENEW_VMEM, PICK_VMEM = 18, 12, 26, 8
 
 
@@ -492,7 +492,7 @@
 
     theirs = to_other_core(theirs)
     summed = None
-    for step_y, step_z in ((0, 1), (2, 1), (2, 0), (3, 1), (1, 1), (3, 0), (1, 0), (0, 0)):
+    for step_y, step_z in ((2, 1), (3, 1), (1, 0), (3, 0), (0, 1), (1, 1), (2, 0), (0, 0)):
         index = step_y * 2 + step_z
         pair = mine[index].astype(jnp.float32) + theirs[index].astype(jnp.float32)
         if index:

time: 146 us -> 139 us (0.952)
  starting transfers between devices: 36.5 us -> 33.4 us
  waiting for transfers between devices: 61.9 us -> 59.2 us
    ppermute x7, starting transfers between devices: 16.8 us -> 13.7 us  [to_chip(): return lax.ppermute(array, 'rep', pairs)]
    ppermute x7, waiting for transfers between devices: 25 us -> 21.9 us  [to_chip(): return lax.ppermute(array, 'rep', pairs)]
  transfers between devices with their start and end apart: 21 -> 21, of which waited for: 12 -> 11; matrix products, arithmetic and copies ran while one was open for 0% -> 0% of each run, Pallas kernels for 14% -> 14%
where the time goes in v3:
time: 139 us
  waiting for transfers between devices  59.2 us (43%)
  Pallas kernels  35.9 us (26%)
  starting transfers between devices  33.4 us (24%)
  local copies, waits for them, and re-layouts  6.82 us (5%)
  other arithmetic  2.65 us (2%)
    pallas_call x6, Pallas kernels, call(): pl.pallas_call(kernel, out_shape=out_shape, in_specs=in_specs, out_specs=...  35.9 us
    ppermute x7, waiting for transfers between devices, to_chip(): return lax.ppermute(array, 'rep', pairs)  21.9 us
    ppermute x4, waiting for transfers between devices, across_z(): lax.ppermute(array, 'grp', [(g, (g + RING) % (2 * RING)) for g in range(2...  17.6 us
    ppermute x9, waiting for transfers between devices, along_x(): return lax.ppermute(array, 'grp', pairs)  15.2 us
    ppermute x7, starting transfers between devices, to_chip(): return lax.ppermute(array, 'rep', pairs)  13.7 us
    ppermute x9, starting transfers between devices, along_x(): return lax.ppermute(array, 'grp', pairs)  12.6 us
    unnamed x36, local copies, waits for them, and re-layouts  6.73 us
    ppermute x4, starting transfers between devices, across_z(): lax.ppermute(array, 'grp', [(g, (g + RING) % (2 * RING)) for g in range(2...  5.16 us
  transfers between devices with their start and end apart: 21, of which 11 were waited for; matrix products, arithmetic and copies ran while one was open for 0% of the time, Pallas kernels for 14%

profile of v3, /device:TPU:1, one launch (start us, length us, event | category | flops | bytes accessed | tf_op | source)
XLA Modules:
  0.0 138.9 jit_solution(5075794992144402762)
XLA Ops:
  0.7 3.4 %collective-permute-start.1 = (bf16[128,5120]{1,0:T(8,128)(2,1)}, bf16[128,5120]{1,0:T(8,128)(2,1)S(1)}, u32[]{:S(2)}, u32[]{:S(2)}) collective-permute-start(bf16[128,5120]{1,0:T(8,128)(2,1)} %refs_5_.1), channel_id=1, source_target_pairs={{0,3},{1,0},{2,1},{3,2},{4,7},{5,4},{6,5},{7,6},{8,11},{9,8},{10,9... | collective-permute-start | bytes 3932168 | tf_op jit(solution)/shard_map/ppermute | solution.py:26
  4.0 1.3 shard_map.103
  5.3 1.7 %collective-permute-start.2 = (bf16[80,5120]{1,0:T(8,128)(2,1)S(1)}, bf16[80,5120]{1,0:T(8,128)(2,1)}, u32[]{:S(2)}, u32[]{:S(2)}) collective-permute-start(bf16[80,5120]{1,0:T(8,128)(2,1)S(1)} %get-tuple-element.16), channel_id=1, source_target_pairs={{0,4},{1,5},{2,6},{3,7},{4,0},{5,1},{6,2},{7,3},{8,12},{9,13},{10,... | collective-permute-start | bytes 2457608 | tf_op jit(solution)/shard_map/ppermute | solution.py:30
  7.1 17.5 %collective-permute-done.2.refs_8_ = bf16[80,5120]{1,0:T(8,128)(2,1)} collective-permute-done((bf16[80,5120]{1,0:T(8,128)(2,1)S(1)}, bf16[80,5120]{1,0:T(8,128)(2,1)}, u32[]{:S(2)}, u32[]{:S(2)}) %collective-permute-start.2) | collective-permute-done | bytes 819232 | tf_op jit(solution)/shard_map/ppermute | solution.py:30
  24.7 2.4 %collective-permute-start.6 = (bf16[80,5120]{1,0:T(8,128)(2,1)}, bf16[80,5120]{1,0:T(8,128)(2,1)}, u32[]{:S(2)}, u32[]{:S(2)}) collective-permute-start(bf16[80,5120]{1,0:T(8,128)(2,1)} %collective-permute-done.2.refs_8_), channel_id=1, source_target_pairs={{0,3},{1,0},{2,1},{3,2},{4,7},{5,4},{6,5},{7,6},{8,11},{9,8},{10,9... | collective-permute-start | bytes 2457608 | tf_op jit(solution)/shard_map/ppermute | solution.py:26
  27.1 4.7 %collective-permute-done.1.refs_1_.refs_7_ = bf16[128,5120]{1,0:T(8,128)(2,1)S(1)} collective-permute-done((bf16[128,5120]{1,0:T(8,128)(2,1)}, bf16[128,5120]{1,0:T(8,128)(2,1)S(1)}, u32[]{:S(2)}, u32[]{:S(2)}) %collective-permute-start.1) | collective-permute-done | bytes 1310752 | tf_op jit(solution)/shard_map/ppermute | solution.py:26
  31.8 3.0 %collective-permute-done.refs_0_.refs_6_ = bf16[128,5120]{1,0:T(8,128)(2,1)S(1)} collective-permute-done((bf16[128,5120]{1,0:T(8,128)(2,1)}, bf16[128,5120]{1,0:T(8,128)(2,1)S(1)}, u32[]{:S(2)}, u32[]{:S(2)}) %collective-permute-start) | collective-permute-done | bytes 1310752 | tf_op jit(solution)/shard_map/ppermute | solution.py:26
  35.9 1.6 %shard_map.104 = (bf16[64,5120]{1,0:T(8,128)(2,1)S(1)}, bf16[16,5120]{1,0:T(8,128)(2,1)S(1)}, bf16[48,5120]{1,0:T(8,128)(2,1)S(1)}, bf16[96,5120]{1,0:T(8,128)(2,1)S(1)}) custom-call(bf16[128,5120]{1,0:T(8,128)(2,1)} %copy-done.5, bf16[128,5120]{1,0:T(8,128)(2,1)} %copy-done.4), custom_call_target="tpu_custom_call" | custom-call | bytes 4587520 | tf_op jit(solution)/shard_map/pallas_call | solution.py:293
  37.5 1.7 %collective-permute-start.9 = (bf16[96,5120]{1,0:T(8,128)(2,1)S(1)}, bf16[96,5120]{1,0:T(8,128)(2,1)}, u32[]{:S(2)}, u32[]{:S(2)}) collective-permute-start(bf16[96,5120]{1,0:T(8,128)(2,1)S(1)} %get-tuple-element.24), channel_id=1, source_target_pairs={{0,4},{1,5},{2,6},{3,7},{4,0},{5,1},{6,2},{7,3},{8,12},{9,13},{10,... | collective-permute-start | bytes 2949128 | tf_op jit(solution)/shard_map/ppermute | solution.py:30
  39.3 1.4 %collective-permute-start.8 = (bf16[48,5120]{1,0:T(8,128)(2,1)S(1)}, bf16[48,5120]{1,0:T(8,128)(2,1)S(1)}, u32[]{:S(2)}, u32[]{:S(2)}) collective-permute-start(bf16[48,5120]{1,0:T(8,128)(2,1)S(1)} %get-tuple-element.23), channel_id=1, source_target_pairs={{0,3},{1,0},{2,1},{3,2},{4,7},{5,4},{6,5},{7,6},{8,11},{9,8},{10,9... | collective-permute-start | bytes 1474568 | tf_op jit(solution)/shard_map/ppermute | solution.py:26
  41.5 2.5 %copy-done = bf16[1,4,128,5120]{3,2,1,0:T(8,128)(2,1)S(1)} copy-done((bf16[1,4,128,5120]{3,2,1,0:T(8,128)(2,1)S(1)}, bf16[1,4,128,5120]{3,2,1,0:T(8,128)(2,1)}, u32[]{:S(2)}) %copy-start) | copy-done | bytes 5242904
  44.0 9.6 %shard_map.105 = (f32[512,5120]{1,0:T(8,128)S(1)}, bf16[16,5120]{1,0:T(8,128)(2,1)S(1)}) custom-call(s32[11]{0:T(128)S(1)} %stack.47.refs_0_, f32[1,128]{1,0:T(1,128)S(1)} %bitcast.44, s32[8,128]{1,0:T(8,128)S(1)} %bitcast.41, bf16[1024,512]{1,0:T(8,128)(2,1)} %refs_3_.5, bf16[512,5120]{1,0:T(8,128)(2,1)S(1)} %bitcast.36, ...), custom_call_target="tpu_custom_call", output_to_operand_aliasing={{1}: (10, {})} | custom-call | flops 5368709120 | bytes 20971520 | tf_op jit(solution)/shard_map/pallas_call | solution.py:293
  54.3 1.2 shard_map.106
  55.5 2.0 %collective-permute-start.7 = (bf16[16,5120]{1,0:T(8,128)(2,1)S(1)}, bf16[16,5120]{1,0:T(8,128)(2,1)S(1)}, u32[]{:S(2)}, u32[]{:S(2)}) collective-permute-start(bf16[16,5120]{1,0:T(8,128)(2,1)S(1)} %get-tuple-element.22), channel_id=1, source_target_pairs={{0,3},{1,0},{2,1},{3,2},{4,7},{5,4},{6,5},{7,6},{8,11},{9,8},{10,9... | collective-permute-start | bytes 491528 | tf_op jit(solution)/shard_map/ppermute | solution.py:26
  57.5 2.3 %collective-permute-done.8.refs_7_.refs_9_ = bf16[48,5120]{1,0:T(8,128)(2,1)S(1)} collective-permute-done((bf16[48,5120]{1,0:T(8,128)(2,1)S(1)}, bf16[48,5120]{1,0:T(8,128)(2,1)S(1)}, u32[]{:S(2)}, u32[]{:S(2)}) %collective-permute-start.8) | collective-permute-done | bytes 491552 | tf_op jit(solution)/shard_map/ppermute | solution.py:26
  59.8 1.6 %collective-permute-start.12 = (bf16[48,5120]{1,0:T(8,128)(2,1)S(1)}, bf16[48,5120]{1,0:T(8,128)(2,1)S(1)}, u32[]{:S(2)}, u32[]{:S(2)}) collective-permute-start(bf16[48,5120]{1,0:T(8,128)(2,1)S(1)} %collective-permute-done.8.refs_7_.refs_9_), channel_id=1, source_target_pairs={{0,4},{1,5},{2,6},{3,7},{4,0},{5,1},{6,2},{7,3},{8,12},{9,13},{10,... | collective-permute-start | bytes 1474568 | tf_op jit(solution)/shard_map/ppermute | solution.py:30
  61.4 1.9 %collective-permute-done.7.refs_6_.refs_8_ = bf16[16,5120]{1,0:T(8,128)(2,1)S(1)} collective-permute-done((bf16[16,5120]{1,0:T(8,128)(2,1)S(1)}, bf16[16,5120]{1,0:T(8,128)(2,1)S(1)}, u32[]{:S(2)}, u32[]{:S(2)}) %collective-permute-start.7) | collective-permute-done | bytes 163872 | tf_op jit(solution)/shard_map/ppermute | solution.py:26
  63.3 3.4 %collective-permute-start.11 = (bf16[32,5120]{1,0:T(8,128)(2,1)S(1)}, bf16[32,5120]{1,0:T(8,128)(2,1)S(1)}, u32[]{:S(2)}, u32[]{:S(2)}) collective-permute-start(bf16[32,5120]{1,0:T(8,128)(2,1)S(1)} %get-tuple-element.26), channel_id=1, source_target_pairs={{0,3},{1,0},{2,1},{3,2},{4,7},{5,4},{6,5},{7,6},{8,11},{9,8},{10,9... | collective-permute-start | bytes 983048 | tf_op jit(solution)/shard_map/ppermute | solution.py:26
  67.5 6.0 %shard_map.107.refs_6_ = bf16[512,384]{1,0:T(8,128)(2,1)S(1)} custom-call(s32[11]{0:T(128)S(1)} %stack.47.refs_0_, f32[1,128]{1,0:T(1,128)S(1)} %bitcast.45, s32[8,128]{1,0:T(8,128)S(1)} %bitcast.42, bf16[1024,512]{1,0:T(8,128)(2,1)} %refs_3_.5, bf16[512,5120]{1,0:T(8,128)(2,1)S(1)} %bitcast.37, bf16[64,5120]{1,0:T(8,128)(2,1)} %copy-done.6, ...), custom_call_target="tpu_custom_call" | custom-call | flops 2013265920 | bytes 9175040 | tf_op jit(solution)/shard_map/pallas_call | solution.py:293
  73.5 3.4 %collective-permute-done.10.refs_14_ = bf16[48,5120]{1,0:T(8,128)(2,1)S(1)} collective-permute-done((bf16[48,5120]{1,0:T(8,128)(2,1)S(1)}, bf16[48,5120]{1,0:T(8,128)(2,1)S(1)}, u32[]{:S(2)}, u32[]{:S(2)}) %collective-permute-start.10) | collective-permute-done | bytes 491552 | tf_op jit(solution)/shard_map/ppermute | solution.py:26
  77.9 16.2 %shard_map.108 = (bf16[8,32,5120]{2,1,0:T(8,128)(2,1)S(1)}, bf16[8,32,5120]{2,1,0:T(8,128)(2,1)S(1)}) custom-call(s32[11]{0:T(128)S(1)} %stack.47.refs_0_, f32[1,128]{1,0:T(1,128)S(1)} %bitcast.46, s32[8,128]{1,0:T(8,128)S(1)} %bitcast.43, bf16[1024,512]{1,0:T(8,128)(2,1)} %refs_3_.5, bf16[512,5120]{1,0:T(8,128)(2,1)S(1)} %bitcast.40, ...), custom_call_target="tpu_custom_call" | custom-call | flops 6710886400 | bytes 20971520 | tf_op jit(solution)/shard_map/pallas_call | solution.py:293
  94.1 1.9 %collective-permute-start.13 = (bf16[8,32,5120]{2,1,0:T(8,128)(2,1)S(1)}, bf16[8,32,5120]{2,1,0:T(8,128)(2,1)S(1)}, u32[]{:S(2)}, u32[]{:S(2)}) collective-permute-start(bf16[8,32,5120]{2,1,0:T(8,128)(2,1)S(1)} %get-tuple-element.28), channel_id=1, source_target_pairs={{0,8},{8,0},{16,24},{24,16},{32,40},{40,32},{48,56},{56,48},{64,72... | collective-permute-start | bytes 7864328 | tf_op jit(solution)/shard_map/ppermute | solution.py:34
  96.0 4.5 %collective-permute-done.13 = bf16[8,32,5120]{2,1,0:T(8,128)(2,1)S(1)} collective-permute-done((bf16[8,32,5120]{2,1,0:T(8,128)(2,1)S(1)}, bf16[8,32,5120]{2,1,0:T(8,128)(2,1)S(1)}, u32[]{:S(2)}, u32[]{:S(2)}) %collective-permute-start.13) | collective-permute-done | bytes 2621472 | tf_op jit(solution)/shard_map/ppermute | solution.py:34
  101.4 6.3 %collective-permute-start.14 = (bf16[32,5120]{1,0:T(8,128)(2,1)S(1)}, bf16[32,5120]{1,0:T(8,128)(2,1)S(1)}, u32[]{:S(2)}, u32[]{:S(2)}) collective-permute-start(bf16[32,5120]{1,0:T(8,128)(2,1)S(1)} %get-tuple-element.32), channel_id=1, source_target_pairs={{0,80},{8,88},{16,64},{24,72},{32,112},{40,120},{48,96},{56,104},{... | collective-permute-start | bytes 983048 | tf_op jit(solution)/shard_map/ppermute | solution.py:45
  108.4 3.3 %collective-permute-start.18 = (bf16[32,5120]{1,0:T(8,128)(2,1)S(1)}, bf16[32,5120]{1,0:T(8,128)(2,1)S(1)}, u32[]{:S(2)}, u32[]{:S(2)}) collective-permute-start(bf16[32,5120]{1,0:T(8,128)(2,1)S(1)} %get-tuple-element.35), channel_id=1, source_target_pairs={{0,16},{8,24},{16,0},{24,8},{32,48},{40,56},{48,32},{56,40},{64,80... | collective-permute-start | bytes 983048 | tf_op jit(solution)/shard_map/ppermute | solution.py:45
  111.8 1.4 collective-permute-start.17
  113.2 2.4 %collective-permute-done.14 = bf16[32,5120]{1,0:T(8,128)(2,1)S(1)} collective-permute-done((bf16[32,5120]{1,0:T(8,128)(2,1)S(1)}, bf16[32,5120]{1,0:T(8,128)(2,1)S(1)}, u32[]{:S(2)}, u32[]{:S(2)}) %collective-permute-start.14) | collective-permute-done | bytes 327712 | tf_op jit(solution)/shard_map/ppermute | solution.py:45
  115.6 6.7 %collective-permute-done.20 = bf16[32,5120]{1,0:T(8,128)(2,1)S(1)} collective-permute-done((bf16[32,5120]{1,0:T(8,128)(2,1)S(1)}, bf16[32,5120]{1,0:T(8,128)(2,1)S(1)}, u32[]{:S(2)}, u32[]{:S(2)}) %collective-permute-start.20) | collective-permute-done | bytes 327712 | tf_op jit(solution)/shard_map/ppermute | solution.py:45
  122.3 1.8 %collective-permute-start.15 = (bf16[32,5120]{1,0:T(8,128)(2,1)S(1)}, bf16[32,5120]{1,0:T(8,128)(2,1)S(1)}, u32[]{:S(2)}, u32[]{:S(2)}) collective-permute-start(bf16[32,5120]{1,0:T(8,128)(2,1)S(1)} %get-tuple-element.38), channel_id=1, source_target_pairs={{0,112},{8,120},{16,96},{24,104},{32,16},{40,24},{48,0},{56,8},{64... | collective-permute-start | bytes 983048 | tf_op jit(solution)/shard_map/ppermute | solution.py:45
  124.1 6.1 %collective-permute-done.19 = bf16[32,5120]{1,0:T(8,128)(2,1)S(1)} collective-permute-done((bf16[32,5120]{1,0:T(8,128)(2,1)S(1)}, bf16[32,5120]{1,0:T(8,128)(2,1)S(1)}, u32[]{:S(2)}, u32[]{:S(2)}) %collective-permute-start.19) | collective-permute-done | bytes 327712 | tf_op jit(solution)/shard_map/ppermute | solution.py:45
  130.3 6.8 %collective-permute-done.16 = bf16[32,5120]{1,0:T(8,128)(2,1)S(1)} collective-permute-done((bf16[32,5120]{1,0:T(8,128)(2,1)S(1)}, bf16[32,5120]{1,0:T(8,128)(2,1)S(1)}, u32[]{:S(2)}, u32[]{:S(2)}) %collective-permute-start.16) | collective-permute-done | bytes 327712 | tf_op jit(solution)/shard_map/ppermute | solution.py:45
  137.0 1.8 %multiply_add_fusion = (f32[4,8,5120]{2,1,0:T(8,128)}, f32[4,8,5120]{2,1,0:T(8,128)}, f32[4,8,5120]{2,1,0:T(8,128)}) fusion(f32[4,8,5120]{2,1,0:T(8,128)S(1)} %copy-done.7, f32[4,8,5120]{2,1,0:T(8,128)S(1)} %copy-done.8, f32[4,8,5120]{2,1,0:T(8,128)S(1)} %copy-done.9, bf16[8,32,5120]{2,1,0:T(8,128)(2,1)S(1)} %collective-permute-done.13, ...), kind=kLoop, calls=%fused_computation.3 | loop fusion | flops 4587520 | bytes 6881280 | tf_op jit(solution)/shard_map/add | solution.py:507
  (56 shorter events, 6.2 us)
Async XLA Ops:
  0.6 40.9 %copy-start.3 = (f32[128]{0:T(128)S(1)}, f32[128]{0:T(128)}, u32[]{:S(2)}) copy-start(f32[128]{0:T(128)} %param.12) | copy-start | bytes 1540
  0.6 40.9 %copy-start.2 = (s32[1024]{0:T(1024)S(1)}, s32[1024]{0:T(1024)}, u32[]{:S(2)}) copy-start(s32[1024]{0:T(1024)} %param.9) | copy-start | bytes 12292
  0.7 31.1 %collective-permute-start.1 = (bf16[128,5120]{1,0:T(8,128)(2,1)}, bf16[128,5120]{1,0:T(8,128)(2,1)S(1)}, u32[]{:S(2)}, u32[]{:S(2)}) collective-permute-start(bf16[128,5120]{1,0:T(8,128)(2,1)} %refs_5_.1), channel_id=1, source_target_pairs={{0,3},{1,0},{2,1},{3,2},{4,7},{5,4},{6,5},{7,6},{8,11},{9,8},{10,9... | collective-permute-start | bytes 3932168 | tf_op jit(solution)/shard_map/ppermute | solution.py:26
  4.0 30.7 %collective-permute-start = (bf16[128,5120]{1,0:T(8,128)(2,1)}, bf16[128,5120]{1,0:T(8,128)(2,1)S(1)}, u32[]{:S(2)}, u32[]{:S(2)}) collective-permute-start(bf16[128,5120]{1,0:T(8,128)(2,1)} %refs_5_.1), channel_id=1, source_target_pairs={{0,1},{1,2},{2,3},{3,0},{4,5},{5,6},{6,7},{7,4},{8,9},{9,10},{10,1... | collective-permute-start | bytes 3932168 | tf_op jit(solution)/shard_map/ppermute | solution.py:26
  5.3 19.4 %collective-permute-start.2 = (bf16[80,5120]{1,0:T(8,128)(2,1)S(1)}, bf16[80,5120]{1,0:T(8,128)(2,1)}, u32[]{:S(2)}, u32[]{:S(2)}) collective-permute-start(bf16[80,5120]{1,0:T(8,128)(2,1)S(1)} %get-tuple-element.16), channel_id=1, source_target_pairs={{0,4},{1,5},{2,6},{3,7},{4,0},{5,1},{6,2},{7,3},{8,12},{9,13},{10,... | collective-permute-start | bytes 2457608 | tf_op jit(solution)/shard_map/ppermute | solution.py:30
  7.0 33.7 %collective-permute-start.3 = (bf16[48,5120]{1,0:T(8,128)(2,1)S(1)}, bf16[48,5120]{1,0:T(8,128)(2,1)S(1)}, u32[]{:S(2)}, u32[]{:S(2)}) collective-permute-start(bf16[48,5120]{1,0:T(8,128)(2,1)S(1)} %get-tuple-element.17), channel_id=1, source_target_pairs={{0,4},{1,5},{2,6},{3,7},{4,0},{5,1},{6,2},{7,3},{8,12},{9,13},{10,... | collective-permute-start | bytes 1474568 | tf_op jit(solution)/shard_map/ppermute | solution.py:30
  24.7 29.6 %collective-permute-start.6 = (bf16[80,5120]{1,0:T(8,128)(2,1)}, bf16[80,5120]{1,0:T(8,128)(2,1)}, u32[]{:S(2)}, u32[]{:S(2)}) collective-permute-start(bf16[80,5120]{1,0:T(8,128)(2,1)} %collective-permute-done.2.refs_8_), channel_id=1, source_target_pairs={{0,3},{1,0},{2,1},{3,2},{4,7},{5,4},{6,5},{7,6},{8,11},{9,8},{10,9... | collective-permute-start | bytes 2457608 | tf_op jit(solution)/shard_map/ppermute | solution.py:26
  27.0 27.3 %collective-permute-start.5 = (bf16[80,5120]{1,0:T(8,128)(2,1)}, bf16[80,5120]{1,0:T(8,128)(2,1)}, u32[]{:S(2)}, u32[]{:S(2)}) collective-permute-start(bf16[80,5120]{1,0:T(8,128)(2,1)} %collective-permute-done.2.refs_8_), channel_id=1, source_target_pairs={{0,1},{1,2},{2,3},{3,0},{4,5},{5,6},{6,7},{7,4},{8,9},{9,10},{10,1... | collective-permute-start | bytes 2457608 | tf_op jit(solution)/shard_map/ppermute | solution.py:26
  31.8 3.0 %copy-start.4 = (bf16[128,5120]{1,0:T(8,128)(2,1)}, bf16[128,5120]{1,0:T(8,128)(2,1)S(1)}, u32[]{:S(2)}) copy-start(bf16[128,5120]{1,0:T(8,128)(2,1)S(1)} %collective-permute-done.1.refs_1_.refs_7_) | copy-start | bytes 3932164
  37.5 29.2 %collective-permute-start.9 = (bf16[96,5120]{1,0:T(8,128)(2,1)S(1)}, bf16[96,5120]{1,0:T(8,128)(2,1)}, u32[]{:S(2)}, u32[]{:S(2)}) collective-permute-start(bf16[96,5120]{1,0:T(8,128)(2,1)S(1)} %get-tuple-element.24), channel_id=1, source_target_pairs={{0,4},{1,5},{2,6},{3,7},{4,0},{5,1},{6,2},{7,3},{8,12},{9,13},{10,... | collective-permute-start | bytes 2949128 | tf_op jit(solution)/shard_map/ppermute | solution.py:30
  39.3 20.4 %collective-permute-start.8 = (bf16[48,5120]{1,0:T(8,128)(2,1)S(1)}, bf16[48,5120]{1,0:T(8,128)(2,1)S(1)}, u32[]{:S(2)}, u32[]{:S(2)}) collective-permute-start(bf16[48,5120]{1,0:T(8,128)(2,1)S(1)} %get-tuple-element.23), channel_id=1, source_target_pairs={{0,3},{1,0},{2,1},{3,2},{4,7},{5,4},{6,5},{7,6},{8,11},{9,8},{10,9... | collective-permute-start | bytes 1474568 | tf_op jit(solution)/shard_map/ppermute | solution.py:26
  40.7 26.0 %collective-permute-start.4 = (bf16[64,5120]{1,0:T(8,128)(2,1)S(1)}, bf16[64,5120]{1,0:T(8,128)(2,1)S(1)}, u32[]{:S(2)}, u32[]{:S(2)}) collective-permute-start(bf16[64,5120]{1,0:T(8,128)(2,1)S(1)} %get-tuple-element.20), channel_id=1, source_target_pairs={{0,1},{1,2},{2,3},{3,0},{4,5},{5,6},{6,7},{7,4},{8,9},{9,10},{10,1... | collective-permute-start | bytes 1966088 | tf_op jit(solution)/shard_map/ppermute | solution.py:26
  55.5 7.8 %collective-permute-start.7 = (bf16[16,5120]{1,0:T(8,128)(2,1)S(1)}, bf16[16,5120]{1,0:T(8,128)(2,1)S(1)}, u32[]{:S(2)}, u32[]{:S(2)}) collective-permute-start(bf16[16,5120]{1,0:T(8,128)(2,1)S(1)} %get-tuple-element.22), channel_id=1, source_target_pairs={{0,3},{1,0},{2,1},{3,2},{4,7},{5,4},{6,5},{7,6},{8,11},{9,8},{10,9... | collective-permute-start | bytes 491528 | tf_op jit(solution)/shard_map/ppermute | solution.py:26
  57.5 19.4 %collective-permute-start.10 = (bf16[48,5120]{1,0:T(8,128)(2,1)S(1)}, bf16[48,5120]{1,0:T(8,128)(2,1)S(1)}, u32[]{:S(2)}, u32[]{:S(2)}) collective-permute-start(bf16[48,5120]{1,0:T(8,128)(2,1)S(1)} %get-tuple-element.25), channel_id=1, source_target_pairs={{0,1},{1,2},{2,3},{3,0},{4,5},{5,6},{6,7},{7,4},{8,9},{9,10},{10,1... | collective-permute-start | bytes 1474568 | tf_op jit(solution)/shard_map/ppermute | solution.py:26
  59.8 6.9 %copy-start.10 = (bf16[48,5120]{1,0:T(8,128)(2,1)}, bf16[48,5120]{1,0:T(8,128)(2,1)S(1)}, u32[]{:S(2)}) copy-start(bf16[48,5120]{1,0:T(8,128)(2,1)S(1)} %collective-permute-done.8.refs_7_.refs_9_) | copy-start | bytes 1474564
  59.8 17.1 %collective-permute-start.12 = (bf16[48,5120]{1,0:T(8,128)(2,1)S(1)}, bf16[48,5120]{1,0:T(8,128)(2,1)S(1)}, u32[]{:S(2)}, u32[]{:S(2)}) collective-permute-start(bf16[48,5120]{1,0:T(8,128)(2,1)S(1)} %collective-permute-done.8.refs_7_.refs_9_), channel_id=1, source_target_pairs={{0,4},{1,5},{2,6},{3,7},{4,0},{5,1},{6,2},{7,3},{8,12},{9,13},{10,... | collective-permute-start | bytes 1474568 | tf_op jit(solution)/shard_map/ppermute | solution.py:30
  63.3 3.4 %copy-start.11 = (bf16[16,5120]{1,0:T(8,128)(2,1)}, bf16[16,5120]{1,0:T(8,128)(2,1)S(1)}, u32[]{:S(2)}) copy-start(bf16[16,5120]{1,0:T(8,128)(2,1)S(1)} %collective-permute-done.7.refs_6_.refs_8_) | copy-start | bytes 491524
  63.3 14.6 %slice-start = ((s8[5242880]{0:T(1024)(128)(4,1)}), s8[4194304]{0:T(1024)(128)(4,1)S(1)}, s32[]{:S(2)}) async-start(s8[5242880]{0:T(1024)(128)(4,1)} %bitcast.38), calls=%async_computation | async-start | bytes 8388608
  63.3 14.6 %slice-start.1 = ((s8[5242880]{0:T(1024)(128)(4,1)}), s8[1048576]{0:T(1024)(128)(4,1)S(1)}, s32[]{:S(2)}) async-start(s8[5242880]{0:T(1024)(128)(4,1)} %bitcast.38), calls=%async_computation.1 | async-start | bytes 2097152
  63.3 10.2 %collective-permute-start.11 = (bf16[32,5120]{1,0:T(8,128)(2,1)S(1)}, bf16[32,5120]{1,0:T(8,128)(2,1)S(1)}, u32[]{:S(2)}, u32[]{:S(2)}) collective-permute-start(bf16[32,5120]{1,0:T(8,128)(2,1)S(1)} %get-tuple-element.26), channel_id=1, source_target_pairs={{0,3},{1,0},{2,1},{3,2},{4,7},{5,4},{6,5},{7,6},{8,11},{9,8},{10,9... | collective-permute-start | bytes 983048 | tf_op jit(solution)/shard_map/ppermute | solution.py:26
  73.5 3.4 %copy-start.15 = (bf16[32,5120]{1,0:T(8,128)(2,1)}, bf16[32,5120]{1,0:T(8,128)(2,1)S(1)}, u32[]{:S(2)}) copy-start(bf16[32,5120]{1,0:T(8,128)(2,1)S(1)} %collective-permute-done.11.refs_15_) | copy-start | bytes 983044
  94.1 6.5 %collective-permute-start.13 = (bf16[8,32,5120]{2,1,0:T(8,128)(2,1)S(1)}, bf16[8,32,5120]{2,1,0:T(8,128)(2,1)S(1)}, u32[]{:S(2)}, u32[]{:S(2)}) collective-permute-start(bf16[8,32,5120]{2,1,0:T(8,128)(2,1)S(1)} %get-tuple-element.28), channel_id=1, source_target_pairs={{0,8},{8,0},{16,24},{24,16},{32,40},{40,32},{48,56},{56,48},{64,72... | collective-permute-start | bytes 7864328 | tf_op jit(solution)/shard_map/ppermute | solution.py:34
  100.6 36.5 %copy-start.7 = (f32[4,8,5120]{2,1,0:T(8,128)S(1)}, f32[4,8,5120]{2,1,0:T(8,128)}, u32[]{:S(2)}) copy-start(f32[4,8,5120]{2,1,0:T(8,128)} %param.15) | copy-start | bytes 1966084
  100.6 36.5 %copy-start.8 = (f32[4,8,5120]{2,1,0:T(8,128)S(1)}, f32[4,8,5120]{2,1,0:T(8,128)}, u32[]{:S(2)}) copy-start(f32[4,8,5120]{2,1,0:T(8,128)} %param.13) | copy-start | bytes 1966084
  100.6 36.5 %copy-start.9 = (f32[4,8,5120]{2,1,0:T(8,128)S(1)}, f32[4,8,5120]{2,1,0:T(8,128)}, u32[]{:S(2)}) copy-start(f32[4,8,5120]{2,1,0:T(8,128)} %param.14) | copy-start | bytes 1966084
  101.4 14.1 %collective-permute-start.14 = (bf16[32,5120]{1,0:T(8,128)(2,1)S(1)}, bf16[32,5120]{1,0:T(8,128)(2,1)S(1)}, u32[]{:S(2)}, u32[]{:S(2)}) collective-permute-start(bf16[32,5120]{1,0:T(8,128)(2,1)S(1)} %get-tuple-element.32), channel_id=1, source_target_pairs={{0,80},{8,88},{16,64},{24,72},{32,112},{40,120},{48,96},{56,104},{... | collective-permute-start | bytes 983048 | tf_op jit(solution)/shard_map/ppermute | solution.py:45
  107.7 14.6 %collective-permute-start.20 = (bf16[32,5120]{1,0:T(8,128)(2,1)S(1)}, bf16[32,5120]{1,0:T(8,128)(2,1)S(1)}, u32[]{:S(2)}, u32[]{:S(2)}) collective-permute-start(bf16[32,5120]{1,0:T(8,128)(2,1)S(1)} %get-tuple-element.33), channel_id=1, source_target_pairs={{0,64},{8,72},{16,80},{24,88},{32,96},{40,104},{48,112},{56,120},{... | collective-permute-start | bytes 983048 | tf_op jit(solution)/shard_map/ppermute | solution.py:45
  107.8 22.5 %collective-permute-start.19 = (bf16[32,5120]{1,0:T(8,128)(2,1)S(1)}, bf16[32,5120]{1,0:T(8,128)(2,1)S(1)}, u32[]{:S(2)}, u32[]{:S(2)}) collective-permute-start(bf16[32,5120]{1,0:T(8,128)(2,1)S(1)} %get-tuple-element.34), channel_id=1, source_target_pairs={{0,48},{8,56},{16,32},{24,40},{32,80},{40,88},{48,64},{56,72},{64,... | collective-permute-start | bytes 983048 | tf_op jit(solution)/shard_map/ppermute | solution.py:45
  108.4 21.8 %collective-permute-start.18 = (bf16[32,5120]{1,0:T(8,128)(2,1)S(1)}, bf16[32,5120]{1,0:T(8,128)(2,1)S(1)}, u32[]{:S(2)}, u32[]{:S(2)}) collective-permute-start(bf16[32,5120]{1,0:T(8,128)(2,1)S(1)} %get-tuple-element.35), channel_id=1, source_target_pairs={{0,16},{8,24},{16,0},{24,8},{32,48},{40,56},{48,32},{56,40},{64,80... | collective-permute-start | bytes 983048 | tf_op jit(solution)/shard_map/ppermute | solution.py:45
  111.8 18.5 %collective-permute-start.17 = (bf16[32,5120]{1,0:T(8,128)(2,1)S(1)}, bf16[32,5120]{1,0:T(8,128)(2,1)S(1)}, u32[]{:S(2)}, u32[]{:S(2)}) collective-permute-start(bf16[32,5120]{1,0:T(8,128)(2,1)S(1)} %get-tuple-element.36), channel_id=1, source_target_pairs={{0,96},{8,104},{16,112},{24,120},{32,0},{40,8},{48,16},{56,24},{64... | collective-permute-start | bytes 983048 | tf_op jit(solution)/shard_map/ppermute | solution.py:45
  115.5 21.5 %collective-permute-start.16 = (bf16[32,5120]{1,0:T(8,128)(2,1)S(1)}, bf16[32,5120]{1,0:T(8,128)(2,1)S(1)}, u32[]{:S(2)}, u32[]{:S(2)}) collective-permute-start(bf16[32,5120]{1,0:T(8,128)(2,1)S(1)} %get-tuple-element.37), channel_id=1, source_target_pairs={{0,32},{8,40},{16,48},{24,56},{32,64},{40,72},{48,80},{56,88},{64,... | collective-permute-start | bytes 983048 | tf_op jit(solution)/shard_map/ppermute | solution.py:45
  122.3 14.7 %collective-permute-start.15 = (bf16[32,5120]{1,0:T(8,128)(2,1)S(1)}, bf16[32,5120]{1,0:T(8,128)(2,1)S(1)}, u32[]{:S(2)}, u32[]{:S(2)}) collective-permute-start(bf16[32,5120]{1,0:T(8,128)(2,1)S(1)} %get-tuple-element.38), channel_id=1, source_target_pairs={{0,112},{8,120},{16,96},{24,104},{32,16},{40,24},{48,0},{56,8},{64... | collective-permute-start | bytes 983048 | tf_op jit(solution)/shard_map/ppermute | solution.py:45
  (7 other events, 7.6 us)

commit v4 on v3

--- a/solution.py
+++ b/solution.py
@@ -189,41 +189,42 @@
 
 def late_kernel(first_block, spans, *refs):
     count = len(spans)
-    place_ref, gain_ref, ids_ref, upstream_ref, weight = refs[:5]
-    pieces, refs = refs[5 : 5 + count], refs[5 + count :]
-    out_ref, tokens, upstream, turned, sems = refs
+    place_ref, gain_ref, ids_ref, upstream_ref, weight, before = refs[:6]
+    pieces, refs = refs[6 : 6 + count], refs[6 + count :]
+    out_ref, tokens, upstream, turned, rotated, sems = refs
     copies = Copies(sems)
     needed = start_upstream(copies, place_ref, first_block, upstream_ref, upstream)
     ready = start_tokens(copies, pieces, spans, tokens)
     wait_all(needed)
     rotated_gradient(
-        place_ref, first_block, gain_ref, ids_ref, tokens, weight, upstream, turned, out_ref, 0, ready
-    )
-
-
-def renew_kernel(first_block, late_spans, spans, *refs):
-    late_count, count = len(late_spans), len(spans)
-    place_ref, gain_ref, ids_ref, upstream_ref, weight, before_ref, late_ref = refs[:7]
-    late, refs = refs[7 : 7 + late_count], refs[7 + late_count :]
+        place_ref, first_block, gain_ref, ids_ref, tokens, weight, upstream, turned, rotated, 0, ready
+    )
+
+    @pl.loop(0, out_ref.shape[1] // TILE)
+    def _(tile):
+        columns = pl.ds(pl.multiple_of(tile * TILE, TILE), TILE)
+        out_ref[:, columns] = before[:, columns] + contract(rotated[...], tokens[:, columns], 1, 0)
+
+
+def renew_kernel(first_block, count, *refs):
+    place_ref, gain_ref, ids_ref, upstream_ref, weight, before_ref = refs[:6]
+    refs = refs[6:]
     pieces, (mine_ref, theirs_ref) = refs[:count], refs[count : count + 2]
     tokens, upstream, turned, rotated, split, factors, sems = refs[count + 2 :]
     all_rows, width = weight.shape
     size = gain_ref.shape[1]
     heads = all_rows // size
     tiles = width // TILE
-    rows = upstream.shape[0]
-    late_rows = tokens.shape[0] - rows
     copies = Copies(sems)
     needed = start_upstream(copies, place_ref, first_block, upstream_ref, upstream)
-    ready = start_tokens(copies, pieces, spans, tokens, late_rows)
-    others = start_tokens(copies, late, late_spans, tokens)
-    rotated[:, :late_rows] = late_ref[...]
+    offset = 0
+    for piece in pieces:
+        tokens[pl.ds(offset, piece.shape[0]), :] = piece[...]
+        offset += piece.shape[0]
     wait_all(needed)
     rotated_gradient(
-        place_ref, first_block, gain_ref, ids_ref, tokens, weight, upstream, turned, rotated,
-        late_rows, ready,
-    )
-    wait_all(others)
+        place_ref, first_block, gain_ref, ids_ref, tokens, weight, upstream, turned, rotated, 0, []
+    )
 
     @pl.loop(0, tiles)
     def _(tile):
@@ -383,48 +384,51 @@
     )
 
 
-def late_call(common, first_block, pieces):
+def late_call(common, first_block, before, pieces):
     all_rows, width = common[-1].shape
     rows = rows_of(pieces)
     return call(
         functools.partial(late_kernel, first_block, spans_of(pieces)),
-        jax.ShapeDtypeStruct((all_rows, rows), jnp.bfloat16),
-        COMMON_SPECS + [OUTSIDE] * len(pieces),
+        jax.ShapeDtypeStruct(before.shape, before.dtype),
+        COMMON_SPECS + [INSIDE] + [OUTSIDE] * len(pieces),
         INSIDE,
         [pltpu.VMEM((rows, width), jnp.bfloat16)]
         + scratch_of(common, rows)
-        + [pltpu.SemaphoreType.DMA((len(pieces) + rows // BLOCK,))],
-        2 * rows * all_rows * width,
+        + [
+            pltpu.VMEM((all_rows, rows), jnp.bfloat16),
+            pltpu.SemaphoreType.DMA((len(pieces) + rows // BLOCK,)),
+        ],
+        4 * rows * all_rows * width,
         2 * (rows + all_rows) * width,
         LATE_VMEM,
-        [*common, *arrays_of(pieces)],
-    )
-
-
-def renew_call(common, first_block, before, late_rotated, late, pieces):
+        [*common, before, *arrays_of(pieces)],
+        {len(common): 0},
+    )
+
+
+def renew_call(common, first_block, before, pieces):
     all_rows, width = common[-1].shape
     size = common[1].shape[1]
     heads = all_rows // size
     rows = rows_of(pieces)
-    total = rows + rows_of(late)
     shape = jax.ShapeDtypeStruct((8, all_rows // 16, width), jnp.bfloat16)
     return call(
-        functools.partial(renew_kernel, first_block, spans_of(late), spans_of(pieces)),
+        functools.partial(renew_kernel, first_block, len(pieces)),
         (shape, shape),
-        COMMON_SPECS + [INSIDE, INSIDE] + [OUTSIDE] * (len(late) + len(pieces)),
+        COMMON_SPECS + [INSIDE] * (1 + len(pieces)),
         (INSIDE, INSIDE),
-        [pltpu.VMEM((total, width), jnp.bfloat16)]
+        [pltpu.VMEM((rows, width), jnp.bfloat16)]
         + scratch_of(common, rows)
         + [
-            pltpu.VMEM((all_rows, total), jnp.bfloat16),
+            pltpu.VMEM((all_rows, rows), jnp.bfloat16),
             pltpu.VMEM((heads, 2 * size, width), jnp.bfloat16),
             pltpu.VMEM((heads, 2 * size, 2 * size), jnp.bfloat16),
-            pltpu.SemaphoreType.DMA((len(late) + len(pieces) + rows // BLOCK,)),
+            pltpu.SemaphoreType.DMA((rows // BLOCK,)),
         ],
         (4 * rows + 16 * size) * all_rows * width,
         8 * all_rows * width,
         RENEW_VMEM,
-        [*common, before, late_rotated, *arrays_of(late), *arrays_of(pieces)],
+        [*common, before, *pieces],
     )
 
 
@@ -445,7 +449,7 @@
     place = lax.axis_index("grp")
     spot = lax.axis_index("rep")
     numbers = []
-    for step_z, step_x in ((0, 0), (0, -1), (0, 1), (1, 0), (0, 2), (1, -1), (1, 1), (1, 2)):
+    for step_z, step_x in ((0, 0), (0, -1), (0, 1), (1, 0), (1, -1), (1, 1), (0, 2), (1, 2)):
         numbers.append(((place // RING + step_z) % 2) * RING + (place + step_x) % RING)
     numbers += [spot // 4, (spot // 2) % 2, spot % 2]
     common = (
@@ -482,13 +486,10 @@
     over_far0, over_far1 = along_x(over_left_far, 1), along_x(over_right_far, -1)
     far1 = along_x(right_far, -1)
     over_far_b = across_z(far_b)
-    late = [
-        far0, far1, far_b, over_left_a, (over_b2, 0, rows_b), over_right_a, (over_b2, rows_b, rows_b)
-    ]
-    late_rotated = late_call(common, 4, late)
-    mine, theirs = renew_call(
-        common, 7, before, late_rotated, late, [over_far0, over_far1, over_far_b]
-    )
+    late = [over_left_a, (over_b2, 0, rows_b), over_right_a, (over_b2, rows_b, rows_b)]
+    before = late_call(common, 4, before, late)
+    last = [far0, far1, far_b, over_far0, over_far1, over_far_b]
+    mine, theirs = renew_call(common, 6, before, last)
 
     theirs = to_other_core(theirs)
     summed = None

time: 139 us -> 136 us (0.978)
  waiting for transfers between devices: 59.2 us -> 54.5 us
  starting transfers between devices: 33.4 us -> 35.6 us
    ppermute x7, starting transfers between devices: 13.7 us -> 17.7 us  [to_chip(): return lax.ppermute(array, 'rep', pairs)]
    ppermute x7, waiting for transfers between devices: 21.9 us -> 19 us  [to_chip(): return lax.ppermute(array, 'rep', pairs)]
    ppermute x9, starting transfers between devices: 12.6 us -> 10.7 us  [along_x(): return lax.ppermute(array, 'grp', pairs)]
    ppermute x9, waiting for transfers between devices: 15.2 us -> 13.6 us  [along_x(): return lax.ppermute(array, 'grp', pairs)]
    unnamed x36 -> x24, local copies, waits for them, and re-layouts: 6.73 us -> 5.91 us
  transfers between devices with their start and end apart: 21 -> 21, of which waited for: 11 -> 11; matrix products, arithmetic and copies ran while one was open for 0% -> 0% of each run, Pallas kernels for 14% -> 15%
where the time goes in v4:
time: 136 us; the launch traced here: 135 us
  waiting for transfers between devices  54.5 us (40%)
  starting transfers between devices  35.6 us (26%)
  Pallas kernels  35.4 us (26%)
  local copies, waits for them, and re-layouts  6 us (4%)
  other arithmetic  2.65 us (2%)
    pallas_call x6, Pallas kernels, call(): pl.pallas_call(kernel, out_shape=out_shape, in_specs=in_specs, out_specs=...  35.4 us
    ppermute x7, waiting for transfers between devices, to_chip(): return lax.ppermute(array, 'rep', pairs)  19 us
    ppermute x7, starting transfers between devices, to_chip(): return lax.ppermute(array, 'rep', pairs)  17.7 us
    ppermute x4, waiting for transfers between devices, across_z(): lax.ppermute(array, 'grp', [(g, (g + RING) % (2 * RING)) for g in range(2...  17.3 us
    ppermute x9, waiting for transfers between devices, along_x(): return lax.ppermute(array, 'grp', pairs)  13.6 us
    ppermute x9, starting transfers between devices, along_x(): return lax.ppermute(array, 'grp', pairs)  10.7 us
    unnamed x24, local copies, waits for them, and re-layouts  5.91 us
    ppermute x4, starting transfers between devices, across_z(): lax.ppermute(array, 'grp', [(g, (g + RING) % (2 * RING)) for g in range(2...  5.49 us
  transfers between devices with their start and end apart: 21, of which 11 were waited for; matrix products, arithmetic and copies ran while one was open for 0% of the time, Pallas kernels for 15%

profile of v4, /device:TPU:1, one launch (start us, length us, event | category | flops | bytes accessed | tf_op | source)
XLA Modules:
  0.0 134.9 jit_solution(4765122830069367622)
XLA Ops:
  0.7 2.1 %collective-permute-start = (bf16[128,5120]{1,0:T(8,128)(2,1)}, bf16[128,5120]{1,0:T(8,128)(2,1)S(1)}, u32[]{:S(2)}, u32[]{:S(2)}) collective-permute-start(bf16[128,5120]{1,0:T(8,128)(2,1)} %refs_5_.1), channel_id=1, source_target_pairs={{0,1},{1,2},{2,3},{3,0},{4,5},{5,6},{6,7},{7,4},{8,9},{9,10},{10,1... | collective-permute-start | bytes 3932168 | tf_op jit(solution)/shard_map/ppermute | solution.py:26
  2.8 1.4 %collective-permute-start.1 = (bf16[128,5120]{1,0:T(8,128)(2,1)}, bf16[128,5120]{1,0:T(8,128)(2,1)S(1)}, u32[]{:S(2)}, u32[]{:S(2)}) collective-permute-start(bf16[128,5120]{1,0:T(8,128)(2,1)} %refs_5_.1), channel_id=1, source_target_pairs={{0,3},{1,0},{2,1},{3,2},{4,7},{5,4},{6,5},{7,6},{8,11},{9,8},{10,9... | collective-permute-start | bytes 3932168 | tf_op jit(solution)/shard_map/ppermute | solution.py:26
  4.1 1.3 shard_map.103
  5.4 1.8 %collective-permute-start.2 = (bf16[80,5120]{1,0:T(8,128)(2,1)S(1)}, bf16[80,5120]{1,0:T(8,128)(2,1)}, u32[]{:S(2)}, u32[]{:S(2)}) collective-permute-start(bf16[80,5120]{1,0:T(8,128)(2,1)S(1)} %get-tuple-element.16), channel_id=1, source_target_pairs={{0,4},{1,5},{2,6},{3,7},{4,0},{5,1},{6,2},{7,3},{8,12},{9,13},{10,... | collective-permute-start | bytes 2457608 | tf_op jit(solution)/shard_map/ppermute | solution.py:30
  7.3 17.3 %collective-permute-done.2.refs_8_ = bf16[80,5120]{1,0:T(8,128)(2,1)} collective-permute-done((bf16[80,5120]{1,0:T(8,128)(2,1)S(1)}, bf16[80,5120]{1,0:T(8,128)(2,1)}, u32[]{:S(2)}, u32[]{:S(2)}) %collective-permute-start.2) | collective-permute-done | bytes 819232 | tf_op jit(solution)/shard_map/ppermute | solution.py:30
  24.7 2.7 %collective-permute-start.6 = (bf16[80,5120]{1,0:T(8,128)(2,1)}, bf16[80,5120]{1,0:T(8,128)(2,1)}, u32[]{:S(2)}, u32[]{:S(2)}) collective-permute-start(bf16[80,5120]{1,0:T(8,128)(2,1)} %collective-permute-done.2.refs_8_), channel_id=1, source_target_pairs={{0,3},{1,0},{2,1},{3,2},{4,7},{5,4},{6,5},{7,6},{8,11},{9,8},{10,9... | collective-permute-start | bytes 2457608 | tf_op jit(solution)/shard_map/ppermute | solution.py:26
  27.3 5.0 %collective-permute-done.refs_0_.refs_6_ = bf16[128,5120]{1,0:T(8,128)(2,1)S(1)} collective-permute-done((bf16[128,5120]{1,0:T(8,128)(2,1)}, bf16[128,5120]{1,0:T(8,128)(2,1)S(1)}, u32[]{:S(2)}, u32[]{:S(2)}) %collective-permute-start) | collective-permute-done | bytes 1310752 | tf_op jit(solution)/shard_map/ppermute | solution.py:26
  34.5 1.6 %shard_map.104 = (bf16[64,5120]{1,0:T(8,128)(2,1)S(1)}, bf16[16,5120]{1,0:T(8,128)(2,1)S(1)}, bf16[48,5120]{1,0:T(8,128)(2,1)S(1)}, bf16[96,5120]{1,0:T(8,128)(2,1)S(1)}) custom-call(bf16[128,5120]{1,0:T(8,128)(2,1)} %copy-done.4, bf16[128,5120]{1,0:T(8,128)(2,1)} %copy-done.5), custom_call_target="tpu_custom_call" | custom-call | bytes 4587520 | tf_op jit(solution)/shard_map/pallas_call | solution.py:294
  36.1 2.0 %collective-permute-start.5 = (bf16[96,5120]{1,0:T(8,128)(2,1)S(1)}, bf16[96,5120]{1,0:T(8,128)(2,1)}, u32[]{:S(2)}, u32[]{:S(2)}) collective-permute-start(bf16[96,5120]{1,0:T(8,128)(2,1)S(1)} %get-tuple-element.20), channel_id=1, source_target_pairs={{0,4},{1,5},{2,6},{3,7},{4,0},{5,1},{6,2},{7,3},{8,12},{9,13},{10,... | collective-permute-start | bytes 2949128 | tf_op jit(solution)/shard_map/ppermute | solution.py:30
  38.2 1.3 collective-permute-start.9
  40.3 2.5 %copy-done = bf16[1,4,128,5120]{3,2,1,0:T(8,128)(2,1)S(1)} copy-done((bf16[1,4,128,5120]{3,2,1,0:T(8,128)(2,1)S(1)}, bf16[1,4,128,5120]{3,2,1,0:T(8,128)(2,1)}, u32[]{:S(2)}) %copy-start) | copy-done | bytes 5242904
  42.8 9.6 %shard_map.105 = (f32[512,5120]{1,0:T(8,128)S(1)}, bf16[16,5120]{1,0:T(8,128)(2,1)S(1)}) custom-call(s32[11]{0:T(128)S(1)} %stack.47.refs_0_, f32[1,128]{1,0:T(1,128)S(1)} %bitcast.44, s32[8,128]{1,0:T(8,128)S(1)} %bitcast.41, bf16[1024,512]{1,0:T(8,128)(2,1)} %refs_3_.5, bf16[512,5120]{1,0:T(8,128)(2,1)S(1)} %bitcast.36, ...), custom_call_target="tpu_custom_call", output_to_operand_aliasing={{1}: (10, {})} | custom-call | flops 5368709120 | bytes 20971520 | tf_op jit(solution)/shard_map/pallas_call | solution.py:294
  53.1 1.3 shard_map.107
  54.7 5.8 %collective-permute-done.9.refs_8_ = bf16[48,5120]{1,0:T(8,128)(2,1)S(1)} collective-permute-done((bf16[48,5120]{1,0:T(8,128)(2,1)S(1)}, bf16[48,5120]{1,0:T(8,128)(2,1)S(1)}, u32[]{:S(2)}, u32[]{:S(2)}) %collective-permute-start.9) | collective-permute-done | bytes 491552 | tf_op jit(solution)/shard_map/ppermute | solution.py:26
  60.5 1.5 %collective-permute-start.12 = (bf16[48,5120]{1,0:T(8,128)(2,1)S(1)}, bf16[48,5120]{1,0:T(8,128)(2,1)S(1)}, u32[]{:S(2)}, u32[]{:S(2)}) collective-permute-start(bf16[48,5120]{1,0:T(8,128)(2,1)S(1)} %collective-permute-done.9.refs_8_), channel_id=1, source_target_pairs={{0,4},{1,5},{2,6},{3,7},{4,0},{5,1},{6,2},{7,3},{8,12},{9,13},{10,... | collective-permute-start | bytes 1474568 | tf_op jit(solution)/shard_map/ppermute | solution.py:30
  62.0 2.7 %collective-permute-start.11 = (bf16[32,5120]{1,0:T(8,128)(2,1)S(1)}, bf16[32,5120]{1,0:T(8,128)(2,1)S(1)}, u32[]{:S(2)}, u32[]{:S(2)}) collective-permute-start(bf16[32,5120]{1,0:T(8,128)(2,1)S(1)} %get-tuple-element.26), channel_id=1, source_target_pairs={{0,3},{1,0},{2,1},{3,2},{4,7},{5,4},{6,5},{7,6},{8,11},{9,8},{10,9... | collective-permute-start | bytes 983048 | tf_op jit(solution)/shard_map/ppermute | solution.py:26
  64.8 6.7 %shard_map.106.refs_5_ = f32[512,5120]{1,0:T(8,128)S(1)} custom-call(s32[11]{0:T(128)S(1)} %stack.47.refs_0_, f32[1,128]{1,0:T(1,128)S(1)} %bitcast.45, s32[8,128]{1,0:T(8,128)S(1)} %bitcast.42, bf16[1024,512]{1,0:T(8,128)(2,1)} %refs_3_.5, bf16[512,5120]{1,0:T(8,128)(2,1)S(1)} %bitcast.37, ...), custom_call_target="tpu_custom_call", output_to_operand_aliasing={{}: (5, {})} | custom-call | flops 2684354560 | bytes 7864320 | tf_op jit(solution)/shard_map/pallas_call | solution.py:294
  71.5 1.6 %collective-permute-done.8.refs_7_ = bf16[16,5120]{1,0:T(8,128)(2,1)S(1)} collective-permute-done((bf16[16,5120]{1,0:T(8,128)(2,1)S(1)}, bf16[16,5120]{1,0:T(8,128)(2,1)S(1)}, u32[]{:S(2)}, u32[]{:S(2)}) %collective-permute-start.8) | collective-permute-done | bytes 163872 | tf_op jit(solution)/shard_map/ppermute | solution.py:26
  73.1 1.4 %collective-permute-done.10.refs_9_ = bf16[48,5120]{1,0:T(8,128)(2,1)S(1)} collective-permute-done((bf16[48,5120]{1,0:T(8,128)(2,1)S(1)}, bf16[48,5120]{1,0:T(8,128)(2,1)S(1)}, u32[]{:S(2)}, u32[]{:S(2)}) %collective-permute-start.10) | collective-permute-done | bytes 491552 | tf_op jit(solution)/shard_map/ppermute | solution.py:26
  74.5 14.8 %shard_map.108 = (bf16[8,32,5120]{2,1,0:T(8,128)(2,1)S(1)}, bf16[8,32,5120]{2,1,0:T(8,128)(2,1)S(1)}) custom-call(s32[11]{0:T(128)S(1)} %stack.47.refs_0_, f32[1,128]{1,0:T(1,128)S(1)} %bitcast.46, s32[8,128]{1,0:T(8,128)S(1)} %bitcast.43, bf16[1024,512]{1,0:T(8,128)(2,1)} %refs_3_.5, bf16[512,5120]{1,0:T(8,128)(2,1)S(1)} %bitcast.40, ...), custom_call_target="tpu_custom_call" | custom-call | flops 8053063680 | bytes 20971520 | tf_op jit(solution)/shard_map/pallas_call | solution.py:294
  89.2 1.8 %collective-permute-start.13 = (bf16[8,32,5120]{2,1,0:T(8,128)(2,1)S(1)}, bf16[8,32,5120]{2,1,0:T(8,128)(2,1)S(1)}, u32[]{:S(2)}, u32[]{:S(2)}) collective-permute-start(bf16[8,32,5120]{2,1,0:T(8,128)(2,1)S(1)} %get-tuple-element.28), channel_id=1, source_target_pairs={{0,8},{8,0},{16,24},{24,16},{32,40},{40,32},{48,56},{56,48},{64,72... | collective-permute-start | bytes 7864328 | tf_op jit(solution)/shard_map/ppermute | solution.py:34
  91.0 4.5 %collective-permute-done.13 = bf16[8,32,5120]{2,1,0:T(8,128)(2,1)S(1)} collective-permute-done((bf16[8,32,5120]{2,1,0:T(8,128)(2,1)S(1)}, bf16[8,32,5120]{2,1,0:T(8,128)(2,1)S(1)}, u32[]{:S(2)}, u32[]{:S(2)}) %collective-permute-start.13) | collective-permute-done | bytes 2621472 | tf_op jit(solution)/shard_map/ppermute | solution.py:34
  96.4 6.4 %collective-permute-start.14 = (bf16[32,5120]{1,0:T(8,128)(2,1)S(1)}, bf16[32,5120]{1,0:T(8,128)(2,1)S(1)}, u32[]{:S(2)}, u32[]{:S(2)}) collective-permute-start(bf16[32,5120]{1,0:T(8,128)(2,1)S(1)} %get-tuple-element.32), channel_id=1, source_target_pairs={{0,80},{8,88},{16,64},{24,72},{32,112},{40,120},{48,96},{56,104},{... | collective-permute-start | bytes 983048 | tf_op jit(solution)/shard_map/ppermute | solution.py:45
  103.4 2.2 %collective-permute-start.17 = (bf16[32,5120]{1,0:T(8,128)(2,1)S(1)}, bf16[32,5120]{1,0:T(8,128)(2,1)S(1)}, u32[]{:S(2)}, u32[]{:S(2)}) collective-permute-start(bf16[32,5120]{1,0:T(8,128)(2,1)S(1)} %get-tuple-element.36), channel_id=1, source_target_pairs={{0,96},{8,104},{16,112},{24,120},{32,0},{40,8},{48,16},{56,24},{64... | collective-permute-start | bytes 983048 | tf_op jit(solution)/shard_map/ppermute | solution.py:45
  105.7 3.3 %collective-permute-start.18 = (bf16[32,5120]{1,0:T(8,128)(2,1)S(1)}, bf16[32,5120]{1,0:T(8,128)(2,1)S(1)}, u32[]{:S(2)}, u32[]{:S(2)}) collective-permute-start(bf16[32,5120]{1,0:T(8,128)(2,1)S(1)} %get-tuple-element.35), channel_id=1, source_target_pairs={{0,16},{8,24},{16,0},{24,8},{32,48},{40,56},{48,32},{56,40},{64,80... | collective-permute-start | bytes 983048 | tf_op jit(solution)/shard_map/ppermute | solution.py:45
  109.0 1.8 %collective-permute-done.14 = bf16[32,5120]{1,0:T(8,128)(2,1)S(1)} collective-permute-done((bf16[32,5120]{1,0:T(8,128)(2,1)S(1)}, bf16[32,5120]{1,0:T(8,128)(2,1)S(1)}, u32[]{:S(2)}, u32[]{:S(2)}) %collective-permute-start.14) | collective-permute-done | bytes 327712 | tf_op jit(solution)/shard_map/ppermute | solution.py:45
  110.8 3.3 %collective-permute-start.19 = (bf16[32,5120]{1,0:T(8,128)(2,1)S(1)}, bf16[32,5120]{1,0:T(8,128)(2,1)S(1)}, u32[]{:S(2)}, u32[]{:S(2)}) collective-permute-start(bf16[32,5120]{1,0:T(8,128)(2,1)S(1)} %get-tuple-element.34), channel_id=1, source_target_pairs={{0,48},{8,56},{16,32},{24,40},{32,80},{40,88},{48,64},{56,72},{64,... | collective-permute-start | bytes 983048 | tf_op jit(solution)/shard_map/ppermute | solution.py:45
  114.1 3.6 %collective-permute-done.15 = bf16[32,5120]{1,0:T(8,128)(2,1)S(1)} collective-permute-done((bf16[32,5120]{1,0:T(8,128)(2,1)S(1)}, bf16[32,5120]{1,0:T(8,128)(2,1)S(1)}, u32[]{:S(2)}, u32[]{:S(2)}) %collective-permute-start.15) | collective-permute-done | bytes 327712 | tf_op jit(solution)/shard_map/ppermute | solution.py:45
  117.7 1.8 %collective-permute-start.20 = (bf16[32,5120]{1,0:T(8,128)(2,1)S(1)}, bf16[32,5120]{1,0:T(8,128)(2,1)S(1)}, u32[]{:S(2)}, u32[]{:S(2)}) collective-permute-start(bf16[32,5120]{1,0:T(8,128)(2,1)S(1)} %get-tuple-element.33), channel_id=1, source_target_pairs={{0,64},{8,72},{16,80},{24,88},{32,96},{40,104},{48,112},{56,120},{... | collective-permute-start | bytes 983048 | tf_op jit(solution)/shard_map/ppermute | solution.py:45
  119.5 5.6 %collective-permute-done.17 = bf16[32,5120]{1,0:T(8,128)(2,1)S(1)} collective-permute-done((bf16[32,5120]{1,0:T(8,128)(2,1)S(1)}, bf16[32,5120]{1,0:T(8,128)(2,1)S(1)}, u32[]{:S(2)}, u32[]{:S(2)}) %collective-permute-start.17) | collective-permute-done | bytes 327712 | tf_op jit(solution)/shard_map/ppermute | solution.py:45
  125.1 7.0 %collective-permute-done.18 = bf16[32,5120]{1,0:T(8,128)(2,1)S(1)} collective-permute-done((bf16[32,5120]{1,0:T(8,128)(2,1)S(1)}, bf16[32,5120]{1,0:T(8,128)(2,1)S(1)}, u32[]{:S(2)}, u32[]{:S(2)}) %collective-permute-start.18) | collective-permute-done | bytes 327712 | tf_op jit(solution)/shard_map/ppermute | solution.py:45
  133.1 1.8 %multiply_add_fusion = (f32[4,8,5120]{2,1,0:T(8,128)}, f32[4,8,5120]{2,1,0:T(8,128)}, f32[4,8,5120]{2,1,0:T(8,128)}) fusion(f32[4,8,5120]{2,1,0:T(8,128)S(1)} %copy-done.6, f32[4,8,5120]{2,1,0:T(8,128)S(1)} %copy-done.7, f32[4,8,5120]{2,1,0:T(8,128)S(1)} %copy-done.8, bf16[8,32,5120]{2,1,0:T(8,128)(2,1)S(1)} %collective-permute-done.13, ...), kind=kLoop, calls=%fused_computation.3 | loop fusion | flops 4587520 | bytes 6881280 | tf_op jit(solution)/shard_map/add | solution.py:508
  (44 shorter events, 6.5 us)
Async XLA Ops:
  0.6 39.7 %copy-start.3 = (f32[128]{0:T(128)S(1)}, f32[128]{0:T(128)}, u32[]{:S(2)}) copy-start(f32[128]{0:T(128)} %param.12) | copy-start | bytes 1540
  0.6 39.7 %copy-start.2 = (s32[1024]{0:T(1024)S(1)}, s32[1024]{0:T(1024)}, u32[]{:S(2)}) copy-start(s32[1024]{0:T(1024)} %param.9) | copy-start | bytes 12292
  0.7 31.6 %collective-permute-start = (bf16[128,5120]{1,0:T(8,128)(2,1)}, bf16[128,5120]{1,0:T(8,128)(2,1)S(1)}, u32[]{:S(2)}, u32[]{:S(2)}) collective-permute-start(bf16[128,5120]{1,0:T(8,128)(2,1)} %refs_5_.1), channel_id=1, source_target_pairs={{0,1},{1,2},{2,3},{3,0},{4,5},{5,6},{6,7},{7,4},{8,9},{9,10},{10,1... | collective-permute-start | bytes 3932168 | tf_op jit(solution)/shard_map/ppermute | solution.py:26
  2.8 29.5 %collective-permute-start.1 = (bf16[128,5120]{1,0:T(8,128)(2,1)}, bf16[128,5120]{1,0:T(8,128)(2,1)S(1)}, u32[]{:S(2)}, u32[]{:S(2)}) collective-permute-start(bf16[128,5120]{1,0:T(8,128)(2,1)} %refs_5_.1), channel_id=1, source_target_pairs={{0,3},{1,0},{2,1},{3,2},{4,7},{5,4},{6,5},{7,6},{8,11},{9,8},{10,9... | collective-permute-start | bytes 3932168 | tf_op jit(solution)/shard_map/ppermute | solution.py:26
  5.4 19.2 %collective-permute-start.2 = (bf16[80,5120]{1,0:T(8,128)(2,1)S(1)}, bf16[80,5120]{1,0:T(8,128)(2,1)}, u32[]{:S(2)}, u32[]{:S(2)}) collective-permute-start(bf16[80,5120]{1,0:T(8,128)(2,1)S(1)} %get-tuple-element.16), channel_id=1, source_target_pairs={{0,4},{1,5},{2,6},{3,7},{4,0},{5,1},{6,2},{7,3},{8,12},{9,13},{10,... | collective-permute-start | bytes 2457608 | tf_op jit(solution)/shard_map/ppermute | solution.py:30
  7.2 32.3 %collective-permute-start.3 = (bf16[48,5120]{1,0:T(8,128)(2,1)S(1)}, bf16[48,5120]{1,0:T(8,128)(2,1)S(1)}, u32[]{:S(2)}, u32[]{:S(2)}) collective-permute-start(bf16[48,5120]{1,0:T(8,128)(2,1)S(1)} %get-tuple-element.17), channel_id=1, source_target_pairs={{0,4},{1,5},{2,6},{3,7},{4,0},{5,1},{6,2},{7,3},{8,12},{9,13},{10,... | collective-permute-start | bytes 1474568 | tf_op jit(solution)/shard_map/ppermute | solution.py:30
  24.7 28.4 %collective-permute-start.4 = (bf16[80,5120]{1,0:T(8,128)(2,1)}, bf16[80,5120]{1,0:T(8,128)(2,1)}, u32[]{:S(2)}, u32[]{:S(2)}) collective-permute-start(bf16[80,5120]{1,0:T(8,128)(2,1)} %collective-permute-done.2.refs_8_), channel_id=1, source_target_pairs={{0,1},{1,2},{2,3},{3,0},{4,5},{5,6},{6,7},{7,4},{8,9},{9,10},{10,1... | collective-permute-start | bytes 2457608 | tf_op jit(solution)/shard_map/ppermute | solution.py:26
  24.7 28.4 %collective-permute-start.6 = (bf16[80,5120]{1,0:T(8,128)(2,1)}, bf16[80,5120]{1,0:T(8,128)(2,1)}, u32[]{:S(2)}, u32[]{:S(2)}) collective-permute-start(bf16[80,5120]{1,0:T(8,128)(2,1)} %collective-permute-done.2.refs_8_), channel_id=1, source_target_pairs={{0,3},{1,0},{2,1},{3,2},{4,7},{5,4},{6,5},{7,6},{8,11},{9,8},{10,9... | collective-permute-start | bytes 2457608 | tf_op jit(solution)/shard_map/ppermute | solution.py:26
  32.3 1.1 copy-start.4
  33.4 1.1 copy-start.5
  36.1 28.6 %collective-permute-start.5 = (bf16[96,5120]{1,0:T(8,128)(2,1)S(1)}, bf16[96,5120]{1,0:T(8,128)(2,1)}, u32[]{:S(2)}, u32[]{:S(2)}) collective-permute-start(bf16[96,5120]{1,0:T(8,128)(2,1)S(1)} %get-tuple-element.20), channel_id=1, source_target_pairs={{0,4},{1,5},{2,6},{3,7},{4,0},{5,1},{6,2},{7,3},{8,12},{9,13},{10,... | collective-permute-start | bytes 2949128 | tf_op jit(solution)/shard_map/ppermute | solution.py:30
  38.2 22.3 %collective-permute-start.9 = (bf16[48,5120]{1,0:T(8,128)(2,1)S(1)}, bf16[48,5120]{1,0:T(8,128)(2,1)S(1)}, u32[]{:S(2)}, u32[]{:S(2)}) collective-permute-start(bf16[48,5120]{1,0:T(8,128)(2,1)S(1)} %get-tuple-element.24), channel_id=1, source_target_pairs={{0,3},{1,0},{2,1},{3,2},{4,7},{5,4},{6,5},{7,6},{8,11},{9,8},{10,9... | collective-permute-start | bytes 1474568 | tf_op jit(solution)/shard_map/ppermute | solution.py:26
  39.5 0.8 copy-start.9
  39.5 33.6 %collective-permute-start.7 = (bf16[64,5120]{1,0:T(8,128)(2,1)S(1)}, bf16[64,5120]{1,0:T(8,128)(2,1)S(1)}, u32[]{:S(2)}, u32[]{:S(2)}) collective-permute-start(bf16[64,5120]{1,0:T(8,128)(2,1)S(1)} %get-tuple-element.21), channel_id=1, source_target_pairs={{0,1},{1,2},{2,3},{3,0},{4,5},{5,6},{6,7},{7,4},{8,9},{9,10},{10,1... | collective-permute-start | bytes 1966088 | tf_op jit(solution)/shard_map/ppermute | solution.py:26
  40.3 2.5 %copy-start = (bf16[1,4,128,5120]{3,2,1,0:T(8,128)(2,1)S(1)}, bf16[1,4,128,5120]{3,2,1,0:T(8,128)(2,1)}, u32[]{:S(2)}) copy-start(bf16[1,4,128,5120]{3,2,1,0:T(8,128)(2,1)} %param.11) | copy-start | bytes 15728644
  53.1 21.3 %slice-start = ((s8[5242880]{0:T(1024)(128)(4,1)}), s8[4194304]{0:T(1024)(128)(4,1)S(1)}, s32[]{:S(2)}) async-start(s8[5242880]{0:T(1024)(128)(4,1)} %bitcast.38), calls=%async_computation | async-start | bytes 8388608
  54.5 20.0 %collective-permute-start.10 = (bf16[48,5120]{1,0:T(8,128)(2,1)S(1)}, bf16[48,5120]{1,0:T(8,128)(2,1)S(1)}, u32[]{:S(2)}, u32[]{:S(2)}) collective-permute-start(bf16[48,5120]{1,0:T(8,128)(2,1)S(1)} %get-tuple-element.25), channel_id=1, source_target_pairs={{0,1},{1,2},{2,3},{3,0},{4,5},{5,6},{6,7},{7,4},{8,9},{9,10},{10,1... | collective-permute-start | bytes 1474568 | tf_op jit(solution)/shard_map/ppermute | solution.py:26
  60.5 13.9 %collective-permute-start.12 = (bf16[48,5120]{1,0:T(8,128)(2,1)S(1)}, bf16[48,5120]{1,0:T(8,128)(2,1)S(1)}, u32[]{:S(2)}, u32[]{:S(2)}) collective-permute-start(bf16[48,5120]{1,0:T(8,128)(2,1)S(1)} %collective-permute-done.9.refs_8_), channel_id=1, source_target_pairs={{0,4},{1,5},{2,6},{3,7},{4,0},{5,1},{6,2},{7,3},{8,12},{9,13},{10,... | collective-permute-start | bytes 1474568 | tf_op jit(solution)/shard_map/ppermute | solution.py:30
  62.0 11.0 %collective-permute-start.11 = (bf16[32,5120]{1,0:T(8,128)(2,1)S(1)}, bf16[32,5120]{1,0:T(8,128)(2,1)S(1)}, u32[]{:S(2)}, u32[]{:S(2)}) collective-permute-start(bf16[32,5120]{1,0:T(8,128)(2,1)S(1)} %get-tuple-element.26), channel_id=1, source_target_pairs={{0,3},{1,0},{2,1},{3,2},{4,7},{5,4},{6,5},{7,6},{8,11},{9,8},{10,9... | collective-permute-start | bytes 983048 | tf_op jit(solution)/shard_map/ppermute | solution.py:26
  64.7 8.4 %collective-permute-start.8 = (bf16[16,5120]{1,0:T(8,128)(2,1)S(1)}, bf16[16,5120]{1,0:T(8,128)(2,1)S(1)}, u32[]{:S(2)}, u32[]{:S(2)}) collective-permute-start(bf16[16,5120]{1,0:T(8,128)(2,1)S(1)} %get-tuple-element.23), channel_id=1, source_target_pairs={{0,3},{1,0},{2,1},{3,2},{4,7},{5,4},{6,5},{7,6},{8,11},{9,8},{10,9... | collective-permute-start | bytes 491528 | tf_op jit(solution)/shard_map/ppermute | solution.py:26
  64.8 9.7 %slice-start.1 = ((s8[5242880]{0:T(1024)(128)(4,1)}), s8[1048576]{0:T(1024)(128)(4,1)S(1)}, s32[]{:S(2)}) async-start(s8[5242880]{0:T(1024)(128)(4,1)} %bitcast.38), calls=%async_computation.1 | async-start | bytes 2097152
  89.2 6.3 %collective-permute-start.13 = (bf16[8,32,5120]{2,1,0:T(8,128)(2,1)S(1)}, bf16[8,32,5120]{2,1,0:T(8,128)(2,1)S(1)}, u32[]{:S(2)}, u32[]{:S(2)}) collective-permute-start(bf16[8,32,5120]{2,1,0:T(8,128)(2,1)S(1)} %get-tuple-element.28), channel_id=1, source_target_pairs={{0,8},{8,0},{16,24},{24,16},{32,40},{40,32},{48,56},{56,48},{64,72... | collective-permute-start | bytes 7864328 | tf_op jit(solution)/shard_map/ppermute | solution.py:34
  95.6 37.5 %copy-start.6 = (f32[4,8,5120]{2,1,0:T(8,128)S(1)}, f32[4,8,5120]{2,1,0:T(8,128)}, u32[]{:S(2)}) copy-start(f32[4,8,5120]{2,1,0:T(8,128)} %param.15) | copy-start | bytes 1966084
  95.6 37.5 %copy-start.7 = (f32[4,8,5120]{2,1,0:T(8,128)S(1)}, f32[4,8,5120]{2,1,0:T(8,128)}, u32[]{:S(2)}) copy-start(f32[4,8,5120]{2,1,0:T(8,128)} %param.13) | copy-start | bytes 1966084
  95.6 37.5 %copy-start.8 = (f32[4,8,5120]{2,1,0:T(8,128)S(1)}, f32[4,8,5120]{2,1,0:T(8,128)}, u32[]{:S(2)}) copy-start(f32[4,8,5120]{2,1,0:T(8,128)} %param.14) | copy-start | bytes 1966084
  96.4 14.4 %collective-permute-start.14 = (bf16[32,5120]{1,0:T(8,128)(2,1)S(1)}, bf16[32,5120]{1,0:T(8,128)(2,1)S(1)}, u32[]{:S(2)}, u32[]{:S(2)}) collective-permute-start(bf16[32,5120]{1,0:T(8,128)(2,1)S(1)} %get-tuple-element.32), channel_id=1, source_target_pairs={{0,80},{8,88},{16,64},{24,72},{32,112},{40,120},{48,96},{56,104},{... | collective-permute-start | bytes 983048 | tf_op jit(solution)/shard_map/ppermute | solution.py:45
  102.9 14.8 %collective-permute-start.15 = (bf16[32,5120]{1,0:T(8,128)(2,1)S(1)}, bf16[32,5120]{1,0:T(8,128)(2,1)S(1)}, u32[]{:S(2)}, u32[]{:S(2)}) collective-permute-start(bf16[32,5120]{1,0:T(8,128)(2,1)S(1)} %get-tuple-element.38), channel_id=1, source_target_pairs={{0,112},{8,120},{16,96},{24,104},{32,16},{40,24},{48,0},{56,8},{64... | collective-permute-start | bytes 983048 | tf_op jit(solution)/shard_map/ppermute | solution.py:45
  103.0 16.5 %collective-permute-start.16 = (bf16[32,5120]{1,0:T(8,128)(2,1)S(1)}, bf16[32,5120]{1,0:T(8,128)(2,1)S(1)}, u32[]{:S(2)}, u32[]{:S(2)}) collective-permute-start(bf16[32,5120]{1,0:T(8,128)(2,1)S(1)} %get-tuple-element.37), channel_id=1, source_target_pairs={{0,32},{8,40},{16,48},{24,56},{32,64},{40,72},{48,80},{56,88},{64,... | collective-permute-start | bytes 983048 | tf_op jit(solution)/shard_map/ppermute | solution.py:45
  103.4 21.7 %collective-permute-start.17 = (bf16[32,5120]{1,0:T(8,128)(2,1)S(1)}, bf16[32,5120]{1,0:T(8,128)(2,1)S(1)}, u32[]{:S(2)}, u32[]{:S(2)}) collective-permute-start(bf16[32,5120]{1,0:T(8,128)(2,1)S(1)} %get-tuple-element.36), channel_id=1, source_target_pairs={{0,96},{8,104},{16,112},{24,120},{32,0},{40,8},{48,16},{56,24},{64... | collective-permute-start | bytes 983048 | tf_op jit(solution)/shard_map/ppermute | solution.py:45
  105.7 26.4 %collective-permute-start.18 = (bf16[32,5120]{1,0:T(8,128)(2,1)S(1)}, bf16[32,5120]{1,0:T(8,128)(2,1)S(1)}, u32[]{:S(2)}, u32[]{:S(2)}) collective-permute-start(bf16[32,5120]{1,0:T(8,128)(2,1)S(1)} %get-tuple-element.35), channel_id=1, source_target_pairs={{0,16},{8,24},{16,0},{24,8},{32,48},{40,56},{48,32},{56,40},{64,80... | collective-permute-start | bytes 983048 | tf_op jit(solution)/shard_map/ppermute | solution.py:45
  110.8 21.3 %collective-permute-start.19 = (bf16[32,5120]{1,0:T(8,128)(2,1)S(1)}, bf16[32,5120]{1,0:T(8,128)(2,1)S(1)}, u32[]{:S(2)}, u32[]{:S(2)}) collective-permute-start(bf16[32,5120]{1,0:T(8,128)(2,1)S(1)} %get-tuple-element.34), channel_id=1, source_target_pairs={{0,48},{8,56},{16,32},{24,40},{32,80},{40,88},{48,64},{56,72},{64,... | collective-permute-start | bytes 983048 | tf_op jit(solution)/shard_map/ppermute | solution.py:45
  117.7 15.4 %collective-permute-start.20 = (bf16[32,5120]{1,0:T(8,128)(2,1)S(1)}, bf16[32,5120]{1,0:T(8,128)(2,1)S(1)}, u32[]{:S(2)}, u32[]{:S(2)}) collective-permute-start(bf16[32,5120]{1,0:T(8,128)(2,1)S(1)} %get-tuple-element.33), channel_id=1, source_target_pairs={{0,64},{8,72},{16,80},{24,88},{32,96},{40,104},{48,112},{56,120},{... | collective-permute-start | bytes 983048 | tf_op jit(solution)/shard_map/ppermute | solution.py:45
  (1 other events, 0.7 us)

commit v5 on v4

--- a/solution.py
+++ b/solution.py
@@ -16,9 +16,9 @@
 RING = 4
 BLOCK = 128
 ROWS_A = 80
-FAR, FAR_A = 64, 48
+FAR = 16
 TILE = 2560
-EARLY_VMEM, LATE_VMEM, RENEW_VMEM, PICK_VMEM = 18, 12, 26, 8
+EARLY_VMEM, LATE_VMEM, RENEW_VMEM, PICK_VMEM, MINE_VMEM = 18, 12, 16, 8, 8
 
 
 def along_x(array, step):
@@ -172,7 +172,7 @@
     count = len(spans)
     place_ref, gain_ref, ids_ref, upstream_ref, weight = refs[:5]
     pieces, refs = refs[5 : 5 + count], refs[5 + count :]
-    _, out_ref, _, tokens, upstream, turned, rotated, sems = refs
+    out_ref, tokens, upstream, turned, rotated, sems = refs
     copies = Copies(sems)
     needed = start_upstream(copies, place_ref, first_block, upstream_ref, upstream)
     ready = start_tokens(copies, pieces, spans, tokens)
@@ -209,8 +209,8 @@
 def renew_kernel(first_block, count, *refs):
     place_ref, gain_ref, ids_ref, upstream_ref, weight, before_ref = refs[:6]
     refs = refs[6:]
-    pieces, (mine_ref, theirs_ref) = refs[:count], refs[count : count + 2]
-    tokens, upstream, turned, rotated, split, factors, sems = refs[count + 2 :]
+    pieces, (theirs_ref, split, factors) = refs[:count], refs[count : count + 3]
+    tokens, upstream, turned, rotated, sems = refs[count + 3 :]
     all_rows, width = weight.shape
     size = gain_ref.shape[1]
     heads = all_rows // size
@@ -243,13 +243,32 @@
         grams.append(
             whole[:size, :size] + whole[:size, size:] + whole[size:, :size] + whole[size:, size:]
         )
+    core_is_zero = place_ref[10] == 0
     for head, factor in enumerate(orthogonal_factors(grams, width)):
-        high, low = halves(factor)
-        factors[head, :size, :size] = high
-        factors[head, :size, size:] = high
-        factors[head, size:, :size] = low
-        factors[head, size:, size:] = jnp.zeros_like(low)
-
+        for which in range(2):
+            high, low = halves(rows_of_core(factor, core_is_zero, which))
+            half = high.shape[0]
+            factors[head, which, :half, :size] = high
+            factors[head, which, :half, size:] = high
+            factors[head, which, half:, :size] = low
+            factors[head, which, half:, size:] = jnp.zeros_like(low)
+    change_rows(place_ref, weight, split, factors, theirs_ref, 1)
+
+
+def rows_of_core(value, core_is_zero, which):
+    rows = []
+    for begin in range(0, value.shape[0], 16):
+        first, second = value[begin : begin + 8], value[begin + 8 : begin + 16]
+        if which:
+            first, second = second, first
+        rows.append(jnp.where(core_is_zero, first, second))
+    return jnp.concatenate(rows, 0)
+
+
+def change_rows(place_ref, weight, split, factors, out_ref, which):
+    all_rows, width = weight.shape
+    heads = split.shape[0]
+    size = all_rows // heads
     core_is_zero = place_ref[10] == 0
     indices = []
     for chip in range(8):
@@ -257,28 +276,24 @@
         step_z = lax.rem(chip % 2 - place_ref[9] + 2, 2)
         indices.append(step_y * 2 + step_z)
 
-    @pl.loop(0, tiles)
+    @pl.loop(0, width // TILE)
     def _(tile):
         columns = pl.ds(pl.multiple_of(tile * TILE, TILE), TILE)
         for pair in range(heads // 2):
             renewed = []
             for head in (2 * pair, 2 * pair + 1):
-                both = contract(factors[head], split[head, :, columns], 1, 0)
-                change = both[:size] + both[size:]
+                both = contract(factors[head, which], split[head, :, columns], 1, 0)
+                change = both[: size // 2] + both[size // 2 :]
                 old = weight[head * size : (head + 1) * size, columns].astype(jnp.float32)
-                renewed.append(old - change)
+                renewed.append(rows_of_core(old, core_is_zero, which) - change)
             span = pl.ds(pair * 16, 16)
             for chip, index in enumerate(indices):
-                parts = []
-                for core in range(2):
-                    begin = (chip * 2 + core) * 8
-                    parts.append(
-                        jnp.concatenate([value[begin : begin + 8] for value in renewed], 0)
-                    )
-                mine = jnp.where(core_is_zero, parts[0], parts[1])
-                theirs = jnp.where(core_is_zero, parts[1], parts[0])
-                mine_ref[index, span, columns] = mine.astype(jnp.bfloat16)
-                theirs_ref[index, span, columns] = theirs.astype(jnp.bfloat16)
+                rows = [value[chip * 8 : chip * 8 + 8] for value in renewed]
+                out_ref[index, span, columns] = jnp.concatenate(rows, 0).astype(jnp.bfloat16)
+
+
+def mine_kernel(place_ref, weight, split, factors, mine_ref):
+    change_rows(place_ref, weight, split, factors, mine_ref, 0)
 
 
 OUTSIDE = pl.BlockSpec(memory_space=pltpu.HBM)
@@ -339,7 +354,7 @@
     wait_all(started)
 
 
-def pick_call(arrays, picks):
+def pick_call(arrays, picks, after=()):
     shapes = []
     for parts in picks:
         rows = sum(part[2] for part in parts)
@@ -349,27 +364,24 @@
     return call(
         functools.partial(pick_kernel, picks, len(arrays)),
         tuple(shapes),
-        [OUTSIDE] * len(arrays),
+        [OUTSIDE] * (len(arrays) + len(after)),
         (INSIDE,) * len(shapes),
         scratch,
         0,
         moved,
         PICK_VMEM,
-        list(map(outside, arrays)),
-    )
-
-
-def early_call(common, first_block, pieces, passed):
+        [*map(outside, arrays), *after],
+    )
+
+
+def early_call(common, first_block, pieces):
     all_rows, width = common[-1].shape
     rows = rows_of(pieces)
     return call(
         functools.partial(early_kernel, first_block, spans_of(pieces)),
-        (
-            jax.ShapeDtypeStruct((all_rows, width), jnp.float32),
-            jax.ShapeDtypeStruct(passed.shape, passed.dtype),
-        ),
-        COMMON_SPECS + [OUTSIDE] * (len(pieces) + 1),
-        (INSIDE, OUTSIDE),
+        jax.ShapeDtypeStruct((all_rows, width), jnp.float32),
+        COMMON_SPECS + [OUTSIDE] * len(pieces),
+        INSIDE,
         [pltpu.VMEM((rows, width), jnp.bfloat16)]
         + scratch_of(common, rows)
         + [
@@ -379,8 +391,7 @@
         4 * rows * all_rows * width,
         (6 * all_rows + 2 * rows) * width,
         EARLY_VMEM,
-        [*common, *arrays_of(pieces), passed],
-        {len(common) + len(pieces): 1},
+        [*common, *arrays_of(pieces)],
     )
 
 
@@ -414,21 +425,38 @@
     shape = jax.ShapeDtypeStruct((8, all_rows // 16, width), jnp.bfloat16)
     return call(
         functools.partial(renew_kernel, first_block, len(pieces)),
-        (shape, shape),
+        (
+            shape,
+            jax.ShapeDtypeStruct((heads, 2 * size, width), jnp.bfloat16),
+            jax.ShapeDtypeStruct((heads, 2, size, 2 * size), jnp.bfloat16),
+        ),
         COMMON_SPECS + [INSIDE] * (1 + len(pieces)),
-        (INSIDE, INSIDE),
+        (INSIDE, INSIDE, INSIDE),
         [pltpu.VMEM((rows, width), jnp.bfloat16)]
         + scratch_of(common, rows)
         + [
             pltpu.VMEM((all_rows, rows), jnp.bfloat16),
-            pltpu.VMEM((heads, 2 * size, width), jnp.bfloat16),
-            pltpu.VMEM((heads, 2 * size, 2 * size), jnp.bfloat16),
             pltpu.SemaphoreType.DMA((rows // BLOCK,)),
         ],
         (4 * rows + 16 * size) * all_rows * width,
         8 * all_rows * width,
         RENEW_VMEM,
         [*common, before, *pieces],
+    )
+
+
+def mine_call(common, split, factors, shape):
+    all_rows, width = common[-1].shape
+    return call(
+        mine_kernel,
+        jax.ShapeDtypeStruct(shape, jnp.bfloat16),
+        [SCALARS, INSIDE, INSIDE, INSIDE],
+        INSIDE,
+        [],
+        4 * all_rows * split.shape[1] * width,
+        4 * all_rows * width,
+        MINE_VMEM,
+        [common[0], common[-1], split, factors],
     )
 
 
@@ -466,30 +494,28 @@
     over_a = across_z(own_a)
     over_left_a, over_right_a = along_x(over_a, 1), along_x(over_a, -1)
     over_b = across_z(own_b)
-    left_far, right_far, right_b, sides_b = pick_call(
+    left_far, right_b, sides_b = pick_call(
         [left, right],
         [
-            [(0, 0, FAR)],
-            [(1, FAR, ROWS_A - FAR)],
+            [(0, 0, ROWS_A)],
             [(1, ROWS_A, rows_b)],
             [(0, ROWS_A, rows_b), (1, ROWS_A, rows_b)],
         ],
     )
     far_b = along_x(right_b, -1)
-    far0 = along_x(left_far, 1)
+    far_a = along_x(left_far, 1)
     over_b2 = across_z(sides_b)
-    before, right_far = early_call(common, 0, [activations, left, right, over_a, over_b], right_far)
-    over_left_far, over_right_far, right_far = pick_call(
-        [over_left_a, over_right_a, right_far],
-        [[(0, 0, FAR_A)], [(1, FAR_A, ROWS_A - FAR_A)], [(2, 0, ROWS_A - FAR)]],
+    before = early_call(common, 0, [activations, left, right, over_a, over_b])
+    over_left_far, over_right_far = pick_call(
+        [over_left_a, over_right_a], [[(0, 0, FAR)], [(1, FAR, ROWS_A - FAR)]], [before]
     )
     over_far0, over_far1 = along_x(over_left_far, 1), along_x(over_right_far, -1)
-    far1 = along_x(right_far, -1)
     over_far_b = across_z(far_b)
     late = [over_left_a, (over_b2, 0, rows_b), over_right_a, (over_b2, rows_b, rows_b)]
     before = late_call(common, 4, before, late)
-    last = [far0, far1, far_b, over_far0, over_far1, over_far_b]
-    mine, theirs = renew_call(common, 6, before, last)
+    last = [far_a, far_b, over_far0, over_far1, over_far_b]
+    theirs, split, factors = renew_call(common, 6, before, last)
+    mine = mine_call(common, split, factors, theirs.shape)
 
     theirs = to_other_core(theirs)
     summed = None

time: 136 us -> 133 us (0.978)
  starting transfers between devices: 35.6 us -> 31.5 us
  local copies, waits for them, and re-layouts: 6 us -> 3.69 us
  waiting for transfers between devices: 54.5 us -> 56.4 us
  Pallas kernels: 35.4 us -> 36.8 us
    ppermute x7, starting transfers between devices: 17.7 us -> 13.7 us  [to_chip(): return lax.ppermute(array, 'rep', pairs)]
    ppermute x7, waiting for transfers between devices: 19 us -> 21.9 us  [to_chip(): return lax.ppermute(array, 'rep', pairs)]
    ppermute x1, waiting for transfers between devices: 4.54 us -> 1.87 us  [to_other_core(): return lax.ppermute(array, 'rep', [(r, r ^ 1) for r in range(16)])]
    unnamed x24 -> x22, local copies, waits for them, and re-layouts: 5.91 us -> 3.6 us
    ppermute x9 -> x8, waiting for transfers between devices: 13.6 us -> 15.1 us  [along_x(): return lax.ppermute(array, 'grp', pairs)]
    pallas_call x6 -> x7, Pallas kernels: 35.4 us -> 36.8 us  [call(): pl.pallas_call(kernel, out_shape=out_shape, in_specs=in_specs, out_specs=...]
    ppermute x9 -> x8, starting transfers between devices: 10.7 us -> 10.8 us  [along_x(): return lax.ppermute(array, 'grp', pairs)]
  transfers between devices with their start and end apart: 21 -> 20, of which waited for: 11 -> 11; matrix products, arithmetic and copies ran while one was open for 0% -> 0% of each run, Pallas kernels for 15% -> 18%
where the time goes in v5:
time: 133 us; the launch traced here: 132 us
  waiting for transfers between devices  56.4 us (42%)
  Pallas kernels  36.8 us (28%)
  starting transfers between devices  31.5 us (24%)
  local copies, waits for them, and re-layouts  3.69 us (3%)
  other arithmetic  2.67 us (2%)
    pallas_call x7, Pallas kernels, call(): pl.pallas_call(kernel, out_shape=out_shape, in_specs=in_specs, out_specs=...  36.8 us
    ppermute x7, waiting for transfers between devices, to_chip(): return lax.ppermute(array, 'rep', pairs)  21.9 us
    ppermute x4, waiting for transfers between devices, across_z(): lax.ppermute(array, 'grp', [(g, (g + RING) % (2 * RING)) for g in range(2...  17.6 us
    ppermute x8, waiting for transfers between devices, along_x(): return lax.ppermute(array, 'grp', pairs)  15.1 us
    ppermute x7, starting transfers between devices, to_chip(): return lax.ppermute(array, 'rep', pairs)  13.7 us
    ppermute x8, starting transfers between devices, along_x(): return lax.ppermute(array, 'grp', pairs)  10.8 us
    ppermute x4, starting transfers between devices, across_z(): lax.ppermute(array, 'grp', [(g, (g + RING) % (2 * RING)) for g in range(2...  5.16 us
    unnamed x22, local copies, waits for them, and re-layouts  3.6 us
  transfers between devices with their start and end apart: 20, of which 11 were waited for; matrix products, arithmetic and copies ran while one was open for 0% of the time, Pallas kernels for 18%

profile of v5, /device:TPU:1, one launch (start us, length us, event | category | flops | bytes accessed | tf_op | source)
XLA Modules:
  0.0 131.9 jit_solution(13476517804622784871)
XLA Ops:
  0.7 3.4 %collective-permute-start.1 = (bf16[128,5120]{1,0:T(8,128)(2,1)}, bf16[128,5120]{1,0:T(8,128)(2,1)S(1)}, u32[]{:S(2)}, u32[]{:S(2)}) collective-permute-start(bf16[128,5120]{1,0:T(8,128)(2,1)} %refs_5_.1), channel_id=1, source_target_pairs={{0,3},{1,0},{2,1},{3,2},{4,7},{5,4},{6,5},{7,6},{8,11},{9,8},{10,9... | collective-permute-start | bytes 3932168 | tf_op jit(solution)/shard_map/ppermute | solution.py:26
  4.0 1.3 shard_map.103
  5.3 1.7 %collective-permute-start.2 = (bf16[80,5120]{1,0:T(8,128)(2,1)S(1)}, bf16[80,5120]{1,0:T(8,128)(2,1)}, u32[]{:S(2)}, u32[]{:S(2)}) collective-permute-start(bf16[80,5120]{1,0:T(8,128)(2,1)S(1)} %get-tuple-element.13), channel_id=1, source_target_pairs={{0,4},{1,5},{2,6},{3,7},{4,0},{5,1},{6,2},{7,3},{8,12},{9,13},{10,... | collective-permute-start | bytes 2457608 | tf_op jit(solution)/shard_map/ppermute | solution.py:30
  7.1 17.5 %collective-permute-done.2.refs_8_ = bf16[80,5120]{1,0:T(8,128)(2,1)} collective-permute-done((bf16[80,5120]{1,0:T(8,128)(2,1)S(1)}, bf16[80,5120]{1,0:T(8,128)(2,1)}, u32[]{:S(2)}, u32[]{:S(2)}) %collective-permute-start.2) | collective-permute-done | bytes 819232 | tf_op jit(solution)/shard_map/ppermute | solution.py:30
  24.7 2.4 %collective-permute-start.6 = (bf16[80,5120]{1,0:T(8,128)(2,1)}, bf16[80,5120]{1,0:T(8,128)(2,1)}, u32[]{:S(2)}, u32[]{:S(2)}) collective-permute-start(bf16[80,5120]{1,0:T(8,128)(2,1)} %collective-permute-done.2.refs_8_), channel_id=1, source_target_pairs={{0,3},{1,0},{2,1},{3,2},{4,7},{5,4},{6,5},{7,6},{8,11},{9,8},{10,9... | collective-permute-start | bytes 2457608 | tf_op jit(solution)/shard_map/ppermute | solution.py:26
  27.1 4.7 %collective-permute-done.1.refs_7_.refs_1_ = bf16[128,5120]{1,0:T(8,128)(2,1)S(1)} collective-permute-done((bf16[128,5120]{1,0:T(8,128)(2,1)}, bf16[128,5120]{1,0:T(8,128)(2,1)S(1)}, u32[]{:S(2)}, u32[]{:S(2)}) %collective-permute-start.1) | collective-permute-done | bytes 1310752 | tf_op jit(solution)/shard_map/ppermute | solution.py:26
  31.8 3.0 %collective-permute-done.refs_6_.refs_0_ = bf16[128,5120]{1,0:T(8,128)(2,1)S(1)} collective-permute-done((bf16[128,5120]{1,0:T(8,128)(2,1)}, bf16[128,5120]{1,0:T(8,128)(2,1)S(1)}, u32[]{:S(2)}, u32[]{:S(2)}) %collective-permute-start) | collective-permute-done | bytes 1310752 | tf_op jit(solution)/shard_map/ppermute | solution.py:26
  34.8 1.1 copy-done.5
  35.9 1.7 %shard_map.105 = (bf16[80,5120]{1,0:T(8,128)(2,1)S(1)}, bf16[48,5120]{1,0:T(8,128)(2,1)S(1)}, bf16[96,5120]{1,0:T(8,128)(2,1)S(1)}) custom-call(bf16[128,5120]{1,0:T(8,128)(2,1)} %copy-done.5, bf16[128,5120]{1,0:T(8,128)(2,1)} %copy-done.4), custom_call_target="tpu_custom_call" | custom-call | bytes 4587520 | tf_op jit(solution)/shard_map/pallas_call | solution.py:309
  37.6 1.7 %collective-permute-start.5 = (bf16[96,5120]{1,0:T(8,128)(2,1)S(1)}, bf16[96,5120]{1,0:T(8,128)(2,1)}, u32[]{:S(2)}, u32[]{:S(2)}) collective-permute-start(bf16[96,5120]{1,0:T(8,128)(2,1)S(1)} %get-tuple-element.15), channel_id=1, source_target_pairs={{0,4},{1,5},{2,6},{3,7},{4,0},{5,1},{6,2},{7,3},{8,12},{9,13},{10,... | collective-permute-start | bytes 2949128 | tf_op jit(solution)/shard_map/ppermute | solution.py:30
  39.4 1.4 %collective-permute-start.8 = (bf16[48,5120]{1,0:T(8,128)(2,1)}, bf16[48,5120]{1,0:T(8,128)(2,1)S(1)}, u32[]{:S(2)}, u32[]{:S(2)}) collective-permute-start(bf16[48,5120]{1,0:T(8,128)(2,1)} %copy-done.3), channel_id=1, source_target_pairs={{0,3},{1,0},{2,1},{3,2},{4,7},{5,4},{6,5},{7,6},{8,11},{9,8},{10,9... | collective-permute-start | bytes 1474568 | tf_op jit(solution)/shard_map/ppermute | solution.py:26
  40.9 2.5 %copy-done = bf16[1,4,128,5120]{3,2,1,0:T(8,128)(2,1)S(1)} copy-done((bf16[1,4,128,5120]{3,2,1,0:T(8,128)(2,1)S(1)}, bf16[1,4,128,5120]{3,2,1,0:T(8,128)(2,1)}, u32[]{:S(2)}) %copy-start) | copy-done | bytes 5242904
  43.4 9.9 %shard_map.104.refs_5_.refs_2_ = f32[512,5120]{1,0:T(8,128)S(1)} custom-call(s32[11]{0:T(128)S(1)} %stack.47.refs_0_.place_ref, f32[1,128]{1,0:T(1,128)S(1)} %bitcast.45, s32[8,128]{1,0:T(8,128)S(1)} %bitcast.42, bf16[1024,512]{1,0:T(8,128)(2,1)} %refs_3_.5, bf16[512,5120]{1,0:T(8,128)(2,1)S(1)} %bitcast.36, bf16[128,5120]{1,0:T(8,128)(2,1)} %refs_5_.1, ...), custom_call_target="tpu_custom_call" | custom-call | flops 5368709120 | bytes 20971520 | tf_op jit(solution)/shard_map/pallas_call | solution.py:309
  53.3 1.2 shard_map.107
  54.5 2.7 %collective-permute-start.10 = (bf16[64,5120]{1,0:T(8,128)(2,1)S(1)}, bf16[64,5120]{1,0:T(8,128)(2,1)S(1)}, u32[]{:S(2)}, u32[]{:S(2)}) collective-permute-start(bf16[64,5120]{1,0:T(8,128)(2,1)S(1)} %get-tuple-element.19), channel_id=1, source_target_pairs={{0,3},{1,0},{2,1},{3,2},{4,7},{5,4},{6,5},{7,6},{8,11},{9,8},{10,9... | collective-permute-start | bytes 1966088 | tf_op jit(solution)/shard_map/ppermute | solution.py:26
  57.2 2.7 %collective-permute-done.8.refs_7_ = bf16[48,5120]{1,0:T(8,128)(2,1)S(1)} collective-permute-done((bf16[48,5120]{1,0:T(8,128)(2,1)}, bf16[48,5120]{1,0:T(8,128)(2,1)S(1)}, u32[]{:S(2)}, u32[]{:S(2)}) %collective-permute-start.8) | collective-permute-done | bytes 491552 | tf_op jit(solution)/shard_map/ppermute | solution.py:26
  59.9 1.6 %collective-permute-start.11 = (bf16[48,5120]{1,0:T(8,128)(2,1)S(1)}, bf16[48,5120]{1,0:T(8,128)(2,1)S(1)}, u32[]{:S(2)}, u32[]{:S(2)}) collective-permute-start(bf16[48,5120]{1,0:T(8,128)(2,1)S(1)} %collective-permute-done.8.refs_7_), channel_id=1, source_target_pairs={{0,4},{1,5},{2,6},{3,7},{4,0},{5,1},{6,2},{7,3},{8,12},{9,13},{10,... | collective-permute-start | bytes 1474568 | tf_op jit(solution)/shard_map/ppermute | solution.py:30
  62.4 6.7 %shard_map.106.refs_5_ = f32[512,5120]{1,0:T(8,128)S(1)} custom-call(s32[11]{0:T(128)S(1)} %stack.47.refs_0_.place_ref, f32[1,128]{1,0:T(1,128)S(1)} %bitcast.46, s32[8,128]{1,0:T(8,128)S(1)} %bitcast.43, bf16[1024,512]{1,0:T(8,128)(2,1)} %refs_3_.5, bf16[512,5120]{1,0:T(8,128)(2,1)S(1)} %bitcast.39, ...), custom_call_target="tpu_custom_call", output_to_operand_aliasing={{}: (5, {})} | custom-call | flops 2684354560 | bytes 7864320 | tf_op jit(solution)/shard_map/pallas_call | solution.py:309
  69.2 4.2 %collective-permute-done.9.refs_8_ = bf16[16,5120]{1,0:T(8,128)(2,1)S(1)} collective-permute-done((bf16[16,5120]{1,0:T(8,128)(2,1)S(1)}, bf16[16,5120]{1,0:T(8,128)(2,1)S(1)}, u32[]{:S(2)}, u32[]{:S(2)}) %collective-permute-start.9) | collective-permute-done | bytes 163872 | tf_op jit(solution)/shard_map/ppermute | solution.py:26
  73.8 13.3 %shard_map.108 = (bf16[8,32,5120]{2,1,0:T(8,128)(2,1)S(1)}, bf16[4,256,5120]{2,1,0:T(8,128)(2,1)S(1)}, bf16[4,2,128,256]{3,2,1,0:T(8,128)(2,1)S(1)}) custom-call(s32[11]{0:T(128)S(1)} %stack.47.refs_0_.place_ref, f32[1,128]{1,0:T(1,128)S(1)} %bitcast.47, s32[8,128]{1,0:T(8,128)S(1)} %bitcast.44, bf16[1024,512]{1,0:T(8,128)(2,1)} %refs_3_.5, ...), custom_call_target="tpu_custom_call" | custom-call | flops 8053063680 | bytes 20971520 | tf_op jit(solution)/shard_map/pallas_call | solution.py:309
  87.2 1.8 %collective-permute-start.12 = (bf16[8,32,5120]{2,1,0:T(8,128)(2,1)S(1)}, bf16[8,32,5120]{2,1,0:T(8,128)(2,1)S(1)}, u32[]{:S(2)}, u32[]{:S(2)}) collective-permute-start(bf16[8,32,5120]{2,1,0:T(8,128)(2,1)S(1)} %get-tuple-element.22), channel_id=1, source_target_pairs={{0,8},{8,0},{16,24},{24,16},{32,40},{40,32},{48,56},{56,48},{64,72... | collective-permute-start | bytes 7864328 | tf_op jit(solution)/shard_map/ppermute | solution.py:34
  89.0 2.6 %shard_map.109 = bf16[8,32,5120]{2,1,0:T(8,128)(2,1)S(1)} custom-call(s32[11]{0:T(128)S(1)} %stack.47.refs_0_.place_ref, bf16[512,5120]{1,0:T(8,128)(2,1)S(1)} %bitcast.41, bf16[4,256,5120]{2,1,0:T(8,128)(2,1)S(1)} %get-tuple-element.20.split, bf16[4,2,128,256]{3,2,1,0:T(8,128)(2,1)S(1)} %get-tuple-element.21.factors), custom_call_target="tpu_custom_call" | custom-call | flops 2684354560 | bytes 10485760 | tf_op jit(solution)/shard_map/pallas_call | solution.py:309
  91.7 1.9 %collective-permute-done.12 = bf16[8,32,5120]{2,1,0:T(8,128)(2,1)S(1)} collective-permute-done((bf16[8,32,5120]{2,1,0:T(8,128)(2,1)S(1)}, bf16[8,32,5120]{2,1,0:T(8,128)(2,1)S(1)}, u32[]{:S(2)}, u32[]{:S(2)}) %collective-permute-start.12) | collective-permute-done | bytes 2621472 | tf_op jit(solution)/shard_map/ppermute | solution.py:34
  94.4 6.3 %collective-permute-start.13 = (bf16[32,5120]{1,0:T(8,128)(2,1)S(1)}, bf16[32,5120]{1,0:T(8,128)(2,1)S(1)}, u32[]{:S(2)}, u32[]{:S(2)}) collective-permute-start(bf16[32,5120]{1,0:T(8,128)(2,1)S(1)} %get-tuple-element.26), channel_id=1, source_target_pairs={{0,80},{8,88},{16,64},{24,72},{32,112},{40,120},{48,96},{56,104},{... | collective-permute-start | bytes 983048 | tf_op jit(solution)/shard_map/ppermute | solution.py:45
  101.2 3.5 %collective-permute-start.17 = (bf16[32,5120]{1,0:T(8,128)(2,1)S(1)}, bf16[32,5120]{1,0:T(8,128)(2,1)S(1)}, u32[]{:S(2)}, u32[]{:S(2)}) collective-permute-start(bf16[32,5120]{1,0:T(8,128)(2,1)S(1)} %get-tuple-element.29), channel_id=1, source_target_pairs={{0,16},{8,24},{16,0},{24,8},{32,48},{40,56},{48,32},{56,40},{64,80... | collective-permute-start | bytes 983048 | tf_op jit(solution)/shard_map/ppermute | solution.py:45
  104.8 1.4 %collective-permute-start.16 = (bf16[32,5120]{1,0:T(8,128)(2,1)S(1)}, bf16[32,5120]{1,0:T(8,128)(2,1)S(1)}, u32[]{:S(2)}, u32[]{:S(2)}) collective-permute-start(bf16[32,5120]{1,0:T(8,128)(2,1)S(1)} %get-tuple-element.30), channel_id=1, source_target_pairs={{0,96},{8,104},{16,112},{24,120},{32,0},{40,8},{48,16},{56,24},{64... | collective-permute-start | bytes 983048 | tf_op jit(solution)/shard_map/ppermute | solution.py:45
  106.2 2.4 %collective-permute-done.13 = bf16[32,5120]{1,0:T(8,128)(2,1)S(1)} collective-permute-done((bf16[32,5120]{1,0:T(8,128)(2,1)S(1)}, bf16[32,5120]{1,0:T(8,128)(2,1)S(1)}, u32[]{:S(2)}, u32[]{:S(2)}) %collective-permute-start.13) | collective-permute-done | bytes 327712 | tf_op jit(solution)/shard_map/ppermute | solution.py:45
  108.7 6.7 %collective-permute-done.19 = bf16[32,5120]{1,0:T(8,128)(2,1)S(1)} collective-permute-done((bf16[32,5120]{1,0:T(8,128)(2,1)S(1)}, bf16[32,5120]{1,0:T(8,128)(2,1)S(1)}, u32[]{:S(2)}, u32[]{:S(2)}) %collective-permute-start.19) | collective-permute-done | bytes 327712 | tf_op jit(solution)/shard_map/ppermute | solution.py:45
  115.3 1.8 %collective-permute-start.14 = (bf16[32,5120]{1,0:T(8,128)(2,1)S(1)}, bf16[32,5120]{1,0:T(8,128)(2,1)S(1)}, u32[]{:S(2)}, u32[]{:S(2)}) collective-permute-start(bf16[32,5120]{1,0:T(8,128)(2,1)S(1)} %get-tuple-element.32), channel_id=1, source_target_pairs={{0,112},{8,120},{16,96},{24,104},{32,16},{40,24},{48,0},{56,8},{64... | collective-permute-start | bytes 983048 | tf_op jit(solution)/shard_map/ppermute | solution.py:45
  117.1 6.1 %collective-permute-done.18 = bf16[32,5120]{1,0:T(8,128)(2,1)S(1)} collective-permute-done((bf16[32,5120]{1,0:T(8,128)(2,1)S(1)}, bf16[32,5120]{1,0:T(8,128)(2,1)S(1)}, u32[]{:S(2)}, u32[]{:S(2)}) %collective-permute-start.18) | collective-permute-done | bytes 327712 | tf_op jit(solution)/shard_map/ppermute | solution.py:45
  123.2 6.8 %collective-permute-done.15 = bf16[32,5120]{1,0:T(8,128)(2,1)S(1)} collective-permute-done((bf16[32,5120]{1,0:T(8,128)(2,1)S(1)}, bf16[32,5120]{1,0:T(8,128)(2,1)S(1)}, u32[]{:S(2)}, u32[]{:S(2)}) %collective-permute-start.15) | collective-permute-done | bytes 327712 | tf_op jit(solution)/shard_map/ppermute | solution.py:45
  130.0 1.8 %multiply_add_fusion = (f32[4,8,5120]{2,1,0:T(8,128)}, f32[4,8,5120]{2,1,0:T(8,128)}, f32[4,8,5120]{2,1,0:T(8,128)}) fusion(f32[4,8,5120]{2,1,0:T(8,128)S(1)} %copy-done.6, f32[4,8,5120]{2,1,0:T(8,128)S(1)} %copy-done.7, f32[4,8,5120]{2,1,0:T(8,128)S(1)} %copy-done.8, bf16[8,32,5120]{2,1,0:T(8,128)(2,1)S(1)} %collective-permute-done.12, ...), kind=kLoop, calls=%fused_computation.3 | loop fusion | flops 4587520 | bytes 6881280 | tf_op jit(solution)/shard_map/add | solution.py:534
  (41 shorter events, 3.1 us)
Async XLA Ops:
  0.6 40.3 %copy-start.2 = (f32[128]{0:T(128)S(1)}, f32[128]{0:T(128)}, u32[]{:S(2)}) copy-start(f32[128]{0:T(128)} %param.12) | copy-start | bytes 1540
  0.6 40.3 %copy-start.1 = (s32[1024]{0:T(1024)S(1)}, s32[1024]{0:T(1024)}, u32[]{:S(2)}) copy-start(s32[1024]{0:T(1024)} %param.9) | copy-start | bytes 12292
  0.7 31.1 %collective-permute-start.1 = (bf16[128,5120]{1,0:T(8,128)(2,1)}, bf16[128,5120]{1,0:T(8,128)(2,1)S(1)}, u32[]{:S(2)}, u32[]{:S(2)}) collective-permute-start(bf16[128,5120]{1,0:T(8,128)(2,1)} %refs_5_.1), channel_id=1, source_target_pairs={{0,3},{1,0},{2,1},{3,2},{4,7},{5,4},{6,5},{7,6},{8,11},{9,8},{10,9... | collective-permute-start | bytes 3932168 | tf_op jit(solution)/shard_map/ppermute | solution.py:26
  4.0 30.7 %collective-permute-start = (bf16[128,5120]{1,0:T(8,128)(2,1)}, bf16[128,5120]{1,0:T(8,128)(2,1)S(1)}, u32[]{:S(2)}, u32[]{:S(2)}) collective-permute-start(bf16[128,5120]{1,0:T(8,128)(2,1)} %refs_5_.1), channel_id=1, source_target_pairs={{0,1},{1,2},{2,3},{3,0},{4,5},{5,6},{6,7},{7,4},{8,9},{9,10},{10,1... | collective-permute-start | bytes 3932168 | tf_op jit(solution)/shard_map/ppermute | solution.py:26
  5.3 19.4 %collective-permute-start.2 = (bf16[80,5120]{1,0:T(8,128)(2,1)S(1)}, bf16[80,5120]{1,0:T(8,128)(2,1)}, u32[]{:S(2)}, u32[]{:S(2)}) collective-permute-start(bf16[80,5120]{1,0:T(8,128)(2,1)S(1)} %get-tuple-element.13), channel_id=1, source_target_pairs={{0,4},{1,5},{2,6},{3,7},{4,0},{5,1},{6,2},{7,3},{8,12},{9,13},{10,... | collective-permute-start | bytes 2457608 | tf_op jit(solution)/shard_map/ppermute | solution.py:30
  7.0 33.8 %collective-permute-start.3 = (bf16[48,5120]{1,0:T(8,128)(2,1)S(1)}, bf16[48,5120]{1,0:T(8,128)(2,1)}, u32[]{:S(2)}, u32[]{:S(2)}) collective-permute-start(bf16[48,5120]{1,0:T(8,128)(2,1)S(1)} %get-tuple-element.14), channel_id=1, source_target_pairs={{0,4},{1,5},{2,6},{3,7},{4,0},{5,1},{6,2},{7,3},{8,12},{9,13},{10,... | collective-permute-start | bytes 1474568 | tf_op jit(solution)/shard_map/ppermute | solution.py:30
  24.7 28.6 %collective-permute-start.6 = (bf16[80,5120]{1,0:T(8,128)(2,1)}, bf16[80,5120]{1,0:T(8,128)(2,1)}, u32[]{:S(2)}, u32[]{:S(2)}) collective-permute-start(bf16[80,5120]{1,0:T(8,128)(2,1)} %collective-permute-done.2.refs_8_), channel_id=1, source_target_pairs={{0,3},{1,0},{2,1},{3,2},{4,7},{5,4},{6,5},{7,6},{8,11},{9,8},{10,9... | collective-permute-start | bytes 2457608 | tf_op jit(solution)/shard_map/ppermute | solution.py:26
  27.0 26.2 %collective-permute-start.4 = (bf16[80,5120]{1,0:T(8,128)(2,1)}, bf16[80,5120]{1,0:T(8,128)(2,1)}, u32[]{:S(2)}, u32[]{:S(2)}) collective-permute-start(bf16[80,5120]{1,0:T(8,128)(2,1)} %collective-permute-done.2.refs_8_), channel_id=1, source_target_pairs={{0,1},{1,2},{2,3},{3,0},{4,5},{5,6},{6,7},{7,4},{8,9},{9,10},{10,1... | collective-permute-start | bytes 2457608 | tf_op jit(solution)/shard_map/ppermute | solution.py:26
  31.8 3.0 %copy-start.4 = (bf16[128,5120]{1,0:T(8,128)(2,1)}, bf16[128,5120]{1,0:T(8,128)(2,1)S(1)}, u32[]{:S(2)}) copy-start(bf16[128,5120]{1,0:T(8,128)(2,1)S(1)} %collective-permute-done.1.refs_7_.refs_1_) | copy-start | bytes 3932164
  34.8 1.1 copy-start.5
  35.8 26.6 %slice-start = ((s8[5242880]{0:T(1024)(128)(4,1)}), s8[1048576]{0:T(1024)(128)(4,1)S(1)}, s32[]{:S(2)}) async-start(s8[5242880]{0:T(1024)(128)(4,1)} %bitcast.37), calls=%async_computation | async-start | bytes 2097152
  37.6 1.7 %copy-start.3 = (bf16[48,5120]{1,0:T(8,128)(2,1)}, bf16[48,5120]{1,0:T(8,128)(2,1)S(1)}, u32[]{:S(2)}) copy-start(bf16[48,5120]{1,0:T(8,128)(2,1)S(1)} %get-tuple-element.17) | copy-start | bytes 1474564
  37.6 24.9 %collective-permute-start.5 = (bf16[96,5120]{1,0:T(8,128)(2,1)S(1)}, bf16[96,5120]{1,0:T(8,128)(2,1)}, u32[]{:S(2)}, u32[]{:S(2)}) collective-permute-start(bf16[96,5120]{1,0:T(8,128)(2,1)S(1)} %get-tuple-element.15), channel_id=1, source_target_pairs={{0,4},{1,5},{2,6},{3,7},{4,0},{5,1},{6,2},{7,3},{8,12},{9,13},{10,... | collective-permute-start | bytes 2949128 | tf_op jit(solution)/shard_map/ppermute | solution.py:30
  39.4 20.5 %collective-permute-start.8 = (bf16[48,5120]{1,0:T(8,128)(2,1)}, bf16[48,5120]{1,0:T(8,128)(2,1)S(1)}, u32[]{:S(2)}, u32[]{:S(2)}) collective-permute-start(bf16[48,5120]{1,0:T(8,128)(2,1)} %copy-done.3), channel_id=1, source_target_pairs={{0,3},{1,0},{2,1},{3,2},{4,7},{5,4},{6,5},{7,6},{8,11},{9,8},{10,9... | collective-permute-start | bytes 1474568 | tf_op jit(solution)/shard_map/ppermute | solution.py:26
  40.8 32.6 %collective-permute-start.7 = (bf16[80,5120]{1,0:T(8,128)(2,1)S(1)}, bf16[80,5120]{1,0:T(8,128)(2,1)S(1)}, u32[]{:S(2)}, u32[]{:S(2)}) collective-permute-start(bf16[80,5120]{1,0:T(8,128)(2,1)S(1)} %get-tuple-element.16), channel_id=1, source_target_pairs={{0,1},{1,2},{2,3},{3,0},{4,5},{5,6},{6,7},{7,4},{8,9},{9,10},{10,1... | collective-permute-start | bytes 2457608 | tf_op jit(solution)/shard_map/ppermute | solution.py:26
  40.9 2.5 %copy-start = (bf16[1,4,128,5120]{3,2,1,0:T(8,128)(2,1)S(1)}, bf16[1,4,128,5120]{3,2,1,0:T(8,128)(2,1)}, u32[]{:S(2)}) copy-start(bf16[1,4,128,5120]{3,2,1,0:T(8,128)(2,1)} %param.11) | copy-start | bytes 15728644
  43.4 19.0 %slice-start.1 = ((s8[5242880]{0:T(1024)(128)(4,1)}), s8[4194304]{0:T(1024)(128)(4,1)S(1)}, s32[]{:S(2)}) async-start(s8[5242880]{0:T(1024)(128)(4,1)} %bitcast.37), calls=%async_computation.1 | async-start | bytes 8388608
  54.5 19.3 %collective-permute-start.10 = (bf16[64,5120]{1,0:T(8,128)(2,1)S(1)}, bf16[64,5120]{1,0:T(8,128)(2,1)S(1)}, u32[]{:S(2)}, u32[]{:S(2)}) collective-permute-start(bf16[64,5120]{1,0:T(8,128)(2,1)S(1)} %get-tuple-element.19), channel_id=1, source_target_pairs={{0,3},{1,0},{2,1},{3,2},{4,7},{5,4},{6,5},{7,6},{8,11},{9,8},{10,9... | collective-permute-start | bytes 1966088 | tf_op jit(solution)/shard_map/ppermute | solution.py:26
  59.9 13.9 %collective-permute-start.11 = (bf16[48,5120]{1,0:T(8,128)(2,1)S(1)}, bf16[48,5120]{1,0:T(8,128)(2,1)S(1)}, u32[]{:S(2)}, u32[]{:S(2)}) collective-permute-start(bf16[48,5120]{1,0:T(8,128)(2,1)S(1)} %collective-permute-done.8.refs_7_), channel_id=1, source_target_pairs={{0,4},{1,5},{2,6},{3,7},{4,0},{5,1},{6,2},{7,3},{8,12},{9,13},{10,... | collective-permute-start | bytes 1474568 | tf_op jit(solution)/shard_map/ppermute | solution.py:30
  61.5 11.9 %collective-permute-start.9 = (bf16[16,5120]{1,0:T(8,128)(2,1)S(1)}, bf16[16,5120]{1,0:T(8,128)(2,1)S(1)}, u32[]{:S(2)}, u32[]{:S(2)}) collective-permute-start(bf16[16,5120]{1,0:T(8,128)(2,1)S(1)} %get-tuple-element.18), channel_id=1, source_target_pairs={{0,1},{1,2},{2,3},{3,0},{4,5},{5,6},{6,7},{7,4},{8,9},{9,10},{10,1... | collective-permute-start | bytes 491528 | tf_op jit(solution)/shard_map/ppermute | solution.py:26
  87.2 6.4 %collective-permute-start.12 = (bf16[8,32,5120]{2,1,0:T(8,128)(2,1)S(1)}, bf16[8,32,5120]{2,1,0:T(8,128)(2,1)S(1)}, u32[]{:S(2)}, u32[]{:S(2)}) collective-permute-start(bf16[8,32,5120]{2,1,0:T(8,128)(2,1)S(1)} %get-tuple-element.22), channel_id=1, source_target_pairs={{0,8},{8,0},{16,24},{24,16},{32,40},{40,32},{48,56},{56,48},{64,72... | collective-permute-start | bytes 7864328 | tf_op jit(solution)/shard_map/ppermute | solution.py:34
  91.7 38.4 %copy-start.6 = (f32[4,8,5120]{2,1,0:T(8,128)S(1)}, f32[4,8,5120]{2,1,0:T(8,128)}, u32[]{:S(2)}) copy-start(f32[4,8,5120]{2,1,0:T(8,128)} %param.15) | copy-start | bytes 1966084
  91.7 38.4 %copy-start.7 = (f32[4,8,5120]{2,1,0:T(8,128)S(1)}, f32[4,8,5120]{2,1,0:T(8,128)}, u32[]{:S(2)}) copy-start(f32[4,8,5120]{2,1,0:T(8,128)} %param.13) | copy-start | bytes 1966084
  91.7 38.4 %copy-start.8 = (f32[4,8,5120]{2,1,0:T(8,128)S(1)}, f32[4,8,5120]{2,1,0:T(8,128)}, u32[]{:S(2)}) copy-start(f32[4,8,5120]{2,1,0:T(8,128)} %param.14) | copy-start | bytes 1966084
  94.4 14.1 %collective-permute-start.13 = (bf16[32,5120]{1,0:T(8,128)(2,1)S(1)}, bf16[32,5120]{1,0:T(8,128)(2,1)S(1)}, u32[]{:S(2)}, u32[]{:S(2)}) collective-permute-start(bf16[32,5120]{1,0:T(8,128)(2,1)S(1)} %get-tuple-element.26), channel_id=1, source_target_pairs={{0,80},{8,88},{16,64},{24,72},{32,112},{40,120},{48,96},{56,104},{... | collective-permute-start | bytes 983048 | tf_op jit(solution)/shard_map/ppermute | solution.py:45
  100.7 14.6 %collective-permute-start.19 = (bf16[32,5120]{1,0:T(8,128)(2,1)S(1)}, bf16[32,5120]{1,0:T(8,128)(2,1)S(1)}, u32[]{:S(2)}, u32[]{:S(2)}) collective-permute-start(bf16[32,5120]{1,0:T(8,128)(2,1)S(1)} %get-tuple-element.27), channel_id=1, source_target_pairs={{0,64},{8,72},{16,80},{24,88},{32,96},{40,104},{48,112},{56,120},{... | collective-permute-start | bytes 983048 | tf_op jit(solution)/shard_map/ppermute | solution.py:45
  100.8 22.5 %collective-permute-start.18 = (bf16[32,5120]{1,0:T(8,128)(2,1)S(1)}, bf16[32,5120]{1,0:T(8,128)(2,1)S(1)}, u32[]{:S(2)}, u32[]{:S(2)}) collective-permute-start(bf16[32,5120]{1,0:T(8,128)(2,1)S(1)} %get-tuple-element.28), channel_id=1, source_target_pairs={{0,48},{8,56},{16,32},{24,40},{32,80},{40,88},{48,64},{56,72},{64,... | collective-permute-start | bytes 983048 | tf_op jit(solution)/shard_map/ppermute | solution.py:45
  101.2 22.0 %collective-permute-start.17 = (bf16[32,5120]{1,0:T(8,128)(2,1)S(1)}, bf16[32,5120]{1,0:T(8,128)(2,1)S(1)}, u32[]{:S(2)}, u32[]{:S(2)}) collective-permute-start(bf16[32,5120]{1,0:T(8,128)(2,1)S(1)} %get-tuple-element.29), channel_id=1, source_target_pairs={{0,16},{8,24},{16,0},{24,8},{32,48},{40,56},{48,32},{56,40},{64,80... | collective-permute-start | bytes 983048 | tf_op jit(solution)/shard_map/ppermute | solution.py:45
  104.8 18.5 %collective-permute-start.16 = (bf16[32,5120]{1,0:T(8,128)(2,1)S(1)}, bf16[32,5120]{1,0:T(8,128)(2,1)S(1)}, u32[]{:S(2)}, u32[]{:S(2)}) collective-permute-start(bf16[32,5120]{1,0:T(8,128)(2,1)S(1)} %get-tuple-element.30), channel_id=1, source_target_pairs={{0,96},{8,104},{16,112},{24,120},{32,0},{40,8},{48,16},{56,24},{64... | collective-permute-start | bytes 983048 | tf_op jit(solution)/shard_map/ppermute | solution.py:45
  108.5 21.5 %collective-permute-start.15 = (bf16[32,5120]{1,0:T(8,128)(2,1)S(1)}, bf16[32,5120]{1,0:T(8,128)(2,1)S(1)}, u32[]{:S(2)}, u32[]{:S(2)}) collective-permute-start(bf16[32,5120]{1,0:T(8,128)(2,1)S(1)} %get-tuple-element.31), channel_id=1, source_target_pairs={{0,32},{8,40},{16,48},{24,56},{32,64},{40,72},{48,80},{56,88},{64,... | collective-permute-start | bytes 983048 | tf_op jit(solution)/shard_map/ppermute | solution.py:45
  115.3 14.7 %collective-permute-start.14 = (bf16[32,5120]{1,0:T(8,128)(2,1)S(1)}, bf16[32,5120]{1,0:T(8,128)(2,1)S(1)}, u32[]{:S(2)}, u32[]{:S(2)}) collective-permute-start(bf16[32,5120]{1,0:T(8,128)(2,1)S(1)} %get-tuple-element.32), channel_id=1, source_target_pairs={{0,112},{8,120},{16,96},{24,104},{32,16},{40,24},{48,0},{56,8},{64... | collective-permute-start | bytes 983048 | tf_op jit(solution)/shard_map/ppermute | solution.py:45

commit v6 on v5

--- a/solution.py
+++ b/solution.py
@@ -59,10 +59,12 @@
 def product(left, right):
     high, low = left
     right_high, right_low = right
-    wide = contract(
-        jnp.concatenate([high, low], 1), jnp.concatenate([right_high, right_high], 0), 1, 0
-    )
-    return wide + contract(high, right_low, 1, 0)
+    return contract(
+        jnp.concatenate([high, low, high], 1),
+        jnp.concatenate([right_high, right_high, right_low], 0),
+        1,
+        0,
+    )
 
 
 def orthogonal_factors(grams, width):

time: 133 us -> 132 us (level)
  no operation moved by 1% of the time
where the time goes in v6:
time: 132 us
  waiting for transfers between devices  56.4 us (43%)
  Pallas kernels  36.5 us (28%)
  starting transfers between devices  31.5 us (24%)
  local copies, waits for them, and re-layouts  3.69 us (3%)
  other arithmetic  2.67 us (2%)
    pallas_call x7, Pallas kernels, call(): pl.pallas_call(kernel, out_shape=out_shape, in_specs=in_specs, out_specs=...  36.5 us
    ppermute x7, waiting for transfers between devices, to_chip(): return lax.ppermute(array, 'rep', pairs)  21.9 us
    ppermute x4, waiting for transfers between devices, across_z(): lax.ppermute(array, 'grp', [(g, (g + RING) % (2 * RING)) for g in range(2...  17.6 us
    ppermute x8, waiting for transfers between devices, along_x(): return lax.ppermute(array, 'grp', pairs)  15.1 us
    ppermute x7, starting transfers between devices, to_chip(): return lax.ppermute(array, 'rep', pairs)  13.9 us
    ppermute x8, starting transfers between devices, along_x(): return lax.ppermute(array, 'grp', pairs)  10.8 us
    ppermute x4, starting transfers between devices, across_z(): lax.ppermute(array, 'grp', [(g, (g + RING) % (2 * RING)) for g in range(2...  5.16 us
    unnamed x22, local copies, waits for them, and re-layouts  3.6 us
  transfers between devices with their start and end apart: 20, of which 11 were waited for; matrix products, arithmetic and copies ran while one was open for 0% of the time, Pallas kernels for 18%

profile of v6, /device:TPU:1, one launch (start us, length us, event | category | flops | bytes accessed | tf_op | source)
XLA Modules:
  0.0 131.6 jit_solution(10246632048198785672)
XLA Ops:
  0.7 3.4 %collective-permute-start.1 = (bf16[128,5120]{1,0:T(8,128)(2,1)}, bf16[128,5120]{1,0:T(8,128)(2,1)S(1)}, u32[]{:S(2)}, u32[]{:S(2)}) collective-permute-start(bf16[128,5120]{1,0:T(8,128)(2,1)} %refs_5_.1), channel_id=1, source_target_pairs={{0,3},{1,0},{2,1},{3,2},{4,7},{5,4},{6,5},{7,6},{8,11},{9,8},{10,9... | collective-permute-start | bytes 3932168 | tf_op jit(solution)/shard_map/ppermute | solution.py:26
  4.0 1.3 shard_map.103
  5.3 1.7 %collective-permute-start.2 = (bf16[80,5120]{1,0:T(8,128)(2,1)S(1)}, bf16[80,5120]{1,0:T(8,128)(2,1)}, u32[]{:S(2)}, u32[]{:S(2)}) collective-permute-start(bf16[80,5120]{1,0:T(8,128)(2,1)S(1)} %get-tuple-element.13), channel_id=1, source_target_pairs={{0,4},{1,5},{2,6},{3,7},{4,0},{5,1},{6,2},{7,3},{8,12},{9,13},{10,... | collective-permute-start | bytes 2457608 | tf_op jit(solution)/shard_map/ppermute | solution.py:30
  7.1 17.5 %collective-permute-done.2.refs_8_ = bf16[80,5120]{1,0:T(8,128)(2,1)} collective-permute-done((bf16[80,5120]{1,0:T(8,128)(2,1)S(1)}, bf16[80,5120]{1,0:T(8,128)(2,1)}, u32[]{:S(2)}, u32[]{:S(2)}) %collective-permute-start.2) | collective-permute-done | bytes 819232 | tf_op jit(solution)/shard_map/ppermute | solution.py:30
  24.7 2.4 %collective-permute-start.6 = (bf16[80,5120]{1,0:T(8,128)(2,1)}, bf16[80,5120]{1,0:T(8,128)(2,1)}, u32[]{:S(2)}, u32[]{:S(2)}) collective-permute-start(bf16[80,5120]{1,0:T(8,128)(2,1)} %collective-permute-done.2.refs_8_), channel_id=1, source_target_pairs={{0,3},{1,0},{2,1},{3,2},{4,7},{5,4},{6,5},{7,6},{8,11},{9,8},{10,9... | collective-permute-start | bytes 2457608 | tf_op jit(solution)/shard_map/ppermute | solution.py:26
  27.1 4.7 %collective-permute-done.1.refs_7_.refs_1_ = bf16[128,5120]{1,0:T(8,128)(2,1)S(1)} collective-permute-done((bf16[128,5120]{1,0:T(8,128)(2,1)}, bf16[128,5120]{1,0:T(8,128)(2,1)S(1)}, u32[]{:S(2)}, u32[]{:S(2)}) %collective-permute-start.1) | collective-permute-done | bytes 1310752 | tf_op jit(solution)/shard_map/ppermute | solution.py:26
  31.8 3.0 %collective-permute-done.refs_6_.refs_0_ = bf16[128,5120]{1,0:T(8,128)(2,1)S(1)} collective-permute-done((bf16[128,5120]{1,0:T(8,128)(2,1)}, bf16[128,5120]{1,0:T(8,128)(2,1)S(1)}, u32[]{:S(2)}, u32[]{:S(2)}) %collective-permute-start) | collective-permute-done | bytes 1310752 | tf_op jit(solution)/shard_map/ppermute | solution.py:26
  34.8 1.1 copy-done.5
  35.9 1.7 %shard_map.105 = (bf16[80,5120]{1,0:T(8,128)(2,1)S(1)}, bf16[48,5120]{1,0:T(8,128)(2,1)S(1)}, bf16[96,5120]{1,0:T(8,128)(2,1)S(1)}) custom-call(bf16[128,5120]{1,0:T(8,128)(2,1)} %copy-done.5, bf16[128,5120]{1,0:T(8,128)(2,1)} %copy-done.4), custom_call_target="tpu_custom_call" | custom-call | bytes 4587520 | tf_op jit(solution)/shard_map/pallas_call | solution.py:311
  37.6 1.7 %collective-permute-start.5 = (bf16[96,5120]{1,0:T(8,128)(2,1)S(1)}, bf16[96,5120]{1,0:T(8,128)(2,1)}, u32[]{:S(2)}, u32[]{:S(2)}) collective-permute-start(bf16[96,5120]{1,0:T(8,128)(2,1)S(1)} %get-tuple-element.15), channel_id=1, source_target_pairs={{0,4},{1,5},{2,6},{3,7},{4,0},{5,1},{6,2},{7,3},{8,12},{9,13},{10,... | collective-permute-start | bytes 2949128 | tf_op jit(solution)/shard_map/ppermute | solution.py:30
  39.4 1.4 %collective-permute-start.8 = (bf16[48,5120]{1,0:T(8,128)(2,1)}, bf16[48,5120]{1,0:T(8,128)(2,1)S(1)}, u32[]{:S(2)}, u32[]{:S(2)}) collective-permute-start(bf16[48,5120]{1,0:T(8,128)(2,1)} %copy-done.3), channel_id=1, source_target_pairs={{0,3},{1,0},{2,1},{3,2},{4,7},{5,4},{6,5},{7,6},{8,11},{9,8},{10,9... | collective-permute-start | bytes 1474568 | tf_op jit(solution)/shard_map/ppermute | solution.py:26
  40.9 2.5 %copy-done = bf16[1,4,128,5120]{3,2,1,0:T(8,128)(2,1)S(1)} copy-done((bf16[1,4,128,5120]{3,2,1,0:T(8,128)(2,1)S(1)}, bf16[1,4,128,5120]{3,2,1,0:T(8,128)(2,1)}, u32[]{:S(2)}) %copy-start) | copy-done | bytes 5242904
  43.4 9.9 %shard_map.104.refs_5_.refs_2_ = f32[512,5120]{1,0:T(8,128)S(1)} custom-call(s32[11]{0:T(128)S(1)} %stack.47.refs_0_.place_ref, f32[1,128]{1,0:T(1,128)S(1)} %bitcast.45, s32[8,128]{1,0:T(8,128)S(1)} %bitcast.42, bf16[1024,512]{1,0:T(8,128)(2,1)} %refs_3_.5, bf16[512,5120]{1,0:T(8,128)(2,1)S(1)} %bitcast.36, bf16[128,5120]{1,0:T(8,128)(2,1)} %refs_5_.1, ...), custom_call_target="tpu_custom_call" | custom-call | flops 5368709120 | bytes 20971520 | tf_op jit(solution)/shard_map/pallas_call | solution.py:311
  53.3 1.2 shard_map.107
  54.5 2.7 %collective-permute-start.10 = (bf16[64,5120]{1,0:T(8,128)(2,1)S(1)}, bf16[64,5120]{1,0:T(8,128)(2,1)S(1)}, u32[]{:S(2)}, u32[]{:S(2)}) collective-permute-start(bf16[64,5120]{1,0:T(8,128)(2,1)S(1)} %get-tuple-element.19), channel_id=1, source_target_pairs={{0,3},{1,0},{2,1},{3,2},{4,7},{5,4},{6,5},{7,6},{8,11},{9,8},{10,9... | collective-permute-start | bytes 1966088 | tf_op jit(solution)/shard_map/ppermute | solution.py:26
  57.2 2.7 %collective-permute-done.8.refs_7_ = bf16[48,5120]{1,0:T(8,128)(2,1)S(1)} collective-permute-done((bf16[48,5120]{1,0:T(8,128)(2,1)}, bf16[48,5120]{1,0:T(8,128)(2,1)S(1)}, u32[]{:S(2)}, u32[]{:S(2)}) %collective-permute-start.8) | collective-permute-done | bytes 491552 | tf_op jit(solution)/shard_map/ppermute | solution.py:26
  59.9 1.6 %collective-permute-start.11 = (bf16[48,5120]{1,0:T(8,128)(2,1)S(1)}, bf16[48,5120]{1,0:T(8,128)(2,1)S(1)}, u32[]{:S(2)}, u32[]{:S(2)}) collective-permute-start(bf16[48,5120]{1,0:T(8,128)(2,1)S(1)} %collective-permute-done.8.refs_7_), channel_id=1, source_target_pairs={{0,4},{1,5},{2,6},{3,7},{4,0},{5,1},{6,2},{7,3},{8,12},{9,13},{10,... | collective-permute-start | bytes 1474568 | tf_op jit(solution)/shard_map/ppermute | solution.py:30
  62.4 6.7 %shard_map.106.refs_5_ = f32[512,5120]{1,0:T(8,128)S(1)} custom-call(s32[11]{0:T(128)S(1)} %stack.47.refs_0_.place_ref, f32[1,128]{1,0:T(1,128)S(1)} %bitcast.46, s32[8,128]{1,0:T(8,128)S(1)} %bitcast.43, bf16[1024,512]{1,0:T(8,128)(2,1)} %refs_3_.5, bf16[512,5120]{1,0:T(8,128)(2,1)S(1)} %bitcast.39, ...), custom_call_target="tpu_custom_call", output_to_operand_aliasing={{}: (5, {})} | custom-call | flops 2684354560 | bytes 7864320 | tf_op jit(solution)/shard_map/pallas_call | solution.py:311
  69.2 4.2 %collective-permute-done.9.refs_8_ = bf16[16,5120]{1,0:T(8,128)(2,1)S(1)} collective-permute-done((bf16[16,5120]{1,0:T(8,128)(2,1)S(1)}, bf16[16,5120]{1,0:T(8,128)(2,1)S(1)}, u32[]{:S(2)}, u32[]{:S(2)}) %collective-permute-start.9) | collective-permute-done | bytes 163872 | tf_op jit(solution)/shard_map/ppermute | solution.py:26
  73.8 13.1 %shard_map.108 = (bf16[8,32,5120]{2,1,0:T(8,128)(2,1)S(1)}, bf16[4,256,5120]{2,1,0:T(8,128)(2,1)S(1)}, bf16[4,2,128,256]{3,2,1,0:T(8,128)(2,1)S(1)}) custom-call(s32[11]{0:T(128)S(1)} %stack.47.refs_0_.place_ref, f32[1,128]{1,0:T(1,128)S(1)} %bitcast.47, s32[8,128]{1,0:T(8,128)S(1)} %bitcast.44, bf16[1024,512]{1,0:T(8,128)(2,1)} %refs_3_.5, ...), custom_call_target="tpu_custom_call" | custom-call | flops 8053063680 | bytes 20971520 | tf_op jit(solution)/shard_map/pallas_call | solution.py:311
  86.9 1.6 %collective-permute-start.12 = (bf16[8,32,5120]{2,1,0:T(8,128)(2,1)S(1)}, bf16[8,32,5120]{2,1,0:T(8,128)(2,1)S(1)}, u32[]{:S(2)}, u32[]{:S(2)}) collective-permute-start(bf16[8,32,5120]{2,1,0:T(8,128)(2,1)S(1)} %get-tuple-element.22), channel_id=1, source_target_pairs={{0,8},{8,0},{16,24},{24,16},{32,40},{40,32},{48,56},{56,48},{64,72... | collective-permute-start | bytes 7864328 | tf_op jit(solution)/shard_map/ppermute | solution.py:34
  88.5 2.6 %shard_map.109 = bf16[8,32,5120]{2,1,0:T(8,128)(2,1)S(1)} custom-call(s32[11]{0:T(128)S(1)} %stack.47.refs_0_.place_ref, bf16[512,5120]{1,0:T(8,128)(2,1)S(1)} %bitcast.41, bf16[4,256,5120]{2,1,0:T(8,128)(2,1)S(1)} %get-tuple-element.20.split, bf16[4,2,128,256]{3,2,1,0:T(8,128)(2,1)S(1)} %get-tuple-element.21.factors), custom_call_target="tpu_custom_call" | custom-call | flops 2684354560 | bytes 10485760 | tf_op jit(solution)/shard_map/pallas_call | solution.py:311
  91.2 1.9 %collective-permute-done.12 = bf16[8,32,5120]{2,1,0:T(8,128)(2,1)S(1)} collective-permute-done((bf16[8,32,5120]{2,1,0:T(8,128)(2,1)S(1)}, bf16[8,32,5120]{2,1,0:T(8,128)(2,1)S(1)}, u32[]{:S(2)}, u32[]{:S(2)}) %collective-permute-start.12) | collective-permute-done | bytes 2621472 | tf_op jit(solution)/shard_map/ppermute | solution.py:34
  93.9 6.5 %collective-permute-start.13 = (bf16[32,5120]{1,0:T(8,128)(2,1)S(1)}, bf16[32,5120]{1,0:T(8,128)(2,1)S(1)}, u32[]{:S(2)}, u32[]{:S(2)}) collective-permute-start(bf16[32,5120]{1,0:T(8,128)(2,1)S(1)} %get-tuple-element.26), channel_id=1, source_target_pairs={{0,80},{8,88},{16,64},{24,72},{32,112},{40,120},{48,96},{56,104},{... | collective-permute-start | bytes 983048 | tf_op jit(solution)/shard_map/ppermute | solution.py:45
  100.9 3.5 %collective-permute-start.17 = (bf16[32,5120]{1,0:T(8,128)(2,1)S(1)}, bf16[32,5120]{1,0:T(8,128)(2,1)S(1)}, u32[]{:S(2)}, u32[]{:S(2)}) collective-permute-start(bf16[32,5120]{1,0:T(8,128)(2,1)S(1)} %get-tuple-element.29), channel_id=1, source_target_pairs={{0,16},{8,24},{16,0},{24,8},{32,48},{40,56},{48,32},{56,40},{64,80... | collective-permute-start | bytes 983048 | tf_op jit(solution)/shard_map/ppermute | solution.py:45
  104.5 1.4 %collective-permute-start.16 = (bf16[32,5120]{1,0:T(8,128)(2,1)S(1)}, bf16[32,5120]{1,0:T(8,128)(2,1)S(1)}, u32[]{:S(2)}, u32[]{:S(2)}) collective-permute-start(bf16[32,5120]{1,0:T(8,128)(2,1)S(1)} %get-tuple-element.30), channel_id=1, source_target_pairs={{0,96},{8,104},{16,112},{24,120},{32,0},{40,8},{48,16},{56,24},{64... | collective-permute-start | bytes 983048 | tf_op jit(solution)/shard_map/ppermute | solution.py:45
  105.9 2.4 %collective-permute-done.13 = bf16[32,5120]{1,0:T(8,128)(2,1)S(1)} collective-permute-done((bf16[32,5120]{1,0:T(8,128)(2,1)S(1)}, bf16[32,5120]{1,0:T(8,128)(2,1)S(1)}, u32[]{:S(2)}, u32[]{:S(2)}) %collective-permute-start.13) | collective-permute-done | bytes 327712 | tf_op jit(solution)/shard_map/ppermute | solution.py:45
  108.3 6.7 %collective-permute-done.19 = bf16[32,5120]{1,0:T(8,128)(2,1)S(1)} collective-permute-done((bf16[32,5120]{1,0:T(8,128)(2,1)S(1)}, bf16[32,5120]{1,0:T(8,128)(2,1)S(1)}, u32[]{:S(2)}, u32[]{:S(2)}) %collective-permute-start.19) | collective-permute-done | bytes 327712 | tf_op jit(solution)/shard_map/ppermute | solution.py:45
  115.0 1.8 %collective-permute-start.14 = (bf16[32,5120]{1,0:T(8,128)(2,1)S(1)}, bf16[32,5120]{1,0:T(8,128)(2,1)S(1)}, u32[]{:S(2)}, u32[]{:S(2)}) collective-permute-start(bf16[32,5120]{1,0:T(8,128)(2,1)S(1)} %get-tuple-element.32), channel_id=1, source_target_pairs={{0,112},{8,120},{16,96},{24,104},{32,16},{40,24},{48,0},{56,8},{64... | collective-permute-start | bytes 983048 | tf_op jit(solution)/shard_map/ppermute | solution.py:45
  116.8 6.1 %collective-permute-done.18 = bf16[32,5120]{1,0:T(8,128)(2,1)S(1)} collective-permute-done((bf16[32,5120]{1,0:T(8,128)(2,1)S(1)}, bf16[32,5120]{1,0:T(8,128)(2,1)S(1)}, u32[]{:S(2)}, u32[]{:S(2)}) %collective-permute-start.18) | collective-permute-done | bytes 327712 | tf_op jit(solution)/shard_map/ppermute | solution.py:45
  122.9 6.8 %collective-permute-done.15 = bf16[32,5120]{1,0:T(8,128)(2,1)S(1)} collective-permute-done((bf16[32,5120]{1,0:T(8,128)(2,1)S(1)}, bf16[32,5120]{1,0:T(8,128)(2,1)S(1)}, u32[]{:S(2)}, u32[]{:S(2)}) %collective-permute-start.15) | collective-permute-done | bytes 327712 | tf_op jit(solution)/shard_map/ppermute | solution.py:45
  129.7 1.8 %multiply_add_fusion = (f32[4,8,5120]{2,1,0:T(8,128)}, f32[4,8,5120]{2,1,0:T(8,128)}, f32[4,8,5120]{2,1,0:T(8,128)}) fusion(f32[4,8,5120]{2,1,0:T(8,128)S(1)} %copy-done.6, f32[4,8,5120]{2,1,0:T(8,128)S(1)} %copy-done.7, f32[4,8,5120]{2,1,0:T(8,128)S(1)} %copy-done.8, bf16[8,32,5120]{2,1,0:T(8,128)(2,1)S(1)} %collective-permute-done.12, ...), kind=kLoop, calls=%fused_computation.3 | loop fusion | flops 4587520 | bytes 6881280 | tf_op jit(solution)/shard_map/add | solution.py:536
  (41 shorter events, 3.1 us)
Async XLA Ops:
  0.6 40.3 %copy-start.2 = (f32[128]{0:T(128)S(1)}, f32[128]{0:T(128)}, u32[]{:S(2)}) copy-start(f32[128]{0:T(128)} %param.12) | copy-start | bytes 1540
  0.6 40.3 %copy-start.1 = (s32[1024]{0:T(1024)S(1)}, s32[1024]{0:T(1024)}, u32[]{:S(2)}) copy-start(s32[1024]{0:T(1024)} %param.9) | copy-start | bytes 12292
  0.7 31.1 %collective-permute-start.1 = (bf16[128,5120]{1,0:T(8,128)(2,1)}, bf16[128,5120]{1,0:T(8,128)(2,1)S(1)}, u32[]{:S(2)}, u32[]{:S(2)}) collective-permute-start(bf16[128,5120]{1,0:T(8,128)(2,1)} %refs_5_.1), channel_id=1, source_target_pairs={{0,3},{1,0},{2,1},{3,2},{4,7},{5,4},{6,5},{7,6},{8,11},{9,8},{10,9... | collective-permute-start | bytes 3932168 | tf_op jit(solution)/shard_map/ppermute | solution.py:26
  4.0 30.7 %collective-permute-start = (bf16[128,5120]{1,0:T(8,128)(2,1)}, bf16[128,5120]{1,0:T(8,128)(2,1)S(1)}, u32[]{:S(2)}, u32[]{:S(2)}) collective-permute-start(bf16[128,5120]{1,0:T(8,128)(2,1)} %refs_5_.1), channel_id=1, source_target_pairs={{0,1},{1,2},{2,3},{3,0},{4,5},{5,6},{6,7},{7,4},{8,9},{9,10},{10,1... | collective-permute-start | bytes 3932168 | tf_op jit(solution)/shard_map/ppermute | solution.py:26
  5.3 19.4 %collective-permute-start.2 = (bf16[80,5120]{1,0:T(8,128)(2,1)S(1)}, bf16[80,5120]{1,0:T(8,128)(2,1)}, u32[]{:S(2)}, u32[]{:S(2)}) collective-permute-start(bf16[80,5120]{1,0:T(8,128)(2,1)S(1)} %get-tuple-element.13), channel_id=1, source_target_pairs={{0,4},{1,5},{2,6},{3,7},{4,0},{5,1},{6,2},{7,3},{8,12},{9,13},{10,... | collective-permute-start | bytes 2457608 | tf_op jit(solution)/shard_map/ppermute | solution.py:30
  7.0 33.8 %collective-permute-start.3 = (bf16[48,5120]{1,0:T(8,128)(2,1)S(1)}, bf16[48,5120]{1,0:T(8,128)(2,1)}, u32[]{:S(2)}, u32[]{:S(2)}) collective-permute-start(bf16[48,5120]{1,0:T(8,128)(2,1)S(1)} %get-tuple-element.14), channel_id=1, source_target_pairs={{0,4},{1,5},{2,6},{3,7},{4,0},{5,1},{6,2},{7,3},{8,12},{9,13},{10,... | collective-permute-start | bytes 1474568 | tf_op jit(solution)/shard_map/ppermute | solution.py:30
  24.7 28.6 %collective-permute-start.6 = (bf16[80,5120]{1,0:T(8,128)(2,1)}, bf16[80,5120]{1,0:T(8,128)(2,1)}, u32[]{:S(2)}, u32[]{:S(2)}) collective-permute-start(bf16[80,5120]{1,0:T(8,128)(2,1)} %collective-permute-done.2.refs_8_), channel_id=1, source_target_pairs={{0,3},{1,0},{2,1},{3,2},{4,7},{5,4},{6,5},{7,6},{8,11},{9,8},{10,9... | collective-permute-start | bytes 2457608 | tf_op jit(solution)/shard_map/ppermute | solution.py:26
  27.0 26.2 %collective-permute-start.4 = (bf16[80,5120]{1,0:T(8,128)(2,1)}, bf16[80,5120]{1,0:T(8,128)(2,1)}, u32[]{:S(2)}, u32[]{:S(2)}) collective-permute-start(bf16[80,5120]{1,0:T(8,128)(2,1)} %collective-permute-done.2.refs_8_), channel_id=1, source_target_pairs={{0,1},{1,2},{2,3},{3,0},{4,5},{5,6},{6,7},{7,4},{8,9},{9,10},{10,1... | collective-permute-start | bytes 2457608 | tf_op jit(solution)/shard_map/ppermute | solution.py:26
  31.8 3.0 %copy-start.4 = (bf16[128,5120]{1,0:T(8,128)(2,1)}, bf16[128,5120]{1,0:T(8,128)(2,1)S(1)}, u32[]{:S(2)}) copy-start(bf16[128,5120]{1,0:T(8,128)(2,1)S(1)} %collective-permute-done.1.refs_7_.refs_1_) | copy-start | bytes 3932164
  34.8 1.1 copy-start.5
  35.8 26.6 %slice-start = ((s8[5242880]{0:T(1024)(128)(4,1)}), s8[1048576]{0:T(1024)(128)(4,1)S(1)}, s32[]{:S(2)}) async-start(s8[5242880]{0:T(1024)(128)(4,1)} %bitcast.37), calls=%async_computation | async-start | bytes 2097152
  37.6 1.7 %copy-start.3 = (bf16[48,5120]{1,0:T(8,128)(2,1)}, bf16[48,5120]{1,0:T(8,128)(2,1)S(1)}, u32[]{:S(2)}) copy-start(bf16[48,5120]{1,0:T(8,128)(2,1)S(1)} %get-tuple-element.17) | copy-start | bytes 1474564
  37.6 24.9 %collective-permute-start.5 = (bf16[96,5120]{1,0:T(8,128)(2,1)S(1)}, bf16[96,5120]{1,0:T(8,128)(2,1)}, u32[]{:S(2)}, u32[]{:S(2)}) collective-permute-start(bf16[96,5120]{1,0:T(8,128)(2,1)S(1)} %get-tuple-element.15), channel_id=1, source_target_pairs={{0,4},{1,5},{2,6},{3,7},{4,0},{5,1},{6,2},{7,3},{8,12},{9,13},{10,... | collective-permute-start | bytes 2949128 | tf_op jit(solution)/shard_map/ppermute | solution.py:30
  39.4 20.5 %collective-permute-start.8 = (bf16[48,5120]{1,0:T(8,128)(2,1)}, bf16[48,5120]{1,0:T(8,128)(2,1)S(1)}, u32[]{:S(2)}, u32[]{:S(2)}) collective-permute-start(bf16[48,5120]{1,0:T(8,128)(2,1)} %copy-done.3), channel_id=1, source_target_pairs={{0,3},{1,0},{2,1},{3,2},{4,7},{5,4},{6,5},{7,6},{8,11},{9,8},{10,9... | collective-permute-start | bytes 1474568 | tf_op jit(solution)/shard_map/ppermute | solution.py:26
  40.8 32.6 %collective-permute-start.7 = (bf16[80,5120]{1,0:T(8,128)(2,1)S(1)}, bf16[80,5120]{1,0:T(8,128)(2,1)S(1)}, u32[]{:S(2)}, u32[]{:S(2)}) collective-permute-start(bf16[80,5120]{1,0:T(8,128)(2,1)S(1)} %get-tuple-element.16), channel_id=1, source_target_pairs={{0,1},{1,2},{2,3},{3,0},{4,5},{5,6},{6,7},{7,4},{8,9},{9,10},{10,1... | collective-permute-start | bytes 2457608 | tf_op jit(solution)/shard_map/ppermute | solution.py:26
  40.9 2.5 %copy-start = (bf16[1,4,128,5120]{3,2,1,0:T(8,128)(2,1)S(1)}, bf16[1,4,128,5120]{3,2,1,0:T(8,128)(2,1)}, u32[]{:S(2)}) copy-start(bf16[1,4,128,5120]{3,2,1,0:T(8,128)(2,1)} %param.11) | copy-start | bytes 15728644
  43.4 19.0 %slice-start.1 = ((s8[5242880]{0:T(1024)(128)(4,1)}), s8[4194304]{0:T(1024)(128)(4,1)S(1)}, s32[]{:S(2)}) async-start(s8[5242880]{0:T(1024)(128)(4,1)} %bitcast.37), calls=%async_computation.1 | async-start | bytes 8388608
  54.5 19.3 %collective-permute-start.10 = (bf16[64,5120]{1,0:T(8,128)(2,1)S(1)}, bf16[64,5120]{1,0:T(8,128)(2,1)S(1)}, u32[]{:S(2)}, u32[]{:S(2)}) collective-permute-start(bf16[64,5120]{1,0:T(8,128)(2,1)S(1)} %get-tuple-element.19), channel_id=1, source_target_pairs={{0,3},{1,0},{2,1},{3,2},{4,7},{5,4},{6,5},{7,6},{8,11},{9,8},{10,9... | collective-permute-start | bytes 1966088 | tf_op jit(solution)/shard_map/ppermute | solution.py:26
  59.9 13.9 %collective-permute-start.11 = (bf16[48,5120]{1,0:T(8,128)(2,1)S(1)}, bf16[48,5120]{1,0:T(8,128)(2,1)S(1)}, u32[]{:S(2)}, u32[]{:S(2)}) collective-permute-start(bf16[48,5120]{1,0:T(8,128)(2,1)S(1)} %collective-permute-done.8.refs_7_), channel_id=1, source_target_pairs={{0,4},{1,5},{2,6},{3,7},{4,0},{5,1},{6,2},{7,3},{8,12},{9,13},{10,... | collective-permute-start | bytes 1474568 | tf_op jit(solution)/shard_map/ppermute | solution.py:30
  61.5 11.9 %collective-permute-start.9 = (bf16[16,5120]{1,0:T(8,128)(2,1)S(1)}, bf16[16,5120]{1,0:T(8,128)(2,1)S(1)}, u32[]{:S(2)}, u32[]{:S(2)}) collective-permute-start(bf16[16,5120]{1,0:T(8,128)(2,1)S(1)} %get-tuple-element.18), channel_id=1, source_target_pairs={{0,1},{1,2},{2,3},{3,0},{4,5},{5,6},{6,7},{7,4},{8,9},{9,10},{10,1... | collective-permute-start | bytes 491528 | tf_op jit(solution)/shard_map/ppermute | solution.py:26
  86.9 6.2 %collective-permute-start.12 = (bf16[8,32,5120]{2,1,0:T(8,128)(2,1)S(1)}, bf16[8,32,5120]{2,1,0:T(8,128)(2,1)S(1)}, u32[]{:S(2)}, u32[]{:S(2)}) collective-permute-start(bf16[8,32,5120]{2,1,0:T(8,128)(2,1)S(1)} %get-tuple-element.22), channel_id=1, source_target_pairs={{0,8},{8,0},{16,24},{24,16},{32,40},{40,32},{48,56},{56,48},{64,72... | collective-permute-start | bytes 7864328 | tf_op jit(solution)/shard_map/ppermute | solution.py:34
  91.1 38.6 %copy-start.6 = (f32[4,8,5120]{2,1,0:T(8,128)S(1)}, f32[4,8,5120]{2,1,0:T(8,128)}, u32[]{:S(2)}) copy-start(f32[4,8,5120]{2,1,0:T(8,128)} %param.15) | copy-start | bytes 1966084
  91.2 38.6 %copy-start.7 = (f32[4,8,5120]{2,1,0:T(8,128)S(1)}, f32[4,8,5120]{2,1,0:T(8,128)}, u32[]{:S(2)}) copy-start(f32[4,8,5120]{2,1,0:T(8,128)} %param.13) | copy-start | bytes 1966084
  91.2 38.6 %copy-start.8 = (f32[4,8,5120]{2,1,0:T(8,128)S(1)}, f32[4,8,5120]{2,1,0:T(8,128)}, u32[]{:S(2)}) copy-start(f32[4,8,5120]{2,1,0:T(8,128)} %param.14) | copy-start | bytes 1966084
  93.9 14.3 %collective-permute-start.13 = (bf16[32,5120]{1,0:T(8,128)(2,1)S(1)}, bf16[32,5120]{1,0:T(8,128)(2,1)S(1)}, u32[]{:S(2)}, u32[]{:S(2)}) collective-permute-start(bf16[32,5120]{1,0:T(8,128)(2,1)S(1)} %get-tuple-element.26), channel_id=1, source_target_pairs={{0,80},{8,88},{16,64},{24,72},{32,112},{40,120},{48,96},{56,104},{... | collective-permute-start | bytes 983048 | tf_op jit(solution)/shard_map/ppermute | solution.py:45
  100.4 14.6 %collective-permute-start.19 = (bf16[32,5120]{1,0:T(8,128)(2,1)S(1)}, bf16[32,5120]{1,0:T(8,128)(2,1)S(1)}, u32[]{:S(2)}, u32[]{:S(2)}) collective-permute-start(bf16[32,5120]{1,0:T(8,128)(2,1)S(1)} %get-tuple-element.27), channel_id=1, source_target_pairs={{0,64},{8,72},{16,80},{24,88},{32,96},{40,104},{48,112},{56,120},{... | collective-permute-start | bytes 983048 | tf_op jit(solution)/shard_map/ppermute | solution.py:45
  100.5 22.5 %collective-permute-start.18 = (bf16[32,5120]{1,0:T(8,128)(2,1)S(1)}, bf16[32,5120]{1,0:T(8,128)(2,1)S(1)}, u32[]{:S(2)}, u32[]{:S(2)}) collective-permute-start(bf16[32,5120]{1,0:T(8,128)(2,1)S(1)} %get-tuple-element.28), channel_id=1, source_target_pairs={{0,48},{8,56},{16,32},{24,40},{32,80},{40,88},{48,64},{56,72},{64,... | collective-permute-start | bytes 983048 | tf_op jit(solution)/shard_map/ppermute | solution.py:45
  100.9 22.0 %collective-permute-start.17 = (bf16[32,5120]{1,0:T(8,128)(2,1)S(1)}, bf16[32,5120]{1,0:T(8,128)(2,1)S(1)}, u32[]{:S(2)}, u32[]{:S(2)}) collective-permute-start(bf16[32,5120]{1,0:T(8,128)(2,1)S(1)} %get-tuple-element.29), channel_id=1, source_target_pairs={{0,16},{8,24},{16,0},{24,8},{32,48},{40,56},{48,32},{56,40},{64,80... | collective-permute-start | bytes 983048 | tf_op jit(solution)/shard_map/ppermute | solution.py:45
  104.5 18.5 %collective-permute-start.16 = (bf16[32,5120]{1,0:T(8,128)(2,1)S(1)}, bf16[32,5120]{1,0:T(8,128)(2,1)S(1)}, u32[]{:S(2)}, u32[]{:S(2)}) collective-permute-start(bf16[32,5120]{1,0:T(8,128)(2,1)S(1)} %get-tuple-element.30), channel_id=1, source_target_pairs={{0,96},{8,104},{16,112},{24,120},{32,0},{40,8},{48,16},{56,24},{64... | collective-permute-start | bytes 983048 | tf_op jit(solution)/shard_map/ppermute | solution.py:45
  108.2 21.5 %collective-permute-start.15 = (bf16[32,5120]{1,0:T(8,128)(2,1)S(1)}, bf16[32,5120]{1,0:T(8,128)(2,1)S(1)}, u32[]{:S(2)}, u32[]{:S(2)}) collective-permute-start(bf16[32,5120]{1,0:T(8,128)(2,1)S(1)} %get-tuple-element.31), channel_id=1, source_target_pairs={{0,32},{8,40},{16,48},{24,56},{32,64},{40,72},{48,80},{56,88},{64,... | collective-permute-start | bytes 983048 | tf_op jit(solution)/shard_map/ppermute | solution.py:45
  115.0 14.7 %collective-permute-start.14 = (bf16[32,5120]{1,0:T(8,128)(2,1)S(1)}, bf16[32,5120]{1,0:T(8,128)(2,1)S(1)}, u32[]{:S(2)}, u32[]{:S(2)}) collective-permute-start(bf16[32,5120]{1,0:T(8,128)(2,1)S(1)} %get-tuple-element.32), channel_id=1, source_target_pairs={{0,112},{8,120},{16,96},{24,104},{32,16},{40,24},{48,0},{56,8},{64... | collective-permute-start | bytes 983048 | tf_op jit(solution)/shard_map/ppermute | solution.py:45
